TPU v7x, 256 devices: a whole 4x4x8 slice. The times are simulated.
256 devices in a mesh: row: 16 (over z_lo, y), col: 8 (over x, core), cell: 2 (over z_hi).
Axes of the slice: x: 4, y: 4, z: 8 (z_hi: 2, z_lo: 4; z = z_hi * 4 + z_lo), core: 2. Of those that a mesh axis runs over, the one named last changes fastest.
Arguments:
- counts: int32 [8192, 8192], P(('row', 'col'), 'cell'), may hold values from 0 to 108, as said below
- size_factors: float32 [8192], P('cell'), may hold values from 0.3 to 3
- gene_means: float32 [8192], replicated, may hold values from 0.2 to 20
- dispersions: float32 [8192], replicated, may hold values from 0.5 to 50
- block_order: int32 [128], replicated, may hold values from 0 to 127, each once
Outputs:
- correlation: float32 [8192, 8, 1024], P(('row', 'cell'), 'col')
Inputs may be any that keep to these rules, and one draw needn't show every extreme that they name: `counts`: each cell's count is a uniform noise of 0 to 15 plus a gene's multiplier of 0 to 3 times one of four shared cell programs of 0 to 31. `block_order`: A permutation of the 128 block ids.
All inputs are finite; a program needn't handle non-finite values.
Results may differ from a plain program's by a relative error of at most 0.0003.
Values may be sent and summed in bfloat16 or wider, within the bound.
No kernel may reach another device: no remote copies, remote signals or barrier semaphores. Data moves between devices by JAX's collectives and lax.ppermute only.
A program may use at most 128 MiB of HBM per device.

v0:
```python
import math

import jax
import jax.numpy as jnp
from jax import lax
from jax.sharding import PartitionSpec as P


def residuals(counts, size_factors, gene_means, dispersions, block_order):
    blocks = counts.shape[0]
    place = lax.axis_index(("row", "col"))
    first = block_order[place] * blocks
    mean_gene = lax.dynamic_slice_in_dim(gene_means, first, blocks)[:, None]
    disp_gene = lax.dynamic_slice_in_dim(dispersions, first, blocks)[:, None]
    expected = mean_gene * size_factors[None, :]
    spread = jnp.sqrt(expected + expected * expected / disp_gene)
    limit = math.sqrt(size_factors.shape[0] * lax.axis_size("cell"))
    return jnp.clip((counts.astype(jnp.float32) - expected) / spread, -limit, limit).astype(
        jnp.bfloat16
    )


def row_moments(values):
    total = jnp.sum(values, axis=1, dtype=jnp.float32)
    square = jnp.einsum("ij,ij->i", values, values, preferred_element_type=jnp.float32)
    return (total, square)


def column_terms(rows_res, piece):
    block = lax.dot_general(
        rows_res, piece, (((1,), (1,)), ((), ())), preferred_element_type=jnp.float32
    )
    total, square = row_moments(piece)
    return (block, total[None, :], square[None, :])


def local(counts, size_factors, gene_means, dispersions, block_order):
    resid = residuals(counts, size_factors, gene_means, dispersions, block_order)
    whole = lax.all_gather(resid, "cell", axis=1, tiled=True)
    rows_all = lax.all_gather(whole, "col", axis=0, tiled=True)
    half = rows_all.shape[0] // lax.axis_size("cell")
    own_rows = lax.dynamic_slice_in_dim(rows_all, lax.axis_index("cell") * half, half, 0)
    gram, col_sum, col_sq = column_terms(own_rows, lax.all_gather(whole, "row", axis=0, tiled=True))
    row_sum, row_sq = row_moments(own_rows)
    total_cells = whole.shape[1]
    row_mean = row_sum / total_cells
    col_mean = col_sum[0] / total_cells
    row_inv = lax.rsqrt(row_sq / total_cells - row_mean * row_mean + 1e-05)
    col_inv = lax.rsqrt(col_sq[0] / total_cells - col_mean * col_mean + 1e-05)
    result = (
        (gram / total_cells - row_mean[:, None] * col_mean[None, :])
        * row_inv[:, None]
        * col_inv[None, :]
    )
    return result[:, None, :]


def solution(mesh):
    return jax.shard_map(
        local,
        mesh=mesh,
        in_specs=(P(("row", "col"), "cell"), P("cell"), P(), P(), P()),
        out_specs=P(("row", "cell"), "col", None),
        check_vma=False,
    )
```

profile of v0, /device:TPU:26, one launch (start us, length us, event | category | flops | bytes accessed | tf_op | source)
XLA Modules:
  0.0 317.8 jit_solution(17235260961826448142)
XLA Ops:
  6.5 0.0 all-gather.4.cloned.1.call-start
  6.5 1.2 dynamic_slice.12
  8.4 0.8 dynamic_slice.13
  9.2 0.8 dynamic_slice.14
  10.0 2.4 fusion.21
  12.4 0.0 all-gather.4.cloned.1.call-update
  12.4 0.0 all-gather.6.cloned.1.call-start
  12.4 44.7 %all-gather.4.cloned.1.call-done = bf16[64,8192]{1,0:T(8,128)(2,1)} async-done(((bf16[64,4096]{1,0:T(8,128)(2,1)}), bf16[64,8192]{1,0:T(8,128)(2,1)}) %all-gather.4.cloned.1.call-update) | async-done | bytes 1048592 | tf_op jit(solution)/shard_map/all_gather | solution.py:39
  57.2 0.0 all-gather.6.cloned.1.call-update
  57.2 0.0 all-gather.8.cloned.1.call-start
  57.3 0.7 all-gather.8.cloned.1.call-update
  57.9 48.9 %all-gather.6.cloned.1.call-done = bf16[512,8192]{1,0:T(8,128)(2,1)} async-done(((bf16[64,8192]{1,0:T(8,128)(2,1)}), bf16[512,8192]{1,0:T(8,128)(2,1)}) %all-gather.6.cloned.1.call-update) | async-done | bytes 8388624 | tf_op jit(solution)/shard_map/all_gather | solution.py:40
  106.8 3.4 %convert_reduce_fusion.1 = (f32[256]{0:T(256)S(1)}, f32[256]{0:T(256)S(1)}) fusion(bf16[512,8192]{1,0:T(8,128)(2,1)} %all-gather.6.cloned.1.call-done, s32[]{:T(128)S(6)} %select_n.12), kind=kLoop, calls=%fused_computation.4 | loop fusion | flops 8388096 | bytes 4196356 | tf_op jit(solution)/shard_map/reduce_sum | solution.py:24
  110.2 181.9 %all-gather.8.cloned.1.call-done = bf16[1024,8192]{1,0:T(8,128)(2,1)} async-done(((bf16[64,8192]{1,0:T(8,128)(2,1)}), bf16[1024,8192]{1,0:T(8,128)(2,1)}) %all-gather.8.cloned.1.call-update) | async-done | bytes 16777232 | tf_op jit(solution)/shard_map/all_gather | solution.py:43
  292.1 7.7 %convert_reduce_fusion = (f32[1024]{0:T(1024)S(1)}, f32[1024]{0:T(1024)S(1)}) fusion(bf16[1024,8192]{1,0:T(8,128)(2,1)} %all-gather.8.cloned.1.call-done), kind=kLoop, calls=%fused_computation.1 | loop fusion | flops 33552384 | bytes 16785408 | tf_op jit(solution)/shard_map/reduce_sum | solution.py:24
  299.8 9.4 %fusion.16 = f32[256,1,1024]{2,0,1:T(8,128)S(1)} fusion(bf16[1024,8192]{1,0:T(8,128)(2,1)} %all-gather.8.cloned.1.call-done, bf16[512,8192]{1,0:T(8,128)(2,1)} %all-gather.6.cloned.1.call-done, s32[]{:T(128)S(6)} %select_n.12, f32[1024]{0:T(1024)S(1)} %get-tuple-element.10, f32[256]{0:T(256)S(1)} %get-tuple-element.12, f32[1024]{0:T(1024)S(1)} %get-tuple-element.9, ...), kind=kOutput, calls=%fused_computation.15 | convolution fusion | flops 4296278016 | bytes 22030340 | tf_op jit(solution)/shard_map/dot_general | solution.py:30
  309.2 2.0 copy.6
  (2 shorter events, 0.0 us)
Async XLA Ops:
  6.5 50.6 %all-gather.4.cloned.1.call-start = ((), (), s32[]{:S(2)}) async-start(), calls=%async_computation | async-start | bytes 1572864 | tf_op jit(solution)/shard_map/all_gather | solution.py:39
  12.4 94.4 %all-gather.6.cloned.1.call-start = ((), (), s32[]{:S(2)}) async-start(), calls=%async_computation.1 | async-start | bytes 9437184 | tf_op jit(solution)/shard_map/all_gather | solution.py:40
  57.2 234.9 %all-gather.8.cloned.1.call-start = ((), (), s32[]{:S(2)}) async-start(), calls=%async_computation.2 | async-start | bytes 17825792 | tf_op jit(solution)/shard_map/all_gather | solution.py:43
Sparse Core Ops, SparseCore 0:
  12.5 44.6 all-gather.3
  59.0 47.7 all-gather.5
  108.6 183.4 all-gather.7
where the time goes:
time: 323 us; the launch traced here: 318 us
  waiting for transfers between devices  276 us (85%)
  between operations  13.8 us (4%)
  other arithmetic  13.5 us (4%)
  matrix products  9.39 us (3%)
  local copies, waits for them, and re-layouts  4.81 us (1%)
    all_gather x1, waiting for transfers between devices, local(): lax.all_gather(whole, 'row', axis=0, tiled=True)  182 us
    all_gather x1, waiting for transfers between devices, local(): rows_all = lax.all_gather(whole, 'col', axis=0, tiled=True)  48.9 us
    all_gather x1, waiting for transfers between devices, local(): whole = lax.all_gather(resid, 'cell', axis=1, tiled=True)  44.7 us
    reduce_sum x2, other arithmetic, row_moments(): total = jnp.sum(values, axis=1, dtype=jnp.float32)  11.1 us
    dot_general x1, matrix products, column_terms(): lax.dot_general(rows_res, piece, (((1,), (1,)), ((), ())), preferred_elem...  9.39 us
  transfers between devices with their start and end apart: 3, of which 3 were waited for; matrix products, arithmetic and copies ran while one was open for 1% of the time, Pallas kernels for 0%

commit v1 on v0

v1 whole, which is shorter than its diff:
```python
import functools
import math

import jax
import jax.numpy as jnp
import numpy as np
from jax import lax
from jax.experimental import pallas as pl
from jax.experimental.pallas import tpu as pltpu
from jax.sharding import PartitionSpec as P

AXES = ("row", "col", "cell")
ZL, NY, NX, NC, NH = 4, 4, 4, 2, 2
EPS = 1e-05
FULL = 32767.0
NT = (((1,), (1,)), ((), ()))


def shift(zl=0, y=0, x=0, c=0, h=0):
    dims, step, pairs = (ZL, NY, NX, NC, NH), (zl, y, x, c, h), []
    for i in range(math.prod(dims)):
        at = np.unravel_index(i, dims)
        to = [(int(a) + s) % d for a, s, d in zip(at, step, dims)]
        pairs.append((i, int(np.ravel_multi_index(to, dims))))
    return pairs


def move(value, **steps):
    return lax.ppermute(value, AXES, shift(**steps))


def residuals(counts, size_factors, gene_means, dispersions, block_order):
    blocks = counts.shape[0]
    place = lax.axis_index(("row", "col"))
    first = block_order[place] * blocks
    mean_gene = lax.dynamic_slice_in_dim(gene_means, first, blocks)[:, None]
    disp_gene = lax.dynamic_slice_in_dim(dispersions, first, blocks)[:, None]
    expected = mean_gene * size_factors[None, :]
    spread = jnp.sqrt(expected + expected * expected / disp_gene)
    limit = math.sqrt(size_factors.shape[0] * lax.axis_size("cell"))
    return jnp.clip((counts.astype(jnp.float32) - expected) / spread, -limit, limit).astype(
        jnp.bfloat16
    )


def encode(p):
    root = jnp.minimum(jnp.sqrt(jnp.abs(p)), 1.0) * FULL + 0.5
    return jnp.where(p < 0, -root, root).astype(jnp.int32).astype(jnp.int16)


def decode(q):
    f = q.astype(jnp.int32).astype(jnp.float32)
    return f * jnp.abs(f) * (1.0 / (FULL * FULL))


def lane_sums(parts):
    ones = jnp.ones((8, 128), jnp.float32)
    return lax.dot_general(
        ones, parts, NT, precision=lax.Precision.HIGHEST, preferred_element_type=jnp.float32
    )


def fold(values):
    tiles = [values[:, i : i + 128] for i in range(0, values.shape[1], 128)]
    while len(tiles) > 1:
        tiles = [a + b for a, b in zip(tiles[::2], tiles[1::2])]
    return tiles[0]


def stats_kernel(cells, steps, r_ref, col_ref, lane_ref, s_acc, q_acc):
    k = pl.program_id(0)

    @pl.when(k == 0)
    def _():
        s_acc[...] = jnp.zeros_like(s_acc)
        q_acc[...] = jnp.zeros_like(q_acc)

    wide = r_ref[...].astype(jnp.float32)
    s_acc[...] += fold(wide)
    q_acc[...] += fold(wide * wide)

    @pl.when(k == steps - 1)
    def _():
        s = jnp.sum(s_acc[...], axis=1, keepdims=True) * (1.0 / cells)
        q = jnp.sum(q_acc[...], axis=1, keepdims=True) * (1.0 / cells)
        il = lax.rsqrt(q - s * s + EPS)
        lane = lax.broadcasted_iota(jnp.int32, col_ref.shape, 1)
        col_ref[...] = jnp.where(lane == 0, s, il)
        row = lax.broadcasted_iota(jnp.int32, lane_ref.shape, 0)
        lane_ref[...] = jnp.where(row == 0, lane_sums(s_acc[...]), lane_sums(q_acc[...])) * (
            1.0 / cells
        )


def row_stats(rows):
    n, cells = rows.shape
    steps = 4
    return pl.pallas_call(
        functools.partial(stats_kernel, cells, steps),
        grid=(steps,),
        in_specs=[pl.BlockSpec((n, cells // steps), lambda k: (0, k))],
        out_specs=[pl.BlockSpec((n, 128), lambda k: (0, 0)), pl.BlockSpec((8, n), lambda k: (0, 0))],
        out_shape=[
            jax.ShapeDtypeStruct((n, 128), jnp.float32),
            jax.ShapeDtypeStruct((8, n), jnp.float32),
        ],
        scratch_shapes=[pltpu.VMEM((n, 128), jnp.float32)] * 2,
        cost_estimate=pl.CostEstimate(
            flops=4 * n * cells, bytes_accessed=2 * n * cells, transcendentals=0
        ),
    )(rows)


def tile_kernel(cells, steps, at, r_ref, p0, p1, p2, p3, rs_ref, own, send, cst, cbuf, acc, s_acc, q_acc):
    k = pl.program_id(0)

    @pl.when(k == 0)
    def _():
        acc[...] = jnp.zeros_like(acc)
        s_acc[...] = jnp.zeros_like(s_acc)
        q_acc[...] = jnp.zeros_like(q_acc)

    for i, p in enumerate((p0, p1, p2, p3)):
        cbuf[pl.ds(pl.multiple_of(at[1 + i] * 64, 64), 64), :] = p[...]
    c = cbuf[...]
    acc[...] += lax.dot_general(r_ref[...], c, NT, preferred_element_type=jnp.float32)
    wide = c.astype(jnp.float32)
    s_acc[...] += fold(wide)
    q_acc[...] += fold(wide * wide)

    @pl.when(k == steps - 1)
    def _():
        half = own.shape[0]
        s = lane_sums(s_acc[...]) * (1.0 / cells)
        q = lane_sums(q_acc[...]) * (1.0 / cells)
        row = lax.broadcasted_iota(jnp.int32, cst.shape, 0)
        cst[...] = jnp.where(row == 0, s, q)
        mean = s[0:1, :]
        il = lax.rsqrt(q[0:1, :] - mean * mean + EPS)
        mine = pl.multiple_of(at[0] * half, half)
        other = pl.multiple_of((1 - at[0]) * half, half)
        cov = acc[pl.ds(mine, half), :] * (1.0 / cells) - rs_ref[pl.ds(mine, half), 0:1] * mean
        own[...] = cov
        cov = acc[pl.ds(other, half), :] * (1.0 / cells) - rs_ref[pl.ds(other, half), 0:1] * mean
        send[...] = encode(cov * rs_ref[pl.ds(other, half), 1:2] * il)


def tile(rows, pieces, rstat, half_id, slots):
    n, cells = rows.shape
    steps, half = 4, n // 2
    at = jnp.stack([half_id, *slots]).astype(jnp.int32)
    width = cells // steps
    piece = pl.BlockSpec((64, width), lambda k, at: (0, k))
    fixed = lambda shape: pl.BlockSpec(shape, lambda k, at: (0, 0))
    return pl.pallas_call(
        functools.partial(tile_kernel, cells, steps),
        grid_spec=pltpu.PrefetchScalarGridSpec(
            num_scalar_prefetch=1,
            grid=(steps,),
            in_specs=[pl.BlockSpec((n, width), lambda k, at: (0, k))]
            + [piece] * 4
            + [fixed((n, 128))],
            out_specs=[fixed((half, 256)), fixed((half, 256)), fixed((8, 256))],
            scratch_shapes=[
                pltpu.VMEM((256, width), jnp.bfloat16),
                pltpu.VMEM((n, 256), jnp.float32),
                pltpu.VMEM((256, 128), jnp.float32),
                pltpu.VMEM((256, 128), jnp.float32),
            ],
        ),
        out_shape=[
            jax.ShapeDtypeStruct((half, 256), jnp.float32),
            jax.ShapeDtypeStruct((half, 256), jnp.int16),
            jax.ShapeDtypeStruct((8, 256), jnp.float32),
        ],
        cost_estimate=pl.CostEstimate(
            flops=2 * n * 256 * cells, bytes_accessed=2 * (n + 256) * cells, transcendentals=0
        ),
    )(at, rows, *pieces, rstat)


def merged(mean, mean2, sq, sq2):
    total = 0.5 * (mean + mean2)
    inv = lax.rsqrt(0.5 * (sq + sq2) - total * total + EPS)
    return inv, jnp.sqrt(sq2 - mean2 * mean2 + EPS) * inv, (mean - mean2) * inv


def row_factors(lane, lane2, half_id):
    half = lane.shape[1] // 2
    cut = lambda v, i: lax.dynamic_slice_in_dim(v[i], half_id * half, half)
    three = merged(cut(lane, 0), cut(lane2, 0), cut(lane, 1), cut(lane2, 1))
    return jnp.pad(jnp.stack(three, axis=1), ((0, 0), (0, 125)))


def joined(own, recv, rf, cst, cst2):
    u, v, w = merged(cst[0:1, :], cst2[0:1, :], cst[1:2, :], cst2[1:2, :])
    return (
        0.5 * own * (rf[:, 0:1] * u)
        + 0.5 * decode(recv) * (rf[:, 1:2] * v)
        + 0.25 * (rf[:, 2:3] * w)
    )


def back_kernel(own, recv, rf, cst, cst2, out):
    out[...] = encode(joined(own[...], recv[...], rf[...], cst[...], cst2[...]))


def final_kernel(at, rf, back, *refs):
    out = refs[-1]
    r = rf[...]
    slot = lax.broadcasted_iota(jnp.int32, (1, 256), 1) // 64
    for k in range(4):
        own, recv, cst, cst2 = refs[4 * k : 4 * k + 4]
        value = joined(own[...], recv[...], r, cst[...], cst2[...])
        piece = decode(back[...])[:, 64 * k : 64 * k + 64]
        far = jnp.concatenate([piece] * 4, axis=1)
        where = pl.multiple_of(at[1 + k] * 256, 256)
        out[:, pl.ds(where, 256)] = jnp.where(slot == at[0], far, value)


def local(counts, size_factors, gene_means, dispersions, block_order):
    row, h = lax.axis_index("row"), lax.axis_index("cell")
    zl, y = row // NY, row % NY
    a = residuals(counts, size_factors, gene_means, dispersions, block_order)
    rows = lax.all_gather(a, "col", axis=0, tiled=True)
    z = [a] + [move(a, zl=k) for k in (1, 2, 3)]
    far_rows = lax.all_gather(move(a, y=2), "col", axis=0, tiled=True)
    rstat, rlane = row_stats(rows)
    fstat, flane = row_stats(far_rows)
    rf = row_factors(rlane, move(rlane, h=1), h)
    ff = row_factors(flane, move(flane, h=1), h)

    slots = [(y - 1) % NY, y, (y + 1) % NY, (y + 2) % NY]
    refs = []
    for k in range(ZL):
        pieces = (move(z[k], y=1), z[k], move(z[k], y=-1), z[k])
        own, send, cst = tile(rows, pieces, rstat, h, slots)
        refs += [own, move(send, h=1), cst, move(cst, h=1)]

    own, send, cst = tile(far_rows, z, fstat, h, [jnp.int32(k) for k in range(4)])
    back = pl.pallas_call(
        back_kernel, out_shape=jax.ShapeDtypeStruct(send.shape, jnp.int16)
    )(own, move(send, h=1), ff, cst, move(cst, h=1))
    back = move(back, y=2)

    at = jnp.stack([(y + 2) % NY] + [(zl - k) % ZL for k in range(ZL)]).astype(jnp.int32)
    whole = pl.BlockSpec(memory_space=pltpu.VMEM)
    result = pl.pallas_call(
        final_kernel,
        in_specs=[pl.BlockSpec(memory_space=pltpu.SMEM)] + [whole] * (2 + len(refs)),
        out_specs=whole,
        out_shape=jax.ShapeDtypeStruct((own.shape[0], 1024), jnp.float32),
    )(at, rf, back, *refs)
    return result[:, None, :]


def solution(mesh):
    return jax.shard_map(
        local,
        mesh=mesh,
        in_specs=(P(("row", "col"), "cell"), P("cell"), P(), P(), P()),
        out_specs=P(("row", "cell"), "col", None),
        check_vma=False,
    )
```

time: 323 us -> 199 us (0.62); the launches traced: 318 us -> 198 us
  waiting for transfers between devices: 276 us -> 65.2 us
  starting transfers between devices: 0.08 us -> 55.9 us
  Pallas kernels: 0 us -> 48.6 us
  other arithmetic: 13.5 us -> 2.49 us
  matrix products: 9.39 us -> 0 us
  local copies, waits for them, and re-layouts: 4.81 us -> 11.9 us
    all_gather x3 -> x2, waiting for transfers between devices: 276 us -> 0.02 us  [the longest x1 0.02 us: local(): far_rows = lax.all_gather(move(a, y=2), 'col', axis=0, tiled=True)]
    ppermute x0 -> x25, waiting for transfers between devices: none -> 65.1 us  [move(): return lax.ppermute(value, AXES, shift(**steps))]
    ppermute x0 -> x25, starting transfers between devices: none -> 55.8 us  [move(): return lax.ppermute(value, AXES, shift(**steps))]
    pallas_call x0 -> x9, Pallas kernels: none -> 48.6 us  [the longest x5 33.8 us: tile(): pl.pallas_call(functools.partial(tile_kernel, cells, steps), grid_spec=pl...]
    reduce_sum x2 -> x0, other arithmetic: 11.1 us -> none  [row_moments(): total = jnp.sum(values, axis=1, dtype=jnp.float32)]
    dot_general x1 -> x0, matrix products: 9.39 us -> none  [column_terms(): lax.dot_general(rows_res, piece, (((1,), (1,)), ((), ())), preferred_elem...]
  transfers between devices with their start and end apart: 3 -> 27, of which waited for: 3 -> 9; matrix products, arithmetic and copies ran while one was open for 1% -> 2% of each run, Pallas kernels for 0% -> 23%
where the time goes in v1:
time: 199 us; the launch traced here: 198 us
  waiting for transfers between devices  65.2 us (33%)
  starting transfers between devices  55.9 us (28%)
  Pallas kernels  48.6 us (24%)
  between operations  14.4 us (7%)
  local copies, waits for them, and re-layouts  11.9 us (6%)
  other arithmetic  2.49 us (1%)
    ppermute x25, waiting for transfers between devices, move(): return lax.ppermute(value, AXES, shift(**steps))  65.1 us
    ppermute x25, starting transfers between devices, move(): return lax.ppermute(value, AXES, shift(**steps))  55.8 us
    pallas_call x5, Pallas kernels, tile(): pl.pallas_call(functools.partial(tile_kernel, cells, steps), grid_spec=pl...  33.8 us
    pallas_call x2, Pallas kernels, row_stats(): pl.pallas_call(functools.partial(stats_kernel, cells, steps), grid=(steps...  9.46 us
  transfers between devices with their start and end apart: 27, of which 9 were waited for; matrix products, arithmetic and copies ran while one was open for 2% of the time, Pallas kernels for 23%

profile of v1, /device:TPU:26, one launch (start us, length us, event | category | flops | bytes accessed | tf_op | source)
XLA Modules:
  0.0 198.4 jit_solution(11931299349183818146)
XLA Ops:
  13.8 14.1 %collective-permute-done.1 = bf16[64,4096]{1,0:T(8,128)(2,1)S(1)} collective-permute-done((bf16[64,4096]{1,0:T(8,128)(2,1)}, bf16[64,4096]{1,0:T(8,128)(2,1)S(1)}, u32[]{:S(2)}, u32[]{:S(2)}) %collective-permute-start.1) | collective-permute-done | bytes 524320 | tf_op jit(solution)/shard_map/ppermute | solution.py:29
  28.8 4.7 %collective-permute-start.4 = (bf16[64,4096]{1,0:T(8,128)(2,1)}, bf16[64,4096]{1,0:T(8,128)(2,1)S(1)}, u32[]{:S(2)}, u32[]{:S(2)}) collective-permute-start(bf16[64,4096]{1,0:T(8,128)(2,1)} %fusion.2.p0.p1.p3), channel_id=1, source_target_pairs={{0,192},{1,193},{2,194},{3,195},{4,196},{5,197},{6,198},{7,199},{8... | collective-permute-start | bytes 1572872 | tf_op jit(solution)/shard_map/ppermute | solution.py:29
  34.2 2.5 %collective-permute-start.9 = (bf16[64,4096]{1,0:T(8,128)(2,1)}, bf16[64,4096]{1,0:T(8,128)(2,1)}, u32[]{:S(2)}, u32[]{:S(2)}) collective-permute-start(bf16[64,4096]{1,0:T(8,128)(2,1)} %fusion.2.p0.p1.p3), channel_id=1, source_target_pairs={{0,16},{1,17},{2,18},{3,19},{4,20},{5,21},{6,22},{7,23},{8,24},{9,... | collective-permute-start | bytes 1572872 | tf_op jit(solution)/shard_map/ppermute | solution.py:29
  37.4 8.8 %collective-permute-done.4.p3.p1 = bf16[64,4096]{1,0:T(8,128)(2,1)S(1)} collective-permute-done((bf16[64,4096]{1,0:T(8,128)(2,1)}, bf16[64,4096]{1,0:T(8,128)(2,1)S(1)}, u32[]{:S(2)}, u32[]{:S(2)}) %collective-permute-start.4) | collective-permute-done | bytes 524320 | tf_op jit(solution)/shard_map/ppermute | solution.py:29
  49.4 27.6 %collective-permute-done.3.p2.p1.p3 = bf16[64,4096]{1,0:T(8,128)(2,1)S(1)} collective-permute-done((bf16[64,4096]{1,0:T(8,128)(2,1)}, bf16[64,4096]{1,0:T(8,128)(2,1)S(1)}, u32[]{:S(2)}, u32[]{:S(2)}) %collective-permute-start.3) | collective-permute-done | bytes 524320 | tf_op jit(solution)/shard_map/ppermute | solution.py:29
  77.8 2.5 %collective-permute-start.17 = (bf16[64,4096]{1,0:T(8,128)(2,1)S(1)}, bf16[64,4096]{1,0:T(8,128)(2,1)}, u32[]{:S(2)}, u32[]{:S(2)}) collective-permute-start(bf16[64,4096]{1,0:T(8,128)(2,1)S(1)} %collective-permute-done.3.p2.p1.p3), channel_id=1, source_target_pairs={{0,16},{1,17},{2,18},{3,19},{4,20},{5,21},{6,22},{7,23},{8,24},{9,... | collective-permute-start | bytes 1572872 | tf_op jit(solution)/shard_map/ppermute | solution.py:29
  81.6 4.7 %shard_map.55 = (f32[512,128]{1,0:T(8,128)}, f32[8,512]{1,0:T(8,128)}) custom-call(bf16[512,4096]{1,0:T(8,128)(2,1)} %all-gather.3.cloned.1.call-done.r_ref), custom_call_target="tpu_custom_call" | custom-call | flops 8388608 | bytes 4194304 | tf_op jit(solution)/shard_map/pallas_call | solution.py:98
  86.5 3.2 %collective-permute-start.13 = (bf16[64,4096]{1,0:T(8,128)(2,1)S(1)}, bf16[64,4096]{1,0:T(8,128)(2,1)}, u32[]{:S(2)}, u32[]{:S(2)}) collective-permute-start(bf16[64,4096]{1,0:T(8,128)(2,1)S(1)} %collective-permute-done.2.p1.p3), channel_id=1, source_target_pairs={{0,16},{1,17},{2,18},{3,19},{4,20},{5,21},{6,22},{7,23},{8,24},{9,... | collective-permute-start | bytes 1572872 | tf_op jit(solution)/shard_map/ppermute | solution.py:29
  89.7 6.7 %shard_map.59 = (f32[256,256]{1,0:T(8,128)}, s16[256,256]{1,0:T(8,128)(2,1)}, f32[8,256]{1,0:T(8,128)}) custom-call(s32[5]{0:T(128)} %stack.81.at, bf16[512,4096]{1,0:T(8,128)(2,1)} %all-gather.3.cloned.1.call-done.r_ref, bf16[64,4096]{1,0:T(8,128)(2,1)} %collective-permute-done.9.p0, bf16[64,4096]{1,0:T(8,128)(2,1)} %fusion.2.p0.p1.p3, ...), custom_call_target="tpu_custom_call" | custom-call | flops 1073741824 | bytes 6291456 | tf_op jit(solution)/shard_map/pallas_call | solution.py:155
  96.5 6.4 %collective-permute-start = (f32[8,512]{1,0:T(8,128)S(1)}, f32[8,512]{1,0:T(8,128)S(1)}, u32[]{:S(2)}, u32[]{:S(2)}) collective-permute-start(f32[8,512]{1,0:T(8,128)S(1)} %copy-done.20), channel_id=1, source_target_pairs={{0,1},{1,0},{2,3},{3,2},{4,5},{5,4},{6,7},{7,6},{8,9},{9,8},{10,11... | collective-permute-start | bytes 49160 | tf_op jit(solution)/shard_map/ppermute | solution.py:29
  102.9 6.8 %shard_map.62 = (f32[256,256]{1,0:T(8,128)}, s16[256,256]{1,0:T(8,128)(2,1)}, f32[8,256]{1,0:T(8,128)}) custom-call(s32[5]{0:T(128)} %stack.81.at, bf16[512,4096]{1,0:T(8,128)(2,1)} %all-gather.3.cloned.1.call-done.r_ref, bf16[64,4096]{1,0:T(8,128)(2,1)} %collective-permute-done.21.p0, bf16[64,4096]{1,0:T(8,128)(2,1)} %copy-done, ...), custom_call_target="tpu_custom_call" | custom-call | flops 1073741824 | bytes 6291456 | tf_op jit(solution)/shard_map/pallas_call | solution.py:155
  109.8 5.9 %collective-permute-start.24 = (f32[8,256]{1,0:T(8,128)}, f32[8,256]{1,0:T(8,128)S(1)}, u32[]{:S(2)}, u32[]{:S(2)}) collective-permute-start(f32[8,256]{1,0:T(8,128)} %get-tuple-element.42.refs_14_), channel_id=1, source_target_pairs={{0,1},{1,0},{2,3},{3,2},{4,5},{5,4},{6,7},{7,6},{8,9},{9,8},{10,11... | collective-permute-start | bytes 24584 | tf_op jit(solution)/shard_map/ppermute | solution.py:29
  115.7 6.8 %shard_map.61 = (f32[256,256]{1,0:T(8,128)}, s16[256,256]{1,0:T(8,128)(2,1)}, f32[8,256]{1,0:T(8,128)}) custom-call(s32[5]{0:T(128)} %stack.81.at, bf16[512,4096]{1,0:T(8,128)(2,1)} %all-gather.3.cloned.1.call-done.r_ref, bf16[64,4096]{1,0:T(8,128)(2,1)} %collective-permute-done.17.p0, bf16[64,4096]{1,0:T(8,128)(2,1)} %copy-done.1, ...), custom_call_target="tpu_custom_call" | custom-call | flops 1073741824 | bytes 6291456 | tf_op jit(solution)/shard_map/pallas_call | solution.py:155
  122.7 6.7 %shard_map.60 = (f32[256,256]{1,0:T(8,128)}, s16[256,256]{1,0:T(8,128)(2,1)}, f32[8,256]{1,0:T(8,128)}) custom-call(s32[5]{0:T(128)} %stack.81.at, bf16[512,4096]{1,0:T(8,128)(2,1)} %all-gather.3.cloned.1.call-done.r_ref, bf16[64,4096]{1,0:T(8,128)(2,1)} %collective-permute-done.13.p0, bf16[64,4096]{1,0:T(8,128)(2,1)} %copy-done.2, ...), custom_call_target="tpu_custom_call" | custom-call | flops 1073741824 | bytes 6291456 | tf_op jit(solution)/shard_map/pallas_call | solution.py:155
  129.5 4.7 %shard_map.56 = (f32[512,128]{1,0:T(8,128)}, f32[8,512]{1,0:T(8,128)}) custom-call(bf16[512,4096]{1,0:T(8,128)(2,1)} %all-gather.5.cloned.1.call-done.r_ref), custom_call_target="tpu_custom_call" | custom-call | flops 8388608 | bytes 4194304 | tf_op jit(solution)/shard_map/pallas_call | solution.py:98
  135.0 5.8 %collective-permute-start.6 = (f32[8,512]{1,0:T(8,128)}, f32[8,512]{1,0:T(8,128)S(1)}, u32[]{:S(2)}, u32[]{:S(2)}) collective-permute-start(f32[8,512]{1,0:T(8,128)} %get-tuple-element.28), channel_id=1, source_target_pairs={{0,1},{1,0},{2,3},{3,2},{4,5},{5,4},{6,7},{7,6},{8,9},{9,8},{10,11... | collective-permute-start | bytes 49160 | tf_op jit(solution)/shard_map/ppermute | solution.py:29
  140.9 6.8 %shard_map.57 = (f32[256,256]{1,0:T(8,128)}, s16[256,256]{1,0:T(8,128)(2,1)}, f32[8,256]{1,0:T(8,128)}) custom-call(s32[5]{0:T(128)} %stack.36.at, bf16[512,4096]{1,0:T(8,128)(2,1)} %all-gather.5.cloned.1.call-done.r_ref, bf16[64,4096]{1,0:T(8,128)(2,1)} %fusion.2.p0.p1.p3, bf16[64,4096]{1,0:T(8,128)(2,1)} %copy-done.2, bf16[64,4096]{1,0:T(8,128)(2,1)} %copy-done.1, ...), custom_call_target="tpu_custom_call" | custom-call | flops 1073741824 | bytes 6291456 | tf_op jit(solution)/shard_map/pallas_call | solution.py:155
  147.7 5.8 %collective-permute-start.5 = (s16[256,256]{1,0:T(8,128)(2,1)}, s16[256,256]{1,0:T(8,128)(2,1)S(1)}, u32[]{:S(2)}, u32[]{:S(2)}) collective-permute-start(s16[256,256]{1,0:T(8,128)(2,1)} %get-tuple-element.27), channel_id=1, source_target_pairs={{0,1},{1,0},{2,3},{3,2},{4,5},{5,4},{6,7},{7,6},{8,9},{9,8},{10,11... | collective-permute-start | bytes 393224 | tf_op jit(solution)/shard_map/ppermute | solution.py:29
  157.2 6.6 %collective-permute-start.11 = (s16[256,256]{1,0:T(8,128)(2,1)S(1)}, s16[256,256]{1,0:T(8,128)(2,1)S(1)}, u32[]{:S(2)}, u32[]{:S(2)}) collective-permute-start(s16[256,256]{1,0:T(8,128)(2,1)S(1)} %copy-done.21), channel_id=1, source_target_pairs={{0,1},{1,0},{2,3},{3,2},{4,5},{5,4},{6,7},{7,6},{8,9},{9,8},{10,11... | collective-permute-start | bytes 393224 | tf_op jit(solution)/shard_map/ppermute | solution.py:29
  166.6 5.4 %collective-permute-start.19 = (s16[256,256]{1,0:T(8,128)(2,1)S(1)}, s16[256,256]{1,0:T(8,128)(2,1)S(1)}, u32[]{:S(2)}, u32[]{:S(2)}) collective-permute-start(s16[256,256]{1,0:T(8,128)(2,1)S(1)} %copy-done.23), channel_id=1, source_target_pairs={{0,1},{1,0},{2,3},{3,2},{4,5},{5,4},{6,7},{7,6},{8,9},{9,8},{10,11... | collective-permute-start | bytes 393224 | tf_op jit(solution)/shard_map/ppermute | solution.py:29
  174.2 5.8 %collective-permute-done.23.refs_13_ = s16[256,256]{1,0:T(8,128)(2,1)S(1)} collective-permute-done((s16[256,256]{1,0:T(8,128)(2,1)S(1)}, s16[256,256]{1,0:T(8,128)(2,1)S(1)}, u32[]{:S(2)}, u32[]{:S(2)}) %collective-permute-start.23) | collective-permute-done | bytes 131104 | tf_op jit(solution)/shard_map/ppermute | solution.py:29
  180.0 2.5 %collective-permute-done.19.refs_9_ = s16[256,256]{1,0:T(8,128)(2,1)S(1)} collective-permute-done((s16[256,256]{1,0:T(8,128)(2,1)S(1)}, s16[256,256]{1,0:T(8,128)(2,1)S(1)}, u32[]{:S(2)}, u32[]{:S(2)}) %collective-permute-start.19) | collective-permute-done | bytes 131104 | tf_op jit(solution)/shard_map/ppermute | solution.py:29
  184.9 3.3 %shard_map.63 = f32[256,1024]{1,0:T(8,128)} custom-call(s32[5]{0:T(128)} %stack.33.at, f32[256,128]{1,0:T(8,128)} %pad.7.rf, s16[256,256]{1,0:T(8,128)(2,1)} %copy-done.11, f32[256,256]{1,0:T(8,128)} %get-tuple-element.31.refs_0_, s16[256,256]{1,0:T(8,128)(2,1)} %copy-done.7, f32[8,256]{1,0:T(8,128)} %get-tuple-element.33.refs_2_, f32[8,256]{1,0:T(8,128)} %copy-done.14, ...), custom_call_target="tpu_custom_call" | custom-call | tf_op jit(solution)/shard_map/pallas_call | solution.py:248
  188.3 3.3 %copy.20 = f32[256,1,1024]{2,1,0:T(1,128)} copy(f32[256,1,1024]{2,0,1:T(8,128)} %bitcast.25) | data formatting | bytes 2097152 | tf_op jit(solution)/shard_map/broadcast_in_dim | solution.py:254
  (112 shorter events, 26.4 us)
Async XLA Ops:
  6.5 75.1 %all-gather.3.cloned.1.call-start = ((), (), s32[]{:S(2)}) async-start(), calls=%async_computation | async-start | bytes 4718592 | tf_op jit(solution)/shard_map/all_gather | solution.py:225
  12.4 117.1 %all-gather.5.cloned.1.call-start = ((), (), s32[]{:S(2)}) async-start(), calls=%async_computation.1 | async-start | bytes 4718592 | tf_op jit(solution)/shard_map/all_gather | solution.py:227
  12.4 15.5 %collective-permute-start.1 = (bf16[64,4096]{1,0:T(8,128)(2,1)}, bf16[64,4096]{1,0:T(8,128)(2,1)S(1)}, u32[]{:S(2)}, u32[]{:S(2)}) collective-permute-start(bf16[64,4096]{1,0:T(8,128)(2,1)} %fusion.2.p0.p1.p3), channel_id=1, source_target_pairs={{0,32},{1,33},{2,34},{3,35},{4,36},{5,37},{6,38},{7,39},{8,40},{9,... | collective-permute-start | bytes 1572872 | tf_op jit(solution)/shard_map/ppermute | solution.py:29
  28.8 17.4 %collective-permute-start.4 = (bf16[64,4096]{1,0:T(8,128)(2,1)}, bf16[64,4096]{1,0:T(8,128)(2,1)S(1)}, u32[]{:S(2)}, u32[]{:S(2)}) collective-permute-start(bf16[64,4096]{1,0:T(8,128)(2,1)} %fusion.2.p0.p1.p3), channel_id=1, source_target_pairs={{0,192},{1,193},{2,194},{3,195},{4,196},{5,197},{6,198},{7,199},{8... | collective-permute-start | bytes 1572872 | tf_op jit(solution)/shard_map/ppermute | solution.py:29
  33.5 15.2 %collective-permute-start.10 = (bf16[64,4096]{1,0:T(8,128)(2,1)}, bf16[64,4096]{1,0:T(8,128)(2,1)S(1)}, u32[]{:S(2)}, u32[]{:S(2)}) collective-permute-start(bf16[64,4096]{1,0:T(8,128)(2,1)} %fusion.2.p0.p1.p3), channel_id=1, source_target_pairs={{0,48},{1,49},{2,50},{3,51},{4,52},{5,53},{6,54},{7,55},{8,56},{9,... | collective-permute-start | bytes 1572872 | tf_op jit(solution)/shard_map/ppermute | solution.py:29
  34.2 42.9 %collective-permute-start.3 = (bf16[64,4096]{1,0:T(8,128)(2,1)}, bf16[64,4096]{1,0:T(8,128)(2,1)S(1)}, u32[]{:S(2)}, u32[]{:S(2)}) collective-permute-start(bf16[64,4096]{1,0:T(8,128)(2,1)} %fusion.2.p0.p1.p3), channel_id=1, source_target_pairs={{0,128},{1,129},{2,130},{3,131},{4,132},{5,133},{6,134},{7,135},{8... | collective-permute-start | bytes 1572872 | tf_op jit(solution)/shard_map/ppermute | solution.py:29
  34.2 43.6 %collective-permute-start.9 = (bf16[64,4096]{1,0:T(8,128)(2,1)}, bf16[64,4096]{1,0:T(8,128)(2,1)}, u32[]{:S(2)}, u32[]{:S(2)}) collective-permute-start(bf16[64,4096]{1,0:T(8,128)(2,1)} %fusion.2.p0.p1.p3), channel_id=1, source_target_pairs={{0,16},{1,17},{2,18},{3,19},{4,20},{5,21},{6,22},{7,23},{8,24},{9,... | collective-permute-start | bytes 1572872 | tf_op jit(solution)/shard_map/ppermute | solution.py:29
  36.7 49.6 %collective-permute-start.2 = (bf16[64,4096]{1,0:T(8,128)(2,1)}, bf16[64,4096]{1,0:T(8,128)(2,1)S(1)}, u32[]{:S(2)}, u32[]{:S(2)}) collective-permute-start(bf16[64,4096]{1,0:T(8,128)(2,1)} %fusion.2.p0.p1.p3), channel_id=1, source_target_pairs={{0,64},{1,65},{2,66},{3,67},{4,68},{5,69},{6,70},{7,71},{8,72},{9,... | collective-permute-start | bytes 1572872 | tf_op jit(solution)/shard_map/ppermute | solution.py:29
  46.2 40.2 %collective-permute-start.22 = (bf16[64,4096]{1,0:T(8,128)(2,1)S(1)}, bf16[64,4096]{1,0:T(8,128)(2,1)S(1)}, u32[]{:S(2)}, u32[]{:S(2)}) collective-permute-start(bf16[64,4096]{1,0:T(8,128)(2,1)S(1)} %collective-permute-done.4.p3.p1), channel_id=1, source_target_pairs={{0,48},{1,49},{2,50},{3,51},{4,52},{5,53},{6,54},{7,55},{8,56},{9,... | collective-permute-start | bytes 1572872 | tf_op jit(solution)/shard_map/ppermute | solution.py:29
  48.6 47.8 %collective-permute-start.21 = (bf16[64,4096]{1,0:T(8,128)(2,1)S(1)}, bf16[64,4096]{1,0:T(8,128)(2,1)}, u32[]{:S(2)}, u32[]{:S(2)}) collective-permute-start(bf16[64,4096]{1,0:T(8,128)(2,1)S(1)} %collective-permute-done.4.p3.p1), channel_id=1, source_target_pairs={{0,16},{1,17},{2,18},{3,19},{4,20},{5,21},{6,22},{7,23},{8,24},{9,... | collective-permute-start | bytes 1572872 | tf_op jit(solution)/shard_map/ppermute | solution.py:29
  77.1 32.6 %collective-permute-start.18 = (bf16[64,4096]{1,0:T(8,128)(2,1)S(1)}, bf16[64,4096]{1,0:T(8,128)(2,1)S(1)}, u32[]{:S(2)}, u32[]{:S(2)}) collective-permute-start(bf16[64,4096]{1,0:T(8,128)(2,1)S(1)} %collective-permute-done.3.p2.p1.p3), channel_id=1, source_target_pairs={{0,48},{1,49},{2,50},{3,51},{4,52},{5,53},{6,54},{7,55},{8,56},{9,... | collective-permute-start | bytes 1572872 | tf_op jit(solution)/shard_map/ppermute | solution.py:29
  77.8 31.9 %collective-permute-start.17 = (bf16[64,4096]{1,0:T(8,128)(2,1)S(1)}, bf16[64,4096]{1,0:T(8,128)(2,1)}, u32[]{:S(2)}, u32[]{:S(2)}) collective-permute-start(bf16[64,4096]{1,0:T(8,128)(2,1)S(1)} %collective-permute-done.3.p2.p1.p3), channel_id=1, source_target_pairs={{0,16},{1,17},{2,18},{3,19},{4,20},{5,21},{6,22},{7,23},{8,24},{9,... | collective-permute-start | bytes 1572872 | tf_op jit(solution)/shard_map/ppermute | solution.py:29
  86.3 36.1 %collective-permute-start.14 = (bf16[64,4096]{1,0:T(8,128)(2,1)S(1)}, bf16[64,4096]{1,0:T(8,128)(2,1)}, u32[]{:S(2)}, u32[]{:S(2)}) collective-permute-start(bf16[64,4096]{1,0:T(8,128)(2,1)S(1)} %collective-permute-done.2.p1.p3), channel_id=1, source_target_pairs={{0,48},{1,49},{2,50},{3,51},{4,52},{5,53},{6,54},{7,55},{8,56},{9,... | collective-permute-start | bytes 1572872 | tf_op jit(solution)/shard_map/ppermute | solution.py:29
  86.5 36.2 %collective-permute-start.13 = (bf16[64,4096]{1,0:T(8,128)(2,1)S(1)}, bf16[64,4096]{1,0:T(8,128)(2,1)}, u32[]{:S(2)}, u32[]{:S(2)}) collective-permute-start(bf16[64,4096]{1,0:T(8,128)(2,1)S(1)} %collective-permute-done.2.p1.p3), channel_id=1, source_target_pairs={{0,16},{1,17},{2,18},{3,19},{4,20},{5,21},{6,22},{7,23},{8,24},{9,... | collective-permute-start | bytes 1572872 | tf_op jit(solution)/shard_map/ppermute | solution.py:29
  96.5 33.0 %collective-permute-start = (f32[8,512]{1,0:T(8,128)S(1)}, f32[8,512]{1,0:T(8,128)S(1)}, u32[]{:S(2)}, u32[]{:S(2)}) collective-permute-start(f32[8,512]{1,0:T(8,128)S(1)} %copy-done.20), channel_id=1, source_target_pairs={{0,1},{1,0},{2,3},{3,2},{4,5},{5,4},{6,7},{7,6},{8,9},{9,8},{10,11... | collective-permute-start | bytes 49160 | tf_op jit(solution)/shard_map/ppermute | solution.py:29
  109.7 56.2 %collective-permute-start.12 = (f32[8,256]{1,0:T(8,128)S(1)}, f32[8,256]{1,0:T(8,128)S(1)}, u32[]{:S(2)}, u32[]{:S(2)}) collective-permute-start(f32[8,256]{1,0:T(8,128)S(1)} %copy-done.13), channel_id=1, source_target_pairs={{0,1},{1,0},{2,3},{3,2},{4,5},{5,4},{6,7},{7,6},{8,9},{9,8},{10,11... | collective-permute-start | bytes 24584 | tf_op jit(solution)/shard_map/ppermute | solution.py:29
  109.8 56.8 %collective-permute-start.24 = (f32[8,256]{1,0:T(8,128)}, f32[8,256]{1,0:T(8,128)S(1)}, u32[]{:S(2)}, u32[]{:S(2)}) collective-permute-start(f32[8,256]{1,0:T(8,128)} %get-tuple-element.42.refs_14_), channel_id=1, source_target_pairs={{0,1},{1,0},{2,3},{3,2},{4,5},{5,4},{6,7},{7,6},{8,9},{9,8},{10,11... | collective-permute-start | bytes 24584 | tf_op jit(solution)/shard_map/ppermute | solution.py:29
  122.5 49.5 %collective-permute-start.20 = (f32[8,256]{1,0:T(8,128)}, f32[8,256]{1,0:T(8,128)S(1)}, u32[]{:S(2)}, u32[]{:S(2)}) collective-permute-start(f32[8,256]{1,0:T(8,128)} %get-tuple-element.39.refs_10_), channel_id=1, source_target_pairs={{0,1},{1,0},{2,3},{3,2},{4,5},{5,4},{6,7},{7,6},{8,9},{9,8},{10,11... | collective-permute-start | bytes 24584 | tf_op jit(solution)/shard_map/ppermute | solution.py:29
  135.0 12.7 %collective-permute-start.6 = (f32[8,512]{1,0:T(8,128)}, f32[8,512]{1,0:T(8,128)S(1)}, u32[]{:S(2)}, u32[]{:S(2)}) collective-permute-start(f32[8,512]{1,0:T(8,128)} %get-tuple-element.28), channel_id=1, source_target_pairs={{0,1},{1,0},{2,3},{3,2},{4,5},{5,4},{6,7},{7,6},{8,9},{9,8},{10,11... | collective-permute-start | bytes 49160 | tf_op jit(solution)/shard_map/ppermute | solution.py:29
  155.5 17.2 %collective-permute-start.16 = (f32[8,256]{1,0:T(8,128)S(1)}, f32[8,256]{1,0:T(8,128)S(1)}, u32[]{:S(2)}, u32[]{:S(2)}) collective-permute-start(f32[8,256]{1,0:T(8,128)S(1)} %copy-done.17), channel_id=1, source_target_pairs={{0,1},{1,0},{2,3},{3,2},{4,5},{5,4},{6,7},{7,6},{8,9},{9,8},{10,11... | collective-permute-start | bytes 24584 | tf_op jit(solution)/shard_map/ppermute | solution.py:29
  157.2 17.0 %collective-permute-start.11 = (s16[256,256]{1,0:T(8,128)(2,1)S(1)}, s16[256,256]{1,0:T(8,128)(2,1)S(1)}, u32[]{:S(2)}, u32[]{:S(2)}) collective-permute-start(s16[256,256]{1,0:T(8,128)(2,1)S(1)} %copy-done.21), channel_id=1, source_target_pairs={{0,1},{1,0},{2,3},{3,2},{4,5},{5,4},{6,7},{7,6},{8,9},{9,8},{10,11... | collective-permute-start | bytes 393224 | tf_op jit(solution)/shard_map/ppermute | solution.py:29
  165.9 14.2 %collective-permute-start.23 = (s16[256,256]{1,0:T(8,128)(2,1)S(1)}, s16[256,256]{1,0:T(8,128)(2,1)S(1)}, u32[]{:S(2)}, u32[]{:S(2)}) collective-permute-start(s16[256,256]{1,0:T(8,128)(2,1)S(1)} %copy-done.22), channel_id=1, source_target_pairs={{0,1},{1,0},{2,3},{3,2},{4,5},{5,4},{6,7},{7,6},{8,9},{9,8},{10,11... | collective-permute-start | bytes 393224 | tf_op jit(solution)/shard_map/ppermute | solution.py:29
  166.6 15.9 %collective-permute-start.19 = (s16[256,256]{1,0:T(8,128)(2,1)S(1)}, s16[256,256]{1,0:T(8,128)(2,1)S(1)}, u32[]{:S(2)}, u32[]{:S(2)}) collective-permute-start(s16[256,256]{1,0:T(8,128)(2,1)S(1)} %copy-done.23), channel_id=1, source_target_pairs={{0,1},{1,0},{2,3},{3,2},{4,5},{5,4},{6,7},{7,6},{8,9},{9,8},{10,11... | collective-permute-start | bytes 393224 | tf_op jit(solution)/shard_map/ppermute | solution.py:29
  172.0 12.2 %collective-permute-start.15 = (s16[256,256]{1,0:T(8,128)(2,1)S(1)}, s16[256,256]{1,0:T(8,128)(2,1)S(1)}, u32[]{:S(2)}, u32[]{:S(2)}) collective-permute-start(s16[256,256]{1,0:T(8,128)(2,1)S(1)} %copy-done.24), channel_id=1, source_target_pairs={{0,1},{1,0},{2,3},{3,2},{4,5},{5,4},{6,7},{7,6},{8,9},{9,8},{10,11... | collective-permute-start | bytes 393224 | tf_op jit(solution)/shard_map/ppermute | solution.py:29
  (28 other events, 447.7 us)
Sparse Core Ops, SparseCore 0:
  12.5 36.3 all-gather.2
  50.7 34.6 all-gather.4

commit v2 on v0

v2 whole, which is shorter than its diff:
```python
import functools
import math

import jax
import jax.numpy as jnp
import numpy as np
from jax import lax
from jax.experimental import pallas as pl
from jax.experimental.pallas import tpu as pltpu
from jax.sharding import PartitionSpec as P

AXES = ("row", "col", "cell")
ZL, NY, NX, NC, NH = 4, 4, 4, 2, 2
EPS = 1e-05
FULL = 32767.0
BOUND = 96.0
NT = (((1,), (1,)), ((), ()))


def shift(zl=0, y=0, x=0, c=0, h=0):
    dims, step, pairs = (ZL, NY, NX, NC, NH), (zl, y, x, c, h), []
    for i in range(math.prod(dims)):
        at = np.unravel_index(i, dims)
        to = [(int(a) + s) % d for a, s, d in zip(at, step, dims)]
        pairs.append((i, int(np.ravel_multi_index(to, dims))))
    return pairs


def move(value, **steps):
    return lax.ppermute(value, AXES, shift(**steps))


def resid_kernel(limit, place, order, counts, size, mean, disp, out, turned):
    genes = out.shape[0]
    block = order[place[0]]
    line = block * genes // 128
    start = pl.multiple_of(block * genes % 128, genes)
    both = [ref[pl.ds(line, 1), :] for ref in (mean, disp)]
    index = lax.broadcasted_iota(jnp.int32, (8, 128), 0)
    turned[...] = jnp.where(index == 0, both[0], both[1]).T
    mean_gene = turned[pl.ds(start, genes), 0:1]
    spare = 1.0 / turned[pl.ds(start, genes), 1:2]
    for i in range(0, out.shape[1], 512):
        span = slice(i, i + 512)
        expected = mean_gene * size[:, span]
        scale = lax.rsqrt(expected + expected * expected * spare)
        value = (counts[:, span].astype(jnp.float32) - expected) * scale
        out[:, span] = jnp.clip(value, -limit, limit).astype(jnp.bfloat16)


def residuals(counts, size_factors, gene_means, dispersions, block_order):
    genes, cells = counts.shape
    place = lax.axis_index(("row", "col")).astype(jnp.int32)
    smem, vmem = pl.BlockSpec(memory_space=pltpu.SMEM), pl.BlockSpec(memory_space=pltpu.VMEM)
    return pl.pallas_call(
        functools.partial(resid_kernel, math.sqrt(cells * NH)),
        in_specs=[smem, smem, vmem, vmem, vmem, vmem],
        out_specs=vmem,
        out_shape=jax.ShapeDtypeStruct((genes, cells), jnp.bfloat16),
        scratch_shapes=[pltpu.VMEM((128, 8), jnp.float32)],
    )(
        place[None],
        block_order,
        counts,
        size_factors[None, :],
        gene_means.reshape(-1, 128),
        dispersions.reshape(-1, 128),
    )


def encode(p):
    root = jnp.minimum(jnp.sqrt(jnp.abs(p)), 1.0) * FULL + 0.5
    return jnp.where(p < 0, -root, root).astype(jnp.int32).astype(jnp.int16)


def decode(q):
    f = q.astype(jnp.int32).astype(jnp.float32)
    return f * jnp.abs(f) * (1.0 / (FULL * FULL))


def split(v):
    t = v * (FULL / BOUND)
    high = jnp.round(t)
    return high, jnp.round((t - high) * (2 * FULL))


def unsplit(high, low):
    return (high + low * (0.5 / FULL)) * (BOUND / FULL)


def pack(rows):
    index = lax.broadcasted_iota(jnp.int32, (16, rows[0].shape[1]), 0)
    block = jnp.zeros(index.shape, jnp.float32)
    for i, row in enumerate(rows):
        block = jnp.where(index == i, row, block)
    return block.astype(jnp.int32).astype(jnp.int16)


def lane_sums(parts):
    ones = jnp.ones((8, 128), jnp.float32)
    return lax.dot_general(
        ones, parts, NT, precision=lax.Precision.HIGHEST, preferred_element_type=jnp.float32
    )[0:1, :]


def fold(values):
    tiles = [values[:, i : i + 128] for i in range(0, values.shape[1], 128)]
    while len(tiles) > 1:
        tiles = [a + b for a, b in zip(tiles[::2], tiles[1::2])]
    return tiles[0]


def deviation(square, mean):
    return jnp.sqrt(square - mean * mean + EPS)


def tile_kernel(cells, steps, count, parts, first, at, *refs):
    refs = list(refs)
    rows = [refs.pop(0) for _ in range(parts)]
    pieces = [refs.pop(0) for _ in range(4 * count)]
    given = None if first else refs.pop(0)
    own, msg, cst = refs.pop(0), refs.pop(0), refs.pop(0)
    rst = refs.pop(0) if first else given
    cbuf, acc, s_acc, q_acc = refs[:4]
    k = pl.program_id(0)
    half = own.shape[0]

    @pl.when(k == 0)
    def _():
        acc[...] = jnp.zeros_like(acc)
        s_acc[...] = jnp.zeros_like(s_acc)
        q_acc[...] = jnp.zeros_like(q_acc)
        if first:
            refs[4][...] = jnp.zeros_like(refs[4])
            refs[5][...] = jnp.zeros_like(refs[5])

    for i, p in enumerate(pieces):
        place = 256 * (i // 4) + at[1 + i] * 64
        cbuf[pl.ds(pl.multiple_of(place, 64), 64), :] = p[...]
    if parts == 1:
        r = rows[0][...]
    else:
        rbuf = refs[6]
        for j, part in enumerate(rows):
            for i in range(part.shape[0] // 64):
                place = at[1 + 4 * count + 4 * j + i] * 64
                rbuf[pl.ds(pl.multiple_of(place, 64), 64), :] = part[64 * i : 64 * i + 64, :]
        r = rbuf[...]
    c = cbuf[...]
    acc[...] += lax.dot_general(r, c, NT, preferred_element_type=jnp.float32)
    wide = c.astype(jnp.float32)
    s_acc[...] += fold(wide)
    q_acc[...] += fold(wide * wide)
    if first:
        wide = r.astype(jnp.float32)
        refs[4][...] += fold(wide)
        refs[5][...] += fold(wide * wide)

    @pl.when(k == steps - 1)
    def _():
        scale = 1.0 / cells
        mine = pl.multiple_of(at[0] * half, half)
        other = pl.multiple_of((1 - at[0]) * half, half)
        extra = []
        if first:
            rs, rq = refs[4], refs[5]
            mean = jnp.sum(rs[...], axis=1, keepdims=True) * scale
            dev = deviation(jnp.sum(rq[...], axis=1, keepdims=True) * scale, mean)
            lane = lax.broadcasted_iota(jnp.int32, rst.shape, 1)
            rst[...] = jnp.where(lane == 0, mean, dev)
            mean = lane_sums(rs[pl.ds(other, half), :]) * scale
            dev = deviation(lane_sums(rq[pl.ds(other, half), :]) * scale, mean)
            extra = [*split(mean), *split(dev)]
        for t in range(count):
            span = slice(256 * t, 256 * t + 256)
            mean = lane_sums(s_acc[span, :]) * scale
            dev = deviation(lane_sums(q_acc[span, :]) * scale, mean)
            row = lax.broadcasted_iota(jnp.int32, (8, 256), 0)
            cst[8 * t : 8 * t + 8, :] = jnp.where(row == 0, mean, dev)
            cov = acc[pl.ds(mine, half), span] * scale - rst[pl.ds(mine, half), 0:1] * mean
            own[:, span] = cov
            cov = acc[pl.ds(other, half), span] * scale - rst[pl.ds(other, half), 0:1] * mean
            base = (half + 16) * t
            msg[base : base + half, :] = encode(
                cov * ((1.0 / rst[pl.ds(other, half), 1:2]) * (1.0 / dev))
            )
            msg[base + half : base + half + 16, :] = pack([*split(mean), *split(dev), *extra])


def tiles(rows, sets, rstat, half_id, slots, places=()):
    n, cells = sum(part.shape[0] for part in rows), rows[0].shape[1]
    steps, half, count = 2, n // 2, len(sets)
    first = rstat is None
    at = jnp.stack([half_id, *slots, *places]).astype(jnp.int32)
    width = cells // steps
    piece = pl.BlockSpec((64, width), lambda k, at: (0, k))
    fixed = lambda shape: pl.BlockSpec(shape, lambda k, at: (0, 0))
    f32 = lambda *shape: jax.ShapeDtypeStruct(shape, jnp.float32)
    outs = [
        f32(half, 256 * count),
        jax.ShapeDtypeStruct(((half + 16) * count, 256), jnp.int16),
        f32(8 * count, 256),
    ]
    scratch = [
        pltpu.VMEM((256 * count, width), jnp.bfloat16),
        pltpu.VMEM((n, 256 * count), jnp.float32),
        pltpu.VMEM((256 * count, 128), jnp.float32),
        pltpu.VMEM((256 * count, 128), jnp.float32),
    ]
    if first:
        outs.append(f32(n, 128))
        scratch += [pltpu.VMEM((n, 128), jnp.float32)] * 2
    if len(rows) > 1:
        scratch.append(pltpu.VMEM((n, width), jnp.bfloat16))
    return pl.pallas_call(
        functools.partial(tile_kernel, cells, steps, count, len(rows), first),
        grid_spec=pltpu.PrefetchScalarGridSpec(
            num_scalar_prefetch=1,
            grid=(steps,),
            in_specs=[pl.BlockSpec((r.shape[0], width), lambda k, at: (0, k)) for r in rows]
            + [piece] * (4 * count)
            + ([] if first else [fixed((n, 128))]),
            out_specs=[fixed(o.shape) for o in outs],
            scratch_shapes=scratch,
        ),
        out_shape=outs,
        compiler_params=pltpu.CompilerParams(vmem_limit_bytes=32 * 1024 * 1024),
        cost_estimate=pl.CostEstimate(
            flops=2 * n * 256 * count * cells, bytes_accessed=2 * (n + 256) * cells, transcendentals=0
        ),
    )(at, *rows, *[p for s in sets for p in s], *([] if first else [rstat]))


def merged(mean, mean2, dev, dev2):
    gap = mean - mean2
    inv = lax.rsqrt(0.5 * (dev * dev + dev2 * dev2) + 0.25 * gap * gap)
    return inv, dev2 * inv, gap * inv


def received(block, i):
    f = block.astype(jnp.int32).astype(jnp.float32)
    return unsplit(f[i : i + 1, :], f[i + 1 : i + 2, :]), unsplit(f[i + 2 : i + 3, :], f[i + 3 : i + 4, :])


def row_factors(rst, block, half_id):
    mean2, dev2 = received(block, 4)
    index = lax.broadcasted_iota(jnp.int32, (8, mean2.shape[1]), 0)
    flip = jnp.where(index == 0, mean2, dev2).T
    half = flip.shape[0]
    mine = pl.multiple_of(half_id * half, half)
    own = rst[pl.ds(mine, half), :]
    return merged(own[:, 0:1], flip[:, 0:1], own[:, 1:2], flip[:, 1:2])


def joined(own, msg, cst, factors):
    half = own.shape[0]
    mean2, dev2 = received(msg[half : half + 16, :], 0)
    u, v, w = merged(cst[0:1, :], mean2, cst[1:2, :], dev2)
    ru, rv, rw = factors
    return (
        0.5 * own * (ru * u) + 0.5 * decode(msg[0:half, :]) * (rv * v) + 0.25 * (rw * w)
    )


def back_kernel(at, own, msg, cst, rst, out):
    half = own.shape[0]
    factors = row_factors(rst, msg[half : half + 16, :], at[0])
    out[...] = encode(joined(own[...], msg[...], cst[...], factors))


def final_kernel(groups, at, rst, back, *refs):
    out = refs[-1]
    slot = lax.broadcasted_iota(jnp.int32, (1, 256), 1) // 64
    half = back.shape[0]
    rows = half + 16
    factors = row_factors(rst, refs[1][half:rows, :], at[0])
    far_all = decode(back[...])
    for g, ids in enumerate(groups):
        own, msg, cst = refs[3 * g : 3 * g + 3]
        for t, k in enumerate(ids):
            value = joined(
                own[:, 256 * t : 256 * t + 256],
                msg[rows * t : rows * t + rows, :],
                cst[8 * t : 8 * t + 8, :],
                factors,
            )
            piece = far_all[:, 64 * k : 64 * k + 64]
            far = jnp.concatenate([piece] * 4, axis=1)
            value = jnp.where(slot == at[1], far, value)
            out[:, at[2 + k] * 2, :] = value[:, 0:128]
            out[:, at[2 + k] * 2 + 1, :] = value[:, 128:256]


def after(value, *others):
    return lax.optimization_barrier((value, *others))[0]


def local(counts, size_factors, gene_means, dispersions, block_order):
    row, col, h = lax.axis_index("row"), lax.axis_index("col"), lax.axis_index("cell")
    zl, y = row // NY, row % NY
    x, c = col // NC, col % NC
    a = residuals(counts, size_factors, gene_means, dispersions, block_order)
    rows = lax.all_gather(a, "col", axis=0, tiled=True)
    z1, z3 = move(a, zl=1), move(a, zl=3)
    up, down = {0: move(a, y=1)}, {0: move(a, y=-1)}
    far = move(a, y=2)
    z2 = move(after(a, z1, z3), zl=2)
    z = [a, z1, z2, z3]
    for k in (1, 3, 2):
        up[k], down[k] = move(z[k], y=1), move(z[k], y=-1)
    far_mine = jnp.concatenate([far, move(far, x=1), move(far, x=-1), move(far, x=2)], axis=0)
    far_theirs = move(far_mine, c=1)

    slots = [(y - 1) % NY, y, (y + 1) % NY, (y + 2) % NY]
    pieces = lambda k: (up[k], z[k], down[k], z[k])
    own01, msg01, cst01, rstat = tiles([rows], [pieces(0), pieces(1)], None, h, slots * 2)
    msg01 = move(msg01, h=1)
    order = [(x - d) % NX * 2 for d in (0, 1, 3, 2)]
    places = [o + c for o in order] + [o + 1 - c for o in order]
    ownf, msgf, cstf, fstat = tiles(
        [far_mine, far_theirs], [z], None, h, [jnp.int32(k) for k in range(4)], places
    )
    msgf = move(msgf, h=1)
    own3, msg3, cst3 = tiles([rows], [pieces(3)], rstat, h, slots)
    msg3 = move(msg3, h=1)
    own2, msg2, cst2 = tiles([rows], [pieces(2)], rstat, h, slots)
    msg2 = move(msg2, h=1)

    whole = pl.BlockSpec(memory_space=pltpu.VMEM)
    smem = pl.BlockSpec(memory_space=pltpu.SMEM)
    half = ownf.shape[0]
    back = pl.pallas_call(
        back_kernel,
        in_specs=[smem] + [whole] * 4,
        out_specs=whole,
        out_shape=jax.ShapeDtypeStruct((half, 256), jnp.int16),
    )(jnp.stack([h]).astype(jnp.int32), ownf, msgf, cstf, fstat)
    back = move(back, y=2)

    at = jnp.stack([h, (y + 2) % NY] + [(zl - k) % ZL for k in range(ZL)]).astype(jnp.int32)
    result = pl.pallas_call(
        functools.partial(final_kernel, ((0, 1), (3,), (2,))),
        in_specs=[smem] + [whole] * 11,
        out_specs=whole,
        out_shape=jax.ShapeDtypeStruct((half, 8, 128), jnp.float32),
    )(at, rstat, back, own01, msg01, cst01, own3, msg3, cst3, own2, msg2, cst2)
    return result.reshape(half, 1, 1024)


def solution(mesh):
    return jax.shard_map(
        local,
        mesh=mesh,
        in_specs=(P(("row", "col"), "cell"), P("cell"), P(), P(), P()),
        out_specs=P(("row", "cell"), "col", None),
        check_vma=False,
    )
```

time: 323 us -> 196 us (0.61)
  waiting for transfers between devices: 276 us -> 102 us
  starting transfers between devices: 0.08 us -> 31.1 us
  Pallas kernels: 0 us -> 30 us
  other arithmetic: 13.5 us -> 0 us
  local copies, waits for them, and re-layouts: 4.81 us -> 15.9 us
  matrix products: 9.39 us -> 0 us
    all_gather x3 -> x1, waiting for transfers between devices: 276 us -> 0.01 us  [local(): rows = lax.all_gather(a, 'col', axis=0, tiled=True)]
    ppermute x0 -> x21, waiting for transfers between devices: none -> 102 us  [move(): return lax.ppermute(value, AXES, shift(**steps))]
    ppermute x0 -> x21, starting transfers between devices: none -> 31.1 us  [move(): return lax.ppermute(value, AXES, shift(**steps))]
    pallas_call x0 -> x7, Pallas kernels: none -> 30 us  [the longest x4 20.7 us: tiles(): pl.pallas_call(functools.partial(tile_kernel, cells, steps, count, len(ro...]
    unnamed x0 -> x49, local copies, waits for them, and re-layouts: none -> 14.9 us
    reduce_sum x2 -> x0, other arithmetic: 11.1 us -> none  [row_moments(): total = jnp.sum(values, axis=1, dtype=jnp.float32)]
    dot_general x1 -> x0, matrix products: 9.39 us -> none  [column_terms(): lax.dot_general(rows_res, piece, (((1,), (1,)), ((), ())), preferred_elem...]
  transfers between devices with their start and end apart: 3 -> 22, of which waited for: 3 -> 8; matrix products, arithmetic and copies ran while one was open for 1% -> 1% of each run, Pallas kernels for 0% -> 12%
where the time goes in v2:
time: 196 us; the launch traced here: 193 us
  waiting for transfers between devices  102 us (52%)
  starting transfers between devices  31.1 us (16%)
  Pallas kernels  30 us (15%)
  local copies, waits for them, and re-layouts  15.9 us (8%)
  between operations  13.6 us (7%)
    ppermute x21, waiting for transfers between devices, move(): return lax.ppermute(value, AXES, shift(**steps))  102 us
    ppermute x21, starting transfers between devices, move(): return lax.ppermute(value, AXES, shift(**steps))  31.1 us
    pallas_call x4, Pallas kernels, tiles(): pl.pallas_call(functools.partial(tile_kernel, cells, steps, count, len(ro...  20.7 us
    unnamed x49, local copies, waits for them, and re-layouts  14.9 us
    pallas_call x1, Pallas kernels, local(): pl.pallas_call(functools.partial(final_kernel, ((0, 1), (3,), (2,))), in_...  4.34 us
  transfers between devices with their start and end apart: 22, of which 8 were waited for; matrix products, arithmetic and copies ran while one was open for 1% of the time, Pallas kernels for 12%

profile of v2, /device:TPU:26, one launch (start us, length us, event | category | flops | bytes accessed | tf_op | source)
XLA Modules:
  0.0 192.7 jit_solution(15097388624524175615)
XLA Ops:
  6.5 2.6 %shard_map.55.refs_2_.refs_4_ = bf16[64,4096]{1,0:T(8,128)(2,1)} custom-call(s32[1]{0:T(128)} %bitcast.9.place, s32[128]{0:T(128)} %order.1, s32[64,4096]{1,0:T(8,128)} %counts.1, f32[1,4096]{1,0:T(1,128)} %bitcast.24, f32[64,128]{1,0:T(8,128)} %bitcast.22, f32[64,128]{1,0:T(8,128)} %bitcast.23), custom_call_target="tpu_custom_call" | custom-call | tf_op jit(solution)/shard_map/pallas_call | solution.py:55
  10.5 14.1 %collective-permute-done.5 = bf16[64,4096]{1,0:T(8,128)(2,1)S(1)} collective-permute-done((bf16[64,4096]{1,0:T(8,128)(2,1)}, bf16[64,4096]{1,0:T(8,128)(2,1)S(1)}, u32[]{:S(2)}, u32[]{:S(2)}) %collective-permute-start.5) | collective-permute-done | bytes 524320 | tf_op jit(solution)/shard_map/ppermute | solution.py:30
  26.7 2.2 %collective-permute-start.8 = (bf16[64,4096]{1,0:T(8,128)(2,1)S(1)}, bf16[64,4096]{1,0:T(8,128)(2,1)S(1)}, u32[]{:S(2)}, u32[]{:S(2)}) collective-permute-start(bf16[64,4096]{1,0:T(8,128)(2,1)S(1)} %collective-permute-done.5), channel_id=1, source_target_pairs={{0,8},{1,9},{2,10},{3,11},{4,12},{5,13},{6,14},{7,15},{8,0},{9,1},... | collective-permute-start | bytes 1572872 | tf_op jit(solution)/shard_map/ppermute | solution.py:30
  28.9 21.7 %collective-permute-done.6 = bf16[64,4096]{1,0:T(8,128)(2,1)S(1)} collective-permute-done((bf16[64,4096]{1,0:T(8,128)(2,1)S(1)}, bf16[64,4096]{1,0:T(8,128)(2,1)S(1)}, u32[]{:S(2)}, u32[]{:S(2)}) %collective-permute-start.6) | collective-permute-done | bytes 524320 | tf_op jit(solution)/shard_map/ppermute | solution.py:30
  52.0 15.2 %collective-permute-done.8 = bf16[64,4096]{1,0:T(8,128)(2,1)S(1)} collective-permute-done((bf16[64,4096]{1,0:T(8,128)(2,1)S(1)}, bf16[64,4096]{1,0:T(8,128)(2,1)S(1)}, u32[]{:S(2)}, u32[]{:S(2)}) %collective-permute-start.8) | collective-permute-done | bytes 524320 | tf_op jit(solution)/shard_map/ppermute | solution.py:30
  68.6 3.5 %collective-permute-start.10 = (bf16[64,4096]{1,0:T(8,128)(2,1)S(1)}, bf16[64,4096]{1,0:T(8,128)(2,1)S(1)}, u32[]{:S(2)}, u32[]{:S(2)}) collective-permute-start(bf16[64,4096]{1,0:T(8,128)(2,1)S(1)} %copy-done.2), channel_id=1, source_target_pairs={{0,192},{1,193},{2,194},{3,195},{4,196},{5,197},{6,198},{7,199},{8... | collective-permute-start | bytes 1572872 | tf_op jit(solution)/shard_map/ppermute | solution.py:30
  72.7 11.8 %collective-permute-done.10.refs_5_.refs_2_.refs_4_ = bf16[64,4096]{1,0:T(8,128)(2,1)S(1)} collective-permute-done((bf16[64,4096]{1,0:T(8,128)(2,1)S(1)}, bf16[64,4096]{1,0:T(8,128)(2,1)S(1)}, u32[]{:S(2)}, u32[]{:S(2)}) %collective-permute-start.10) | collective-permute-done | bytes 524320 | tf_op jit(solution)/shard_map/ppermute | solution.py:30
  84.5 11.7 %collective-permute-done.2.refs_6_.refs_8_.refs_3_ = bf16[64,4096]{1,0:T(8,128)(2,1)S(1)} collective-permute-done((bf16[64,4096]{1,0:T(8,128)(2,1)S(1)}, bf16[64,4096]{1,0:T(8,128)(2,1)S(1)}, u32[]{:S(2)}, u32[]{:S(2)}) %collective-permute-start.2) | collective-permute-done | bytes 524320 | tf_op jit(solution)/shard_map/ppermute | solution.py:30
  97.8 2.4 %collective-permute-start.3 = (bf16[64,4096]{1,0:T(8,128)(2,1)S(1)}, bf16[64,4096]{1,0:T(8,128)(2,1)S(1)}, u32[]{:S(2)}, u32[]{:S(2)}) collective-permute-start(bf16[64,4096]{1,0:T(8,128)(2,1)S(1)} %collective-permute-done.2.refs_6_.refs_8_.refs_3_), channel_id=1, source_target_pairs={{0,16},{1,17},{2,18},{3,19},{4,20},{5,21},{6,22},{7,23},{8,24},{9,... | collective-permute-start | bytes 1572872 | tf_op jit(solution)/shard_map/ppermute | solution.py:30
  100.2 21.7 %collective-permute-done.11.refs_4_.refs_2_ = bf16[64,4096]{1,0:T(8,128)(2,1)S(1)} collective-permute-done((bf16[64,4096]{1,0:T(8,128)(2,1)S(1)}, bf16[64,4096]{1,0:T(8,128)(2,1)S(1)}, u32[]{:S(2)}, u32[]{:S(2)}) %collective-permute-start.11) | collective-permute-done | bytes 524320 | tf_op jit(solution)/shard_map/ppermute | solution.py:30
  124.7 1.7 collective-permute-start.15
  130.0 1.6 copy-done.7
  131.6 5.1 %shard_map.57 = (f32[256,256]{1,0:T(8,128)S(1)}, s16[272,256]{1,0:T(8,128)(2,1)}, f32[8,256]{1,0:T(8,128)S(1)}, f32[512,128]{1,0:T(8,128)S(1)}) custom-call(s32[13]{0:T(128)S(1)} %stack.101.at, bf16[256,4096]{1,0:T(8,128)(2,1)S(1)} %copy-done.4, bf16[256,4096]{1,0:T(8,128)(2,1)S(1)} %copy-done.7, bf16[64,4096]{1,0:T(8,128)(2,1)S(1)} %copy-done.2, ...), custom_call_target="tpu_custom_call" | custom-call | flops 1073741824 | bytes 6291456 | tf_op jit(solution)/shard_map/pallas_call | solution.py:215
  138.7 3.9 %collective-permute-start.12 = (s16[272,256]{1,0:T(8,128)(2,1)}, s16[272,256]{1,0:T(8,128)(2,1)}, u32[]{:S(2)}, u32[]{:S(2)}) collective-permute-start(s16[272,256]{1,0:T(8,128)(2,1)} %get-tuple-element.23), channel_id=1, source_target_pairs={{0,1},{1,0},{2,3},{3,2},{4,5},{5,4},{6,7},{7,6},{8,9},{9,8},{10,11... | collective-permute-start | bytes 417800 | tf_op jit(solution)/shard_map/ppermute | solution.py:30
  142.6 2.2 %copy-done = bf16[512,4096]{1,0:T(8,128)(2,1)S(1)} copy-done((bf16[512,4096]{1,0:T(8,128)(2,1)S(1)}, bf16[512,4096]{1,0:T(8,128)(2,1)}, u32[]{:S(2)}) %copy-start) | copy-done | bytes 4194328
  145.8 7.4 %shard_map.56 = (f32[256,512]{1,0:T(8,128)S(1)}, s16[544,256]{1,0:T(8,128)(2,1)}, f32[16,256]{1,0:T(8,128)S(1)}, f32[512,128]{1,0:T(8,128)S(1)}) custom-call(s32[9]{0:T(128)S(1)} %stack.92.at, bf16[512,4096]{1,0:T(8,128)(2,1)S(1)} %copy-done, bf16[64,4096]{1,0:T(8,128)(2,1)S(1)} %collective-permute-done.refs_1_, bf16[64,4096]{1,0:T(8,128)(2,1)S(1)} %copy-done.2, ...), custom_call_target="tpu_custom_call" | custom-call | flops 2147483648 | bytes 6291456 | tf_op jit(solution)/shard_map/pallas_call | solution.py:215
  153.3 2.1 %collective-permute-start.14 = (s16[544,256]{1,0:T(8,128)(2,1)}, s16[544,256]{1,0:T(8,128)(2,1)S(1)}, u32[]{:S(2)}, u32[]{:S(2)}) collective-permute-start(s16[544,256]{1,0:T(8,128)(2,1)} %get-tuple-element.27), channel_id=1, source_target_pairs={{0,1},{1,0},{2,3},{3,2},{4,5},{5,4},{6,7},{7,6},{8,9},{9,8},{10,11... | collective-permute-start | bytes 835592 | tf_op jit(solution)/shard_map/ppermute | solution.py:30
  155.4 4.1 %shard_map.60 = (f32[256,256]{1,0:T(8,128)S(1)}, s16[272,256]{1,0:T(8,128)(2,1)S(1)}, f32[8,256]{1,0:T(8,128)S(1)}) custom-call(s32[5]{0:T(128)S(1)} %stack.102.at, bf16[512,4096]{1,0:T(8,128)(2,1)S(1)} %copy-done.1, bf16[64,4096]{1,0:T(8,128)(2,1)} %collective-permute-done.18.refs_1_, bf16[64,4096]{1,0:T(8,128)(2,1)S(1)} %collective-permute-done.11.refs_4_.refs_2_, ...), custom_call_target="tpu_custom_call" | custom-call | flops 1073741824 | bytes 6291456 | tf_op jit(solution)/shard_map/pallas_call | solution.py:215
  160.2 3.9 %collective-permute-start.20 = (s16[272,256]{1,0:T(8,128)(2,1)S(1)}, s16[272,256]{1,0:T(8,128)(2,1)S(1)}, u32[]{:S(2)}, u32[]{:S(2)}) collective-permute-start(s16[272,256]{1,0:T(8,128)(2,1)S(1)} %get-tuple-element.33), channel_id=1, source_target_pairs={{0,1},{1,0},{2,3},{3,2},{4,5},{5,4},{6,7},{7,6},{8,9},{9,8},{10,11... | collective-permute-start | bytes 417800 | tf_op jit(solution)/shard_map/ppermute | solution.py:30
  164.2 4.1 %shard_map.59 = (f32[256,256]{1,0:T(8,128)S(1)}, s16[272,256]{1,0:T(8,128)(2,1)S(1)}, f32[8,256]{1,0:T(8,128)S(1)}) custom-call(s32[5]{0:T(128)S(1)} %stack.102.at, bf16[512,4096]{1,0:T(8,128)(2,1)S(1)} %copy-done.1, bf16[64,4096]{1,0:T(8,128)(2,1)} %collective-permute-done.15.refs_1_, bf16[64,4096]{1,0:T(8,128)(2,1)S(1)} %collective-permute-done.10.refs_5_.refs_2_.refs_4_, ...), custom_call_target="tpu_custom_call" | custom-call | flops 1073741824 | bytes 6291456 | tf_op jit(solution)/shard_map/pallas_call | solution.py:215
  169.6 2.0 %collective-permute-start.17 = (s16[272,256]{1,0:T(8,128)(2,1)S(1)}, s16[272,256]{1,0:T(8,128)(2,1)S(1)}, u32[]{:S(2)}, u32[]{:S(2)}) collective-permute-start(s16[272,256]{1,0:T(8,128)(2,1)S(1)} %get-tuple-element.30), channel_id=1, source_target_pairs={{0,1},{1,0},{2,3},{3,2},{4,5},{5,4},{6,7},{7,6},{8,9},{9,8},{10,11... | collective-permute-start | bytes 417800 | tf_op jit(solution)/shard_map/ppermute | solution.py:30
  171.6 2.3 %shard_map.58 = s16[256,256]{1,0:T(8,128)(2,1)} custom-call(s32[1]{0:T(128)} %bitcast.at, f32[256,256]{1,0:T(8,128)} %copy-done.13, s16[272,256]{1,0:T(8,128)(2,1)} %collective-permute-done.12.msg, f32[8,256]{1,0:T(8,128)} %copy-done.18, f32[512,128]{1,0:T(8,128)} %copy-done.14), custom_call_target="tpu_custom_call" | custom-call | tf_op jit(solution)/shard_map/pallas_call | solution.py:332
  176.0 4.6 %collective-permute-done.13.back = s16[256,256]{1,0:T(8,128)(2,1)S(1)} collective-permute-done((s16[256,256]{1,0:T(8,128)(2,1)}, s16[256,256]{1,0:T(8,128)(2,1)S(1)}, u32[]{:S(2)}, u32[]{:S(2)}) %collective-permute-start.13) | collective-permute-done | bytes 131104 | tf_op jit(solution)/shard_map/ppermute | solution.py:30
  181.5 4.3 %shard_map.61 = f32[256,8,128]{2,1,0:T(8,128)} custom-call(s32[6]{0:T(128)} %stack.88.at, f32[512,128]{1,0:T(8,128)} %copy-done.5, s16[256,256]{1,0:T(8,128)(2,1)} %copy-done.22, f32[256,512]{1,0:T(8,128)} %copy-done.10, s16[544,256]{1,0:T(8,128)(2,1)} %copy-done.19, f32[16,256]{1,0:T(8,128)} %copy-done.15, f32[256,256]{1,0:T(8,128)} %copy-done.12, ...), custom_call_target="tpu_custom_call" | custom-call | tf_op jit(solution)/shard_map/pallas_call | solution.py:341
  (82 shorter events, 22.7 us)
Async XLA Ops:
  6.5 136.1 %all-gather.2.cloned.1.call-start = ((), (), s32[]{:S(2)}) async-start(), calls=%async_computation | async-start | bytes 4718592 | tf_op jit(solution)/shard_map/all_gather | solution.py:303
  9.2 59.5 %copy-start.2 = (bf16[64,4096]{1,0:T(8,128)(2,1)S(1)}, bf16[64,4096]{1,0:T(8,128)(2,1)}, u32[]{:S(2)}) copy-start(bf16[64,4096]{1,0:T(8,128)(2,1)} %shard_map.55.refs_2_.refs_4_) | copy-start | bytes 1572868
  9.2 15.5 %collective-permute-start.5 = (bf16[64,4096]{1,0:T(8,128)(2,1)}, bf16[64,4096]{1,0:T(8,128)(2,1)S(1)}, u32[]{:S(2)}, u32[]{:S(2)}) collective-permute-start(bf16[64,4096]{1,0:T(8,128)(2,1)} %shard_map.55.refs_2_.refs_4_), channel_id=1, source_target_pairs={{0,32},{1,33},{2,34},{3,35},{4,36},{5,37},{6,38},{7,39},{8,40},{9,... | collective-permute-start | bytes 1572872 | tf_op jit(solution)/shard_map/ppermute | solution.py:30
  24.7 26.0 %collective-permute-start.6 = (bf16[64,4096]{1,0:T(8,128)(2,1)S(1)}, bf16[64,4096]{1,0:T(8,128)(2,1)S(1)}, u32[]{:S(2)}, u32[]{:S(2)}) collective-permute-start(bf16[64,4096]{1,0:T(8,128)(2,1)S(1)} %collective-permute-done.5), channel_id=1, source_target_pairs={{0,4},{1,5},{2,6},{3,7},{4,8},{5,9},{6,10},{7,11},{8,12},{9,13},{1... | collective-permute-start | bytes 1572872 | tf_op jit(solution)/shard_map/ppermute | solution.py:30
  26.1 25.8 %collective-permute-start.7 = (bf16[64,4096]{1,0:T(8,128)(2,1)S(1)}, bf16[64,4096]{1,0:T(8,128)(2,1)S(1)}, u32[]{:S(2)}, u32[]{:S(2)}) collective-permute-start(bf16[64,4096]{1,0:T(8,128)(2,1)S(1)} %collective-permute-done.5), channel_id=1, source_target_pairs={{0,12},{1,13},{2,14},{3,15},{4,0},{5,1},{6,2},{7,3},{8,4},{9,5},{1... | collective-permute-start | bytes 1572872 | tf_op jit(solution)/shard_map/ppermute | solution.py:30
  26.7 40.4 %collective-permute-start.8 = (bf16[64,4096]{1,0:T(8,128)(2,1)S(1)}, bf16[64,4096]{1,0:T(8,128)(2,1)S(1)}, u32[]{:S(2)}, u32[]{:S(2)}) collective-permute-start(bf16[64,4096]{1,0:T(8,128)(2,1)S(1)} %collective-permute-done.5), channel_id=1, source_target_pairs={{0,8},{1,9},{2,10},{3,11},{4,12},{5,13},{6,14},{7,15},{8,0},{9,1},... | collective-permute-start | bytes 1572872 | tf_op jit(solution)/shard_map/ppermute | solution.py:30
  67.2 59.2 %collective-permute-start.9 = (bf16[256,4096]{1,0:T(8,128)(2,1)S(1)}, bf16[256,4096]{1,0:T(8,128)(2,1)S(1)}, u32[]{:S(2)}, u32[]{:S(2)}) collective-permute-start(bf16[256,4096]{1,0:T(8,128)(2,1)S(1)} %constant_dynamic-update-slice_fusion.refs_0_), channel_id=1, source_target_pairs={{0,2},{1,3},{2,0},{3,1},{4,6},{5,7},{6,4},{7,5},{8,10},{9,11},{10,... | collective-permute-start | bytes 6291464 | tf_op jit(solution)/shard_map/ppermute | solution.py:30
  68.6 15.8 %collective-permute-start.10 = (bf16[64,4096]{1,0:T(8,128)(2,1)S(1)}, bf16[64,4096]{1,0:T(8,128)(2,1)S(1)}, u32[]{:S(2)}, u32[]{:S(2)}) collective-permute-start(bf16[64,4096]{1,0:T(8,128)(2,1)S(1)} %copy-done.2), channel_id=1, source_target_pairs={{0,192},{1,193},{2,194},{3,195},{4,196},{5,197},{6,198},{7,199},{8... | collective-permute-start | bytes 1572872 | tf_op jit(solution)/shard_map/ppermute | solution.py:30
  72.2 24.0 %collective-permute-start.2 = (bf16[64,4096]{1,0:T(8,128)(2,1)S(1)}, bf16[64,4096]{1,0:T(8,128)(2,1)S(1)}, u32[]{:S(2)}, u32[]{:S(2)}) collective-permute-start(bf16[64,4096]{1,0:T(8,128)(2,1)S(1)} %copy-done.2), channel_id=1, source_target_pairs={{0,64},{1,65},{2,66},{3,67},{4,68},{5,69},{6,70},{7,71},{8,72},{9,... | collective-permute-start | bytes 1572872 | tf_op jit(solution)/shard_map/ppermute | solution.py:30
  72.2 28.0 %collective-permute-start = (bf16[64,4096]{1,0:T(8,128)(2,1)S(1)}, bf16[64,4096]{1,0:T(8,128)(2,1)S(1)}, u32[]{:S(2)}, u32[]{:S(2)}) collective-permute-start(bf16[64,4096]{1,0:T(8,128)(2,1)S(1)} %copy-done.2), channel_id=1, source_target_pairs={{0,16},{1,17},{2,18},{3,19},{4,20},{5,21},{6,22},{7,23},{8,24},{9,... | collective-permute-start | bytes 1572872 | tf_op jit(solution)/shard_map/ppermute | solution.py:30
  96.2 25.7 %collective-permute-start.11 = (bf16[64,4096]{1,0:T(8,128)(2,1)S(1)}, bf16[64,4096]{1,0:T(8,128)(2,1)S(1)}, u32[]{:S(2)}, u32[]{:S(2)}) collective-permute-start(bf16[64,4096]{1,0:T(8,128)(2,1)S(1)} %copy-done.2), channel_id=1, source_target_pairs={{0,128},{1,129},{2,130},{3,131},{4,132},{5,133},{6,134},{7,135},{8... | collective-permute-start | bytes 1572872 | tf_op jit(solution)/shard_map/ppermute | solution.py:30
  96.9 25.4 %collective-permute-start.1 = (bf16[64,4096]{1,0:T(8,128)(2,1)S(1)}, bf16[64,4096]{1,0:T(8,128)(2,1)S(1)}, u32[]{:S(2)}, u32[]{:S(2)}) collective-permute-start(bf16[64,4096]{1,0:T(8,128)(2,1)S(1)} %copy-done.2), channel_id=1, source_target_pairs={{0,48},{1,49},{2,50},{3,51},{4,52},{5,53},{6,54},{7,55},{8,56},{9,... | collective-permute-start | bytes 1572872 | tf_op jit(solution)/shard_map/ppermute | solution.py:30
  97.8 26.1 %collective-permute-start.3 = (bf16[64,4096]{1,0:T(8,128)(2,1)S(1)}, bf16[64,4096]{1,0:T(8,128)(2,1)S(1)}, u32[]{:S(2)}, u32[]{:S(2)}) collective-permute-start(bf16[64,4096]{1,0:T(8,128)(2,1)S(1)} %collective-permute-done.2.refs_6_.refs_8_.refs_3_), channel_id=1, source_target_pairs={{0,16},{1,17},{2,18},{3,19},{4,20},{5,21},{6,22},{7,23},{8,24},{9,... | collective-permute-start | bytes 1572872 | tf_op jit(solution)/shard_map/ppermute | solution.py:30
  100.2 38.5 %collective-permute-start.4 = (bf16[64,4096]{1,0:T(8,128)(2,1)S(1)}, bf16[64,4096]{1,0:T(8,128)(2,1)}, u32[]{:S(2)}, u32[]{:S(2)}) collective-permute-start(bf16[64,4096]{1,0:T(8,128)(2,1)S(1)} %collective-permute-done.2.refs_6_.refs_8_.refs_3_), channel_id=1, source_target_pairs={{0,48},{1,49},{2,50},{3,51},{4,52},{5,53},{6,54},{7,55},{8,56},{9,... | collective-permute-start | bytes 1572872 | tf_op jit(solution)/shard_map/ppermute | solution.py:30
  121.9 31.4 %collective-permute-start.18 = (bf16[64,4096]{1,0:T(8,128)(2,1)S(1)}, bf16[64,4096]{1,0:T(8,128)(2,1)}, u32[]{:S(2)}, u32[]{:S(2)}) collective-permute-start(bf16[64,4096]{1,0:T(8,128)(2,1)S(1)} %collective-permute-done.11.refs_4_.refs_2_), channel_id=1, source_target_pairs={{0,16},{1,17},{2,18},{3,19},{4,20},{5,21},{6,22},{7,23},{8,24},{9,... | collective-permute-start | bytes 1572872 | tf_op jit(solution)/shard_map/ppermute | solution.py:30
  122.4 33.0 %collective-permute-start.19 = (bf16[64,4096]{1,0:T(8,128)(2,1)S(1)}, bf16[64,4096]{1,0:T(8,128)(2,1)}, u32[]{:S(2)}, u32[]{:S(2)}) collective-permute-start(bf16[64,4096]{1,0:T(8,128)(2,1)S(1)} %collective-permute-done.11.refs_4_.refs_2_), channel_id=1, source_target_pairs={{0,48},{1,49},{2,50},{3,51},{4,52},{5,53},{6,54},{7,55},{8,56},{9,... | collective-permute-start | bytes 1572872 | tf_op jit(solution)/shard_map/ppermute | solution.py:30
  124.7 39.4 %collective-permute-start.15 = (bf16[64,4096]{1,0:T(8,128)(2,1)S(1)}, bf16[64,4096]{1,0:T(8,128)(2,1)}, u32[]{:S(2)}, u32[]{:S(2)}) collective-permute-start(bf16[64,4096]{1,0:T(8,128)(2,1)S(1)} %collective-permute-done.10.refs_5_.refs_2_.refs_4_), channel_id=1, source_target_pairs={{0,16},{1,17},{2,18},{3,19},{4,20},{5,21},{6,22},{7,23},{8,24},{9,... | collective-permute-start | bytes 1572872 | tf_op jit(solution)/shard_map/ppermute | solution.py:30
  127.8 36.4 %collective-permute-start.16 = (bf16[64,4096]{1,0:T(8,128)(2,1)S(1)}, bf16[64,4096]{1,0:T(8,128)(2,1)}, u32[]{:S(2)}, u32[]{:S(2)}) collective-permute-start(bf16[64,4096]{1,0:T(8,128)(2,1)S(1)} %collective-permute-done.10.refs_5_.refs_2_.refs_4_), channel_id=1, source_target_pairs={{0,48},{1,49},{2,50},{3,51},{4,52},{5,53},{6,54},{7,55},{8,56},{9,... | collective-permute-start | bytes 1572872 | tf_op jit(solution)/shard_map/ppermute | solution.py:30
  138.7 32.9 %collective-permute-start.12 = (s16[272,256]{1,0:T(8,128)(2,1)}, s16[272,256]{1,0:T(8,128)(2,1)}, u32[]{:S(2)}, u32[]{:S(2)}) collective-permute-start(s16[272,256]{1,0:T(8,128)(2,1)} %get-tuple-element.23), channel_id=1, source_target_pairs={{0,1},{1,0},{2,3},{3,2},{4,5},{5,4},{6,7},{7,6},{8,9},{9,8},{10,11... | collective-permute-start | bytes 417800 | tf_op jit(solution)/shard_map/ppermute | solution.py:30
  153.3 10.9 %copy-start.5 = (f32[512,128]{1,0:T(8,128)}, f32[512,128]{1,0:T(8,128)S(1)}, u32[]{:S(2)}) copy-start(f32[512,128]{1,0:T(8,128)S(1)} %get-tuple-element.20.refs_5_.rst) | copy-start | bytes 786436
  153.3 27.3 %collective-permute-start.14 = (s16[544,256]{1,0:T(8,128)(2,1)}, s16[544,256]{1,0:T(8,128)(2,1)S(1)}, u32[]{:S(2)}, u32[]{:S(2)}) collective-permute-start(s16[544,256]{1,0:T(8,128)(2,1)} %get-tuple-element.27), channel_id=1, source_target_pairs={{0,1},{1,0},{2,3},{3,2},{4,5},{5,4},{6,7},{7,6},{8,9},{9,8},{10,11... | collective-permute-start | bytes 835592 | tf_op jit(solution)/shard_map/ppermute | solution.py:30
  160.2 20.4 %collective-permute-start.20 = (s16[272,256]{1,0:T(8,128)(2,1)S(1)}, s16[272,256]{1,0:T(8,128)(2,1)S(1)}, u32[]{:S(2)}, u32[]{:S(2)}) collective-permute-start(s16[272,256]{1,0:T(8,128)(2,1)S(1)} %get-tuple-element.33), channel_id=1, source_target_pairs={{0,1},{1,0},{2,3},{3,2},{4,5},{5,4},{6,7},{7,6},{8,9},{9,8},{10,11... | collective-permute-start | bytes 417800 | tf_op jit(solution)/shard_map/ppermute | solution.py:30
  169.6 11.0 %collective-permute-start.17 = (s16[272,256]{1,0:T(8,128)(2,1)S(1)}, s16[272,256]{1,0:T(8,128)(2,1)S(1)}, u32[]{:S(2)}, u32[]{:S(2)}) collective-permute-start(s16[272,256]{1,0:T(8,128)(2,1)S(1)} %get-tuple-element.30), channel_id=1, source_target_pairs={{0,1},{1,0},{2,3},{3,2},{4,5},{5,4},{6,7},{7,6},{8,9},{9,8},{10,11... | collective-permute-start | bytes 417800 | tf_op jit(solution)/shard_map/ppermute | solution.py:30
  173.9 6.7 %collective-permute-start.13 = (s16[256,256]{1,0:T(8,128)(2,1)}, s16[256,256]{1,0:T(8,128)(2,1)S(1)}, u32[]{:S(2)}, u32[]{:S(2)}) collective-permute-start(s16[256,256]{1,0:T(8,128)(2,1)} %shard_map.58), channel_id=1, source_target_pairs={{0,32},{1,33},{2,34},{3,35},{4,36},{5,37},{6,38},{7,39},{8,40},{9,... | collective-permute-start | bytes 393224 | tf_op jit(solution)/shard_map/ppermute | solution.py:30
  (21 other events, 47.0 us)
Sparse Core Ops, SparseCore 0:
  9.3 51.7 all-gather.1

commit v3 on v2

--- a/solution.py
+++ b/solution.py
@@ -114,121 +114,117 @@
     return jnp.sqrt(square - mean * mean + EPS)
 
 
-def tile_kernel(cells, steps, count, parts, first, at, *refs):
+def tile_kernel(cells, count, parts, first, at, *refs):
     refs = list(refs)
     rows = [refs.pop(0) for _ in range(parts)]
     pieces = [refs.pop(0) for _ in range(4 * count)]
     given = None if first else refs.pop(0)
     own, msg, cst = refs.pop(0), refs.pop(0), refs.pop(0)
     rst = refs.pop(0) if first else given
-    cbuf, acc, s_acc, q_acc = refs[:4]
-    k = pl.program_id(0)
+    cbuf, acc = refs[:2]
     half = own.shape[0]
-
-    @pl.when(k == 0)
-    def _():
-        acc[...] = jnp.zeros_like(acc)
-        s_acc[...] = jnp.zeros_like(s_acc)
-        q_acc[...] = jnp.zeros_like(q_acc)
-        if first:
-            refs[4][...] = jnp.zeros_like(refs[4])
-            refs[5][...] = jnp.zeros_like(refs[5])
 
     for i, p in enumerate(pieces):
         place = 256 * (i // 4) + at[1 + i] * 64
         cbuf[pl.ds(pl.multiple_of(place, 64), 64), :] = p[...]
     if parts == 1:
-        r = rows[0][...]
+        rbuf = rows[0]
     else:
-        rbuf = refs[6]
+        rbuf = refs[2]
         for j, part in enumerate(rows):
             for i in range(part.shape[0] // 64):
                 place = at[1 + 4 * count + 4 * j + i] * 64
                 rbuf[pl.ds(pl.multiple_of(place, 64), 64), :] = part[64 * i : 64 * i + 64, :]
-        r = rbuf[...]
-    c = cbuf[...]
-    acc[...] += lax.dot_general(r, c, NT, preferred_element_type=jnp.float32)
-    wide = c.astype(jnp.float32)
-    s_acc[...] += fold(wide)
-    q_acc[...] += fold(wide * wide)
+
+    total = sums = squares = row_sums = row_squares = 0.0
+    for k in range(0, cells, 1024):
+        r, c = rbuf[:, k : k + 1024], cbuf[:, k : k + 1024]
+        total += lax.dot_general(r, c, NT, preferred_element_type=jnp.float32)
+        wide = c.astype(jnp.float32)
+        sums += fold(wide)
+        squares += fold(wide * wide)
+        if first:
+            wide = r.astype(jnp.float32)
+            row_sums += fold(wide)
+            row_squares += fold(wide * wide)
+    acc[...] = total
+
+    scale = 1.0 / cells
+    mine = pl.multiple_of(at[0] * half, half)
+    other = pl.multiple_of((1 - at[0]) * half, half)
+    extra = []
     if first:
-        wide = r.astype(jnp.float32)
-        refs[4][...] += fold(wide)
-        refs[5][...] += fold(wide * wide)
-
-    @pl.when(k == steps - 1)
-    def _():
-        scale = 1.0 / cells
-        mine = pl.multiple_of(at[0] * half, half)
-        other = pl.multiple_of((1 - at[0]) * half, half)
-        extra = []
-        if first:
-            rs, rq = refs[4], refs[5]
-            mean = jnp.sum(rs[...], axis=1, keepdims=True) * scale
-            dev = deviation(jnp.sum(rq[...], axis=1, keepdims=True) * scale, mean)
-            lane = lax.broadcasted_iota(jnp.int32, rst.shape, 1)
-            rst[...] = jnp.where(lane == 0, mean, dev)
-            mean = lane_sums(rs[pl.ds(other, half), :]) * scale
-            dev = deviation(lane_sums(rq[pl.ds(other, half), :]) * scale, mean)
-            extra = [*split(mean), *split(dev)]
-        for t in range(count):
-            span = slice(256 * t, 256 * t + 256)
-            mean = lane_sums(s_acc[span, :]) * scale
-            dev = deviation(lane_sums(q_acc[span, :]) * scale, mean)
-            row = lax.broadcasted_iota(jnp.int32, (8, 256), 0)
-            cst[8 * t : 8 * t + 8, :] = jnp.where(row == 0, mean, dev)
-            cov = acc[pl.ds(mine, half), span] * scale - rst[pl.ds(mine, half), 0:1] * mean
-            own[:, span] = cov
-            cov = acc[pl.ds(other, half), span] * scale - rst[pl.ds(other, half), 0:1] * mean
-            base = (half + 16) * t
-            msg[base : base + half, :] = encode(
-                cov * ((1.0 / rst[pl.ds(other, half), 1:2]) * (1.0 / dev))
-            )
-            msg[base + half : base + half + 16, :] = pack([*split(mean), *split(dev), *extra])
+        rs, rq = refs[-2:]
+        rs[...], rq[...] = row_sums, row_squares
+        mean = jnp.sum(row_sums, axis=1, keepdims=True) * scale
+        dev = deviation(jnp.sum(row_squares, axis=1, keepdims=True) * scale, mean)
+        lane = lax.broadcasted_iota(jnp.int32, rst.shape, 1)
+        rst[...] = jnp.where(lane == 0, mean, dev)
+        mean = lane_sums(rs[pl.ds(other, half), :]) * scale
+        dev = deviation(lane_sums(rq[pl.ds(other, half), :]) * scale, mean)
+        extra = [*split(mean), *split(dev)]
+    means, devs = lane_sums(sums) * scale, lane_sums(squares) * scale
+    devs = deviation(devs, means)
+    for t in range(count):
+        span = slice(256 * t, 256 * t + 256)
+        mean, dev = means[:, span], devs[:, span]
+        row = lax.broadcasted_iota(jnp.int32, (8, 256), 0)
+        cst[8 * t : 8 * t + 8, :] = jnp.where(row == 0, mean, dev)
+        cov = acc[pl.ds(other, half), span] * scale - rst[pl.ds(other, half), 0:1] * mean
+        base = (half + 16) * t
+        msg[base : base + half, :] = encode(
+            cov * ((1.0 / rst[pl.ds(other, half), 1:2]) * (1.0 / dev))
+        )
+        msg[base + half : base + half + 16, :] = pack([*split(mean), *split(dev), *extra])
+        own[:, span] = acc[pl.ds(mine, half), span] * scale - rst[pl.ds(mine, half), 0:1] * mean
+
+
+VMEM_LIMIT = 32 * 1024 * 1024
+VMEM = pl.BlockSpec(memory_space=pltpu.VMEM)
+SMEM = pl.BlockSpec(memory_space=pltpu.SMEM)
+
+
+def call(kernel, outs, scratch, flops, at, *args):
+    return pl.pallas_call(
+        kernel,
+        in_specs=[SMEM] + [VMEM] * len(args),
+        out_specs=[VMEM] * len(outs),
+        out_shape=[jax.ShapeDtypeStruct(*o) for o in outs],
+        scratch_shapes=scratch,
+        compiler_params=pltpu.CompilerParams(vmem_limit_bytes=VMEM_LIMIT),
+        cost_estimate=pl.CostEstimate(flops=flops, bytes_accessed=1 << 20, transcendentals=0),
+    )(jnp.stack(at).astype(jnp.int32), *args)
 
 
 def tiles(rows, sets, rstat, half_id, slots, places=()):
     n, cells = sum(part.shape[0] for part in rows), rows[0].shape[1]
-    steps, half, count = 2, n // 2, len(sets)
-    first = rstat is None
-    at = jnp.stack([half_id, *slots, *places]).astype(jnp.int32)
-    width = cells // steps
-    piece = pl.BlockSpec((64, width), lambda k, at: (0, k))
-    fixed = lambda shape: pl.BlockSpec(shape, lambda k, at: (0, 0))
-    f32 = lambda *shape: jax.ShapeDtypeStruct(shape, jnp.float32)
+    half, count, first = n // 2, len(sets), rstat is None
     outs = [
-        f32(half, 256 * count),
-        jax.ShapeDtypeStruct(((half + 16) * count, 256), jnp.int16),
-        f32(8 * count, 256),
+        ((half, 256 * count), jnp.float32),
+        (((half + 16) * count, 256), jnp.int16),
+        ((8 * count, 256), jnp.float32),
     ]
     scratch = [
-        pltpu.VMEM((256 * count, width), jnp.bfloat16),
+        pltpu.VMEM((256 * count, cells), jnp.bfloat16),
         pltpu.VMEM((n, 256 * count), jnp.float32),
-        pltpu.VMEM((256 * count, 128), jnp.float32),
-        pltpu.VMEM((256 * count, 128), jnp.float32),
     ]
+    if len(rows) > 1:
+        scratch.append(pltpu.VMEM((n, cells), jnp.bfloat16))
     if first:
-        outs.append(f32(n, 128))
+        outs.append(((n, 128), jnp.float32))
         scratch += [pltpu.VMEM((n, 128), jnp.float32)] * 2
-    if len(rows) > 1:
-        scratch.append(pltpu.VMEM((n, width), jnp.bfloat16))
-    return pl.pallas_call(
-        functools.partial(tile_kernel, cells, steps, count, len(rows), first),
-        grid_spec=pltpu.PrefetchScalarGridSpec(
-            num_scalar_prefetch=1,
-            grid=(steps,),
-            in_specs=[pl.BlockSpec((r.shape[0], width), lambda k, at: (0, k)) for r in rows]
-            + [piece] * (4 * count)
-            + ([] if first else [fixed((n, 128))]),
-            out_specs=[fixed(o.shape) for o in outs],
-            scratch_shapes=scratch,
-        ),
-        out_shape=outs,
-        compiler_params=pltpu.CompilerParams(vmem_limit_bytes=32 * 1024 * 1024),
-        cost_estimate=pl.CostEstimate(
-            flops=2 * n * 256 * count * cells, bytes_accessed=2 * (n + 256) * cells, transcendentals=0
-        ),
-    )(at, *rows, *[p for s in sets for p in s], *([] if first else [rstat]))
+    kernel = functools.partial(tile_kernel, cells, count, len(rows), first)
+    stat = [] if first else [rstat]
+    return call(
+        kernel,
+        outs,
+        scratch,
+        2 * n * 256 * count * cells,
+        [half_id, *slots, *places],
+        *rows,
+        *[p for s in sets for p in s],
+        *stat,
+    )
 
 
 def merged(mean, mean2, dev, dev2):
@@ -291,31 +287,37 @@
             out[:, at[2 + k] * 2 + 1, :] = value[:, 128:256]
 
 
-def after(value, *others):
-    return lax.optimization_barrier((value, *others))[0]
-
-
 def local(counts, size_factors, gene_means, dispersions, block_order):
     row, col, h = lax.axis_index("row"), lax.axis_index("col"), lax.axis_index("cell")
     zl, y = row // NY, row % NY
     x, c = col // NC, col % NC
     a = residuals(counts, size_factors, gene_means, dispersions, block_order)
     rows = lax.all_gather(a, "col", axis=0, tiled=True)
-    z1, z3 = move(a, zl=1), move(a, zl=3)
-    up, down = {0: move(a, y=1)}, {0: move(a, y=-1)}
-    far = move(a, y=2)
-    z2 = move(after(a, z1, z3), zl=2)
+    hold = lax.optimization_barrier
+    up, down = {}, {}
+    z1, z3, far = move(a, zl=1), move(a, zl=3), move(a, y=2)
+    up[0], down[0] = move(a, y=1), move(a, y=-1)
+    a, z1, z3, far, up[0], down[0] = hold((a, z1, z3, far, up[0], down[0]))
+
+    z2 = move(a, zl=2)
+    up[1], down[1] = move(z1, y=1), move(z1, y=-1)
+    f1, f3 = move(far, x=1), move(far, x=-1)
+    z3, far, up[1], down[1], f1, f3 = hold((z3, far, up[1], down[1], f1, f3))
+
+    up[3], down[3] = move(z3, y=1), move(z3, y=-1)
+    f2 = move(far, x=2)
+    z2, up[3], down[3], f2 = hold((z2, up[3], down[3], f2))
+
+    up[2], down[2] = move(z2, y=1), move(z2, y=-1)
+    far_mine = jnp.concatenate([far, f1, f2, f3], axis=0)
+    far_theirs = move(far_mine, c=1)
     z = [a, z1, z2, z3]
-    for k in (1, 3, 2):
-        up[k], down[k] = move(z[k], y=1), move(z[k], y=-1)
-    far_mine = jnp.concatenate([far, move(far, x=1), move(far, x=-1), move(far, x=2)], axis=0)
-    far_theirs = move(far_mine, c=1)
 
     slots = [(y - 1) % NY, y, (y + 1) % NY, (y + 2) % NY]
     pieces = lambda k: (up[k], z[k], down[k], z[k])
     own01, msg01, cst01, rstat = tiles([rows], [pieces(0), pieces(1)], None, h, slots * 2)
     msg01 = move(msg01, h=1)
-    order = [(x - d) % NX * 2 for d in (0, 1, 3, 2)]
+    order = [(x - d) % NX * 2 for d in range(4)]
     places = [o + c for o in order] + [o + 1 - c for o in order]
     ownf, msgf, cstf, fstat = tiles(
         [far_mine, far_theirs], [z], None, h, [jnp.int32(k) for k in range(4)], places
@@ -326,24 +328,20 @@
     own2, msg2, cst2 = tiles([rows], [pieces(2)], rstat, h, slots)
     msg2 = move(msg2, h=1)
 
-    whole = pl.BlockSpec(memory_space=pltpu.VMEM)
-    smem = pl.BlockSpec(memory_space=pltpu.SMEM)
     half = ownf.shape[0]
-    back = pl.pallas_call(
-        back_kernel,
-        in_specs=[smem] + [whole] * 4,
-        out_specs=whole,
-        out_shape=jax.ShapeDtypeStruct((half, 256), jnp.int16),
-    )(jnp.stack([h]).astype(jnp.int32), ownf, msgf, cstf, fstat)
+    (back,) = call(
+        back_kernel, [((half, 256), jnp.int16)], [], 1 << 22, [h], ownf, msgf, cstf, fstat
+    )
     back = move(back, y=2)
 
-    at = jnp.stack([h, (y + 2) % NY] + [(zl - k) % ZL for k in range(ZL)]).astype(jnp.int32)
-    result = pl.pallas_call(
+    (result,) = call(
         functools.partial(final_kernel, ((0, 1), (3,), (2,))),
-        in_specs=[smem] + [whole] * 11,
-        out_specs=whole,
-        out_shape=jax.ShapeDtypeStruct((half, 8, 128), jnp.float32),
-    )(at, rstat, back, own01, msg01, cst01, own3, msg3, cst3, own2, msg2, cst2)
+        [((half, 8, 128), jnp.float32)],
+        [],
+        1 << 24,
+        [h, (y + 2) % NY] + [(zl - k) % ZL for k in range(ZL)],
+        *(rstat, back, own01, msg01, cst01, own3, msg3, cst3, own2, msg2, cst2),
+    )
     return result.reshape(half, 1, 1024)
 
 

time: 196 us -> 147 us (0.75); the launches traced: 193 us -> 146 us
  waiting for transfers between devices: 102 us -> 58.8 us
  Pallas kernels: 30 us -> 24.8 us
  starting transfers between devices: 31.1 us -> 35.5 us
  local copies, waits for them, and re-layouts: 15.9 us -> 13.6 us
    ppermute x21, waiting for transfers between devices: 102 us -> 58.8 us  [move(): return lax.ppermute(value, AXES, shift(**steps))]
    pallas_call x6, Pallas kernels: 27.4 us -> 22.2 us  [call(): pl.pallas_call(kernel, in_specs=[SMEM] + [VMEM] * len(args), out_specs=[V...]
    ppermute x21, starting transfers between devices: 31.1 us -> 35.5 us  [move(): return lax.ppermute(value, AXES, shift(**steps))]
    unnamed x49 -> x45, local copies, waits for them, and re-layouts: 14.9 us -> 11.4 us
  transfers between devices with their start and end apart: 22 -> 22, of which waited for: 8 -> 8; matrix products, arithmetic and copies ran while one was open for 1% -> 3% of each run, Pallas kernels for 12% -> 13%
where the time goes in v3:
time: 147 us; the launch traced here: 146 us
  waiting for transfers between devices  58.8 us (40%)
  starting transfers between devices  35.5 us (24%)
  Pallas kernels  24.8 us (17%)
  local copies, waits for them, and re-layouts  13.6 us (9%)
  between operations  13.6 us (9%)
    ppermute x21, waiting for transfers between devices, move(): return lax.ppermute(value, AXES, shift(**steps))  58.8 us
    ppermute x21, starting transfers between devices, move(): return lax.ppermute(value, AXES, shift(**steps))  35.5 us
    pallas_call x6, Pallas kernels, call(): pl.pallas_call(kernel, in_specs=[SMEM] + [VMEM] * len(args), out_specs=[V...  22.2 us
    unnamed x45, local copies, waits for them, and re-layouts  11.4 us
  transfers between devices with their start and end apart: 22, of which 8 were waited for; matrix products, arithmetic and copies ran while one was open for 3% of the time, Pallas kernels for 13%

profile of v3, /device:TPU:26, one launch (start us, length us, event | category | flops | bytes accessed | tf_op | source)
XLA Modules:
  0.0 146.3 jit_solution(15408227131650019952)
XLA Ops:
  6.5 2.6 %shard_map.55.refs_2_.refs_4_ = bf16[64,4096]{1,0:T(8,128)(2,1)} custom-call(s32[1]{0:T(128)} %bitcast.9.place, s32[128]{0:T(128)} %order.1, s32[64,4096]{1,0:T(8,128)} %counts.1, f32[1,4096]{1,0:T(1,128)} %bitcast.24, f32[64,128]{1,0:T(8,128)} %bitcast.22, f32[64,128]{1,0:T(8,128)} %bitcast.23), custom_call_target="tpu_custom_call" | custom-call | tf_op jit(solution)/shard_map/pallas_call | solution.py:55
  10.0 2.5 %collective-permute-start.3 = (bf16[64,4096]{1,0:T(8,128)(2,1)}, bf16[64,4096]{1,0:T(8,128)(2,1)S(1)}, u32[]{:S(2)}, u32[]{:S(2)}) collective-permute-start(bf16[64,4096]{1,0:T(8,128)(2,1)} %shard_map.55.refs_2_.refs_4_), channel_id=1, source_target_pairs={{0,16},{1,17},{2,18},{3,19},{4,20},{5,21},{6,22},{7,23},{8,24},{9,... | collective-permute-start | bytes 1572872 | tf_op jit(solution)/shard_map/ppermute | solution.py:30
  12.5 4.6 %collective-permute-start.1 = (bf16[64,4096]{1,0:T(8,128)(2,1)}, bf16[64,4096]{1,0:T(8,128)(2,1)S(1)}, u32[]{:S(2)}, u32[]{:S(2)}) collective-permute-start(bf16[64,4096]{1,0:T(8,128)(2,1)} %shard_map.55.refs_2_.refs_4_), channel_id=1, source_target_pairs={{0,192},{1,193},{2,194},{3,195},{4,196},{5,197},{6,198},{7,199},{8... | collective-permute-start | bytes 1572872 | tf_op jit(solution)/shard_map/ppermute | solution.py:30
  17.2 18.4 %collective-permute-done.4.refs_3_ = bf16[64,4096]{1,0:T(8,128)(2,1)S(1)} collective-permute-done((bf16[64,4096]{1,0:T(8,128)(2,1)}, bf16[64,4096]{1,0:T(8,128)(2,1)S(1)}, u32[]{:S(2)}, u32[]{:S(2)}) %collective-permute-start.4) | collective-permute-done | bytes 524320 | tf_op jit(solution)/shard_map/ppermute | solution.py:30
  35.6 4.4 %collective-permute-done.refs_6_.refs_8_.refs_3_ = bf16[64,4096]{1,0:T(8,128)(2,1)S(1)} collective-permute-done((bf16[64,4096]{1,0:T(8,128)(2,1)}, bf16[64,4096]{1,0:T(8,128)(2,1)S(1)}, u32[]{:S(2)}, u32[]{:S(2)}) %collective-permute-start) | collective-permute-done | bytes 524320 | tf_op jit(solution)/shard_map/ppermute | solution.py:30
  40.5 1.5 %collective-permute-start.7 = (bf16[64,4096]{1,0:T(8,128)(2,1)S(1)}, bf16[64,4096]{1,0:T(8,128)(2,1)S(1)}, u32[]{:S(2)}, u32[]{:S(2)}) collective-permute-start(bf16[64,4096]{1,0:T(8,128)(2,1)S(1)} %collective-permute-done.2), channel_id=1, source_target_pairs={{0,4},{1,5},{2,6},{3,7},{4,8},{5,9},{6,10},{7,11},{8,12},{9,13},{1... | collective-permute-start | bytes 1572872 | tf_op jit(solution)/shard_map/ppermute | solution.py:30
  42.9 2.4 %collective-permute-start.5 = (bf16[64,4096]{1,0:T(8,128)(2,1)S(1)}, bf16[64,4096]{1,0:T(8,128)(2,1)S(1)}, u32[]{:S(2)}, u32[]{:S(2)}) collective-permute-start(bf16[64,4096]{1,0:T(8,128)(2,1)S(1)} %collective-permute-done.refs_6_.refs_8_.refs_3_), channel_id=1, source_target_pairs={{0,16},{1,17},{2,18},{3,19},{4,20},{5,21},{6,22},{7,23},{8,24},{9,... | collective-permute-start | bytes 1572872 | tf_op jit(solution)/shard_map/ppermute | solution.py:30
  45.6 9.7 %collective-permute-done.8 = bf16[64,4096]{1,0:T(8,128)(2,1)S(1)} collective-permute-done((bf16[64,4096]{1,0:T(8,128)(2,1)S(1)}, bf16[64,4096]{1,0:T(8,128)(2,1)S(1)}, u32[]{:S(2)}, u32[]{:S(2)}) %collective-permute-start.8) | collective-permute-done | bytes 524320 | tf_op jit(solution)/shard_map/ppermute | solution.py:30
  57.8 2.4 %collective-permute-start.10 = (bf16[64,4096]{1,0:T(8,128)(2,1)S(1)}, bf16[64,4096]{1,0:T(8,128)(2,1)S(1)}, u32[]{:S(2)}, u32[]{:S(2)}) collective-permute-start(bf16[64,4096]{1,0:T(8,128)(2,1)S(1)} %collective-permute-done.1.refs_5_.refs_2_.refs_4_), channel_id=1, source_target_pairs={{0,16},{1,17},{2,18},{3,19},{4,20},{5,21},{6,22},{7,23},{8,24},{9,... | collective-permute-start | bytes 1572872 | tf_op jit(solution)/shard_map/ppermute | solution.py:30
  60.2 3.1 %collective-permute-start.12 = (bf16[64,4096]{1,0:T(8,128)(2,1)S(1)}, bf16[64,4096]{1,0:T(8,128)(2,1)S(1)}, u32[]{:S(2)}, u32[]{:S(2)}) collective-permute-start(bf16[64,4096]{1,0:T(8,128)(2,1)S(1)} %collective-permute-done.2), channel_id=1, source_target_pairs={{0,8},{1,9},{2,10},{3,11},{4,12},{5,13},{6,14},{7,15},{8,0},{9,1},... | collective-permute-start | bytes 1572872 | tf_op jit(solution)/shard_map/ppermute | solution.py:30
  64.9 3.9 %collective-permute-done.9.refs_4_.refs_2_ = bf16[64,4096]{1,0:T(8,128)(2,1)S(1)} collective-permute-done((bf16[64,4096]{1,0:T(8,128)(2,1)}, bf16[64,4096]{1,0:T(8,128)(2,1)S(1)}, u32[]{:S(2)}, u32[]{:S(2)}) %collective-permute-start.9) | collective-permute-done | bytes 524320 | tf_op jit(solution)/shard_map/ppermute | solution.py:30
  68.9 5.4 %collective-permute-done.12 = bf16[64,4096]{1,0:T(8,128)(2,1)S(1)} collective-permute-done((bf16[64,4096]{1,0:T(8,128)(2,1)S(1)}, bf16[64,4096]{1,0:T(8,128)(2,1)S(1)}, u32[]{:S(2)}, u32[]{:S(2)}) %collective-permute-start.12) | collective-permute-done | bytes 524320 | tf_op jit(solution)/shard_map/ppermute | solution.py:30
  76.1 3.2 %collective-permute-start.18 = (bf16[64,4096]{1,0:T(8,128)(2,1)S(1)}, bf16[64,4096]{1,0:T(8,128)(2,1)}, u32[]{:S(2)}, u32[]{:S(2)}) collective-permute-start(bf16[64,4096]{1,0:T(8,128)(2,1)S(1)} %collective-permute-done.9.refs_4_.refs_2_), channel_id=1, source_target_pairs={{0,16},{1,17},{2,18},{3,19},{4,20},{5,21},{6,22},{7,23},{8,24},{9,... | collective-permute-start | bytes 1572872 | tf_op jit(solution)/shard_map/ppermute | solution.py:30
  80.7 6.3 %shard_map.57 = (f32[256,256]{1,0:T(8,128)S(1)}, s16[272,256]{1,0:T(8,128)(2,1)}, f32[8,256]{1,0:T(8,128)S(1)}, f32[512,128]{1,0:T(8,128)S(1)}) custom-call(s32[13]{0:T(128)S(1)} %stack.101.at, bf16[256,4096]{1,0:T(8,128)(2,1)} %constant_dynamic-update-slice_fusion.refs_0_, bf16[256,4096]{1,0:T(8,128)(2,1)} %collective-permute-done.13.refs_1_, ...), custom_call_target="tpu_custom_call" | custom-call | flops 1073741824 | bytes 1048576 | tf_op jit(solution)/shard_map/pallas_call | solution.py:188
  88.4 5.7 %collective-permute-start.14 = (s16[272,256]{1,0:T(8,128)(2,1)}, s16[272,256]{1,0:T(8,128)(2,1)S(1)}, u32[]{:S(2)}, u32[]{:S(2)}) collective-permute-start(s16[272,256]{1,0:T(8,128)(2,1)} %get-tuple-element.51), channel_id=1, source_target_pairs={{0,1},{1,0},{2,3},{3,2},{4,5},{5,4},{6,7},{7,6},{8,9},{9,8},{10,11... | collective-permute-start | bytes 417800 | tf_op jit(solution)/shard_map/ppermute | solution.py:30
  94.0 2.2 %copy-done = bf16[512,4096]{1,0:T(8,128)(2,1)S(1)} copy-done((bf16[512,4096]{1,0:T(8,128)(2,1)S(1)}, bf16[512,4096]{1,0:T(8,128)(2,1)}, u32[]{:S(2)}) %copy-start) | copy-done | bytes 4194328
  98.9 5.9 %shard_map.56 = (f32[256,512]{1,0:T(8,128)S(1)}, s16[544,256]{1,0:T(8,128)(2,1)}, f32[16,256]{1,0:T(8,128)S(1)}, f32[512,128]{1,0:T(8,128)S(1)}) custom-call(s32[9]{0:T(128)S(1)} %copy-done.20, bf16[512,4096]{1,0:T(8,128)(2,1)S(1)} %copy-done, bf16[64,4096]{1,0:T(8,128)(2,1)S(1)} %collective-permute-done.3.refs_1_, bf16[64,4096]{1,0:T(8,128)(2,1)S(1)} %copy-done.2, ...), custom_call_target="tpu_custom_call" | custom-call | flops 2147483648 | bytes 1048576 | tf_op jit(solution)/shard_map/pallas_call | solution.py:188
  105.9 2.7 %shard_map.59 = (f32[256,256]{1,0:T(8,128)S(1)}, s16[272,256]{1,0:T(8,128)(2,1)S(1)}, f32[8,256]{1,0:T(8,128)S(1)}) custom-call(s32[5]{0:T(128)S(1)} %copy-done.19, bf16[512,4096]{1,0:T(8,128)(2,1)S(1)} %copy-done.1, bf16[64,4096]{1,0:T(8,128)(2,1)S(1)} %copy-done.12, bf16[64,4096]{1,0:T(8,128)(2,1)S(1)} %collective-permute-done.1.refs_5_.refs_2_.refs_4_, ...), custom_call_target="tpu_custom_call" | custom-call | flops 1073741824 | bytes 1048576 | tf_op jit(solution)/shard_map/pallas_call | solution.py:188
  108.7 6.0 %collective-permute-start.17 = (s16[272,256]{1,0:T(8,128)(2,1)S(1)}, s16[272,256]{1,0:T(8,128)(2,1)S(1)}, u32[]{:S(2)}, u32[]{:S(2)}) collective-permute-start(s16[272,256]{1,0:T(8,128)(2,1)S(1)} %get-tuple-element.60), channel_id=1, source_target_pairs={{0,1},{1,0},{2,3},{3,2},{4,5},{5,4},{6,7},{7,6},{8,9},{9,8},{10,11... | collective-permute-start | bytes 417800 | tf_op jit(solution)/shard_map/ppermute | solution.py:30
  114.7 3.4 %shard_map.60 = (f32[256,256]{1,0:T(8,128)S(1)}, s16[272,256]{1,0:T(8,128)(2,1)S(1)}, f32[8,256]{1,0:T(8,128)S(1)}) custom-call(s32[5]{0:T(128)S(1)} %copy-done.19, bf16[512,4096]{1,0:T(8,128)(2,1)S(1)} %copy-done.1, bf16[64,4096]{1,0:T(8,128)(2,1)} %collective-permute-done.18.refs_1_, bf16[64,4096]{1,0:T(8,128)(2,1)S(1)} %collective-permute-done.9.refs_4_.refs_2_, ...), custom_call_target="tpu_custom_call" | custom-call | flops 1073741824 | bytes 1048576 | tf_op jit(solution)/shard_map/pallas_call | solution.py:188
  119.2 6.3 %collective-permute-done.15.back = s16[256,256]{1,0:T(8,128)(2,1)S(1)} collective-permute-done((s16[256,256]{1,0:T(8,128)(2,1)S(1)}, s16[256,256]{1,0:T(8,128)(2,1)S(1)}, u32[]{:S(2)}, u32[]{:S(2)}) %collective-permute-start.15) | collective-permute-done | bytes 131104 | tf_op jit(solution)/shard_map/ppermute | solution.py:30
  125.5 3.0 %collective-permute-done.17.refs_4_ = s16[272,256]{1,0:T(8,128)(2,1)S(1)} collective-permute-done((s16[272,256]{1,0:T(8,128)(2,1)S(1)}, s16[272,256]{1,0:T(8,128)(2,1)S(1)}, u32[]{:S(2)}, u32[]{:S(2)}) %collective-permute-start.17) | collective-permute-done | bytes 139296 | tf_op jit(solution)/shard_map/ppermute | solution.py:30
  128.5 7.6 %collective-permute-done.20.refs_7_ = s16[272,256]{1,0:T(8,128)(2,1)S(1)} collective-permute-done((s16[272,256]{1,0:T(8,128)(2,1)S(1)}, s16[272,256]{1,0:T(8,128)(2,1)S(1)}, u32[]{:S(2)}, u32[]{:S(2)}) %collective-permute-start.20) | collective-permute-done | bytes 139296 | tf_op jit(solution)/shard_map/ppermute | solution.py:30
  136.1 3.3 %shard_map.61 = f32[256,8,128]{2,1,0:T(8,128)} custom-call(s32[6]{0:T(128)S(1)} %stack.88.at, f32[512,128]{1,0:T(8,128)S(1)} %get-tuple-element.43.refs_5_.rst, s16[256,256]{1,0:T(8,128)(2,1)S(1)} %collective-permute-done.15.back, f32[256,512]{1,0:T(8,128)S(1)} %copy-done.8, s16[544,256]{1,0:T(8,128)(2,1)S(1)} %collective-permute-done.16.refs_1_, ...), custom_call_target="tpu_custom_call" | custom-call | flops 16777216 | bytes 1048576 | tf_op jit(solution)/shard_map/pallas_call | solution.py:188
  (78 shorter events, 16.2 us)
Async XLA Ops:
  6.5 87.5 %all-gather.2.cloned.1.call-start = ((), (), s32[]{:S(2)}) async-start(), calls=%async_computation | async-start | bytes 4718592 | tf_op jit(solution)/shard_map/all_gather | solution.py:295
  9.2 71.5 %copy-start.2 = (bf16[64,4096]{1,0:T(8,128)(2,1)S(1)}, bf16[64,4096]{1,0:T(8,128)(2,1)}, u32[]{:S(2)}) copy-start(bf16[64,4096]{1,0:T(8,128)(2,1)} %shard_map.55.refs_2_.refs_4_) | copy-start | bytes 1572868
  9.2 26.4 %collective-permute-start.4 = (bf16[64,4096]{1,0:T(8,128)(2,1)}, bf16[64,4096]{1,0:T(8,128)(2,1)S(1)}, u32[]{:S(2)}, u32[]{:S(2)}) collective-permute-start(bf16[64,4096]{1,0:T(8,128)(2,1)} %shard_map.55.refs_2_.refs_4_), channel_id=1, source_target_pairs={{0,48},{1,49},{2,50},{3,51},{4,52},{5,53},{6,54},{7,55},{8,56},{9,... | collective-permute-start | bytes 1572872 | tf_op jit(solution)/shard_map/ppermute | solution.py:30
  10.0 25.6 %collective-permute-start.3 = (bf16[64,4096]{1,0:T(8,128)(2,1)}, bf16[64,4096]{1,0:T(8,128)(2,1)S(1)}, u32[]{:S(2)}, u32[]{:S(2)}) collective-permute-start(bf16[64,4096]{1,0:T(8,128)(2,1)} %shard_map.55.refs_2_.refs_4_), channel_id=1, source_target_pairs={{0,16},{1,17},{2,18},{3,19},{4,20},{5,21},{6,22},{7,23},{8,24},{9,... | collective-permute-start | bytes 1572872 | tf_op jit(solution)/shard_map/ppermute | solution.py:30
  12.5 23.1 %collective-permute-start.2 = (bf16[64,4096]{1,0:T(8,128)(2,1)}, bf16[64,4096]{1,0:T(8,128)(2,1)S(1)}, u32[]{:S(2)}, u32[]{:S(2)}) collective-permute-start(bf16[64,4096]{1,0:T(8,128)(2,1)} %shard_map.55.refs_2_.refs_4_), channel_id=1, source_target_pairs={{0,32},{1,33},{2,34},{3,35},{4,36},{5,37},{6,38},{7,39},{8,40},{9,... | collective-permute-start | bytes 1572872 | tf_op jit(solution)/shard_map/ppermute | solution.py:30
  12.5 23.1 %collective-permute-start.1 = (bf16[64,4096]{1,0:T(8,128)(2,1)}, bf16[64,4096]{1,0:T(8,128)(2,1)S(1)}, u32[]{:S(2)}, u32[]{:S(2)}) collective-permute-start(bf16[64,4096]{1,0:T(8,128)(2,1)} %shard_map.55.refs_2_.refs_4_), channel_id=1, source_target_pairs={{0,192},{1,193},{2,194},{3,195},{4,196},{5,197},{6,198},{7,199},{8... | collective-permute-start | bytes 1572872 | tf_op jit(solution)/shard_map/ppermute | solution.py:30
  17.2 22.8 %collective-permute-start = (bf16[64,4096]{1,0:T(8,128)(2,1)}, bf16[64,4096]{1,0:T(8,128)(2,1)S(1)}, u32[]{:S(2)}, u32[]{:S(2)}) collective-permute-start(bf16[64,4096]{1,0:T(8,128)(2,1)} %shard_map.55.refs_2_.refs_4_), channel_id=1, source_target_pairs={{0,64},{1,65},{2,66},{3,67},{4,68},{5,69},{6,70},{7,71},{8,72},{9,... | collective-permute-start | bytes 1572872 | tf_op jit(solution)/shard_map/ppermute | solution.py:30
  40.0 15.3 %collective-permute-start.8 = (bf16[64,4096]{1,0:T(8,128)(2,1)S(1)}, bf16[64,4096]{1,0:T(8,128)(2,1)S(1)}, u32[]{:S(2)}, u32[]{:S(2)}) collective-permute-start(bf16[64,4096]{1,0:T(8,128)(2,1)S(1)} %collective-permute-done.2), channel_id=1, source_target_pairs={{0,12},{1,13},{2,14},{3,15},{4,0},{5,1},{6,2},{7,3},{8,4},{9,5},{1... | collective-permute-start | bytes 1572872 | tf_op jit(solution)/shard_map/ppermute | solution.py:30
  40.5 14.8 %collective-permute-start.7 = (bf16[64,4096]{1,0:T(8,128)(2,1)S(1)}, bf16[64,4096]{1,0:T(8,128)(2,1)S(1)}, u32[]{:S(2)}, u32[]{:S(2)}) collective-permute-start(bf16[64,4096]{1,0:T(8,128)(2,1)S(1)} %collective-permute-done.2), channel_id=1, source_target_pairs={{0,4},{1,5},{2,6},{3,7},{4,8},{5,9},{6,10},{7,11},{8,12},{9,13},{1... | collective-permute-start | bytes 1572872 | tf_op jit(solution)/shard_map/ppermute | solution.py:30
  42.0 13.3 %collective-permute-start.6 = (bf16[64,4096]{1,0:T(8,128)(2,1)S(1)}, bf16[64,4096]{1,0:T(8,128)(2,1)S(1)}, u32[]{:S(2)}, u32[]{:S(2)}) collective-permute-start(bf16[64,4096]{1,0:T(8,128)(2,1)S(1)} %collective-permute-done.refs_6_.refs_8_.refs_3_), channel_id=1, source_target_pairs={{0,48},{1,49},{2,50},{3,51},{4,52},{5,53},{6,54},{7,55},{8,56},{9,... | collective-permute-start | bytes 1572872 | tf_op jit(solution)/shard_map/ppermute | solution.py:30
  42.9 13.3 %collective-permute-start.5 = (bf16[64,4096]{1,0:T(8,128)(2,1)S(1)}, bf16[64,4096]{1,0:T(8,128)(2,1)S(1)}, u32[]{:S(2)}, u32[]{:S(2)}) collective-permute-start(bf16[64,4096]{1,0:T(8,128)(2,1)S(1)} %collective-permute-done.refs_6_.refs_8_.refs_3_), channel_id=1, source_target_pairs={{0,16},{1,17},{2,18},{3,19},{4,20},{5,21},{6,22},{7,23},{8,24},{9,... | collective-permute-start | bytes 1572872 | tf_op jit(solution)/shard_map/ppermute | solution.py:30
  45.3 23.6 %collective-permute-start.9 = (bf16[64,4096]{1,0:T(8,128)(2,1)}, bf16[64,4096]{1,0:T(8,128)(2,1)S(1)}, u32[]{:S(2)}, u32[]{:S(2)}) collective-permute-start(bf16[64,4096]{1,0:T(8,128)(2,1)} %shard_map.55.refs_2_.refs_4_), channel_id=1, source_target_pairs={{0,128},{1,129},{2,130},{3,131},{4,132},{5,133},{6,134},{7,135},{8... | collective-permute-start | bytes 1572872 | tf_op jit(solution)/shard_map/ppermute | solution.py:30
  56.9 17.3 %collective-permute-start.11 = (bf16[64,4096]{1,0:T(8,128)(2,1)S(1)}, bf16[64,4096]{1,0:T(8,128)(2,1)S(1)}, u32[]{:S(2)}, u32[]{:S(2)}) collective-permute-start(bf16[64,4096]{1,0:T(8,128)(2,1)S(1)} %collective-permute-done.1.refs_5_.refs_2_.refs_4_), channel_id=1, source_target_pairs={{0,48},{1,49},{2,50},{3,51},{4,52},{5,53},{6,54},{7,55},{8,56},{9,... | collective-permute-start | bytes 1572872 | tf_op jit(solution)/shard_map/ppermute | solution.py:30
  57.8 16.5 %collective-permute-start.10 = (bf16[64,4096]{1,0:T(8,128)(2,1)S(1)}, bf16[64,4096]{1,0:T(8,128)(2,1)S(1)}, u32[]{:S(2)}, u32[]{:S(2)}) collective-permute-start(bf16[64,4096]{1,0:T(8,128)(2,1)S(1)} %collective-permute-done.1.refs_5_.refs_2_.refs_4_), channel_id=1, source_target_pairs={{0,16},{1,17},{2,18},{3,19},{4,20},{5,21},{6,22},{7,23},{8,24},{9,... | collective-permute-start | bytes 1572872 | tf_op jit(solution)/shard_map/ppermute | solution.py:30
  60.2 14.1 %collective-permute-start.12 = (bf16[64,4096]{1,0:T(8,128)(2,1)S(1)}, bf16[64,4096]{1,0:T(8,128)(2,1)S(1)}, u32[]{:S(2)}, u32[]{:S(2)}) collective-permute-start(bf16[64,4096]{1,0:T(8,128)(2,1)S(1)} %collective-permute-done.2), channel_id=1, source_target_pairs={{0,8},{1,9},{2,10},{3,11},{4,12},{5,13},{6,14},{7,15},{8,0},{9,1},... | collective-permute-start | bytes 1572872 | tf_op jit(solution)/shard_map/ppermute | solution.py:30
  76.1 4.5 %collective-permute-start.13 = (bf16[256,4096]{1,0:T(8,128)(2,1)}, bf16[256,4096]{1,0:T(8,128)(2,1)}, u32[]{:S(2)}, u32[]{:S(2)}) collective-permute-start(bf16[256,4096]{1,0:T(8,128)(2,1)} %constant_dynamic-update-slice_fusion.refs_0_), channel_id=1, source_target_pairs={{0,2},{1,3},{2,0},{3,1},{4,6},{5,7},{6,4},{7,5},{8,10},{9,11},{10,... | collective-permute-start | bytes 6291464 | tf_op jit(solution)/shard_map/ppermute | solution.py:30
  76.1 38.5 %collective-permute-start.19 = (bf16[64,4096]{1,0:T(8,128)(2,1)S(1)}, bf16[64,4096]{1,0:T(8,128)(2,1)}, u32[]{:S(2)}, u32[]{:S(2)}) collective-permute-start(bf16[64,4096]{1,0:T(8,128)(2,1)S(1)} %collective-permute-done.9.refs_4_.refs_2_), channel_id=1, source_target_pairs={{0,48},{1,49},{2,50},{3,51},{4,52},{5,53},{6,54},{7,55},{8,56},{9,... | collective-permute-start | bytes 1572872 | tf_op jit(solution)/shard_map/ppermute | solution.py:30
  76.1 38.5 %collective-permute-start.18 = (bf16[64,4096]{1,0:T(8,128)(2,1)S(1)}, bf16[64,4096]{1,0:T(8,128)(2,1)}, u32[]{:S(2)}, u32[]{:S(2)}) collective-permute-start(bf16[64,4096]{1,0:T(8,128)(2,1)S(1)} %collective-permute-done.9.refs_4_.refs_2_), channel_id=1, source_target_pairs={{0,16},{1,17},{2,18},{3,19},{4,20},{5,21},{6,22},{7,23},{8,24},{9,... | collective-permute-start | bytes 1572872 | tf_op jit(solution)/shard_map/ppermute | solution.py:30
  88.4 30.0 %collective-permute-start.14 = (s16[272,256]{1,0:T(8,128)(2,1)}, s16[272,256]{1,0:T(8,128)(2,1)S(1)}, u32[]{:S(2)}, u32[]{:S(2)}) collective-permute-start(s16[272,256]{1,0:T(8,128)(2,1)} %get-tuple-element.51), channel_id=1, source_target_pairs={{0,1},{1,0},{2,3},{3,2},{4,5},{5,4},{6,7},{7,6},{8,9},{9,8},{10,11... | collective-permute-start | bytes 417800 | tf_op jit(solution)/shard_map/ppermute | solution.py:30
  105.6 30.5 %collective-permute-start.16 = (s16[544,256]{1,0:T(8,128)(2,1)}, s16[544,256]{1,0:T(8,128)(2,1)S(1)}, u32[]{:S(2)}, u32[]{:S(2)}) collective-permute-start(s16[544,256]{1,0:T(8,128)(2,1)} %get-tuple-element.55), channel_id=1, source_target_pairs={{0,1},{1,0},{2,3},{3,2},{4,5},{5,4},{6,7},{7,6},{8,9},{9,8},{10,11... | collective-permute-start | bytes 835592 | tf_op jit(solution)/shard_map/ppermute | solution.py:30
  108.7 27.5 %copy-start.8 = (f32[256,512]{1,0:T(8,128)S(1)}, f32[256,512]{1,0:T(8,128)}, u32[]{:S(2)}) copy-start(f32[256,512]{1,0:T(8,128)} %copy-done.7) | copy-start | bytes 1572868
  108.7 19.9 %collective-permute-start.17 = (s16[272,256]{1,0:T(8,128)(2,1)S(1)}, s16[272,256]{1,0:T(8,128)(2,1)S(1)}, u32[]{:S(2)}, u32[]{:S(2)}) collective-permute-start(s16[272,256]{1,0:T(8,128)(2,1)S(1)} %get-tuple-element.60), channel_id=1, source_target_pairs={{0,1},{1,0},{2,3},{3,2},{4,5},{5,4},{6,7},{7,6},{8,9},{9,8},{10,11... | collective-permute-start | bytes 417800 | tf_op jit(solution)/shard_map/ppermute | solution.py:30
  118.0 18.1 %collective-permute-start.20 = (s16[272,256]{1,0:T(8,128)(2,1)S(1)}, s16[272,256]{1,0:T(8,128)(2,1)S(1)}, u32[]{:S(2)}, u32[]{:S(2)}) collective-permute-start(s16[272,256]{1,0:T(8,128)(2,1)S(1)} %get-tuple-element.63), channel_id=1, source_target_pairs={{0,1},{1,0},{2,3},{3,2},{4,5},{5,4},{6,7},{7,6},{8,9},{9,8},{10,11... | collective-permute-start | bytes 417800 | tf_op jit(solution)/shard_map/ppermute | solution.py:30
  119.0 6.6 %collective-permute-start.15 = (s16[256,256]{1,0:T(8,128)(2,1)S(1)}, s16[256,256]{1,0:T(8,128)(2,1)S(1)}, u32[]{:S(2)}, u32[]{:S(2)}) collective-permute-start(s16[256,256]{1,0:T(8,128)(2,1)S(1)} %shard_map.58), channel_id=1, source_target_pairs={{0,32},{1,33},{2,34},{3,35},{4,36},{5,37},{6,38},{7,39},{8,40},{9,... | collective-permute-start | bytes 393224 | tf_op jit(solution)/shard_map/ppermute | solution.py:30
  (19 other events, 90.4 us)
Sparse Core Ops, SparseCore 0:
  9.3 38.6 all-gather.1

commit v4 on v3

--- a/solution.py
+++ b/solution.py
@@ -7,30 +7,31 @@
 from jax import lax
 from jax.experimental import pallas as pl
 from jax.experimental.pallas import tpu as pltpu
+from jax.sharding import Mesh
 from jax.sharding import PartitionSpec as P
 
-AXES = ("row", "col", "cell")
-ZL, NY, NX, NC, NH = 4, 4, 4, 2, 2
+AXES = ("z", "y", "x", "core", "cell")
+DIMS = (4, 4, 4, 2, 2)
+NZ, NY, NX, NC, NH = DIMS
 EPS = 1e-05
 FULL = 32767.0
 BOUND = 96.0
 NT = (((1,), (1,)), ((), ()))
 
 
-def shift(zl=0, y=0, x=0, c=0, h=0):
-    dims, step, pairs = (ZL, NY, NX, NC, NH), (zl, y, x, c, h), []
-    for i in range(math.prod(dims)):
-        at = np.unravel_index(i, dims)
-        to = [(int(a) + s) % d for a, s, d in zip(at, step, dims)]
-        pairs.append((i, int(np.ravel_multi_index(to, dims))))
-    return pairs
-
-
 def move(value, **steps):
-    return lax.ppermute(value, AXES, shift(**steps))
-
-
-def resid_kernel(limit, place, order, counts, size, mean, disp, out, turned):
+    step, pairs = [steps.get(axis, 0) for axis in AXES], []
+    for i in range(math.prod(DIMS)):
+        to = [(int(a) + s) % d for a, s, d in zip(np.unravel_index(i, DIMS), step, DIMS)]
+        pairs.append((i, int(np.ravel_multi_index(to, DIMS))))
+    return lax.ppermute(value, AXES, pairs)
+
+
+def spread_x(copies):
+    return lax.all_to_all(copies, "x", 0, 0, tiled=True)
+
+
+def resid_kernel(limit, place, order, counts, size, mean, disp, out, copies, turned):
     genes = out.shape[0]
     block = order[place[0]]
     line = block * genes // 128
@@ -45,18 +46,24 @@
         expected = mean_gene * size[:, span]
         scale = lax.rsqrt(expected + expected * expected * spare)
         value = (counts[:, span].astype(jnp.float32) - expected) * scale
-        out[:, span] = jnp.clip(value, -limit, limit).astype(jnp.bfloat16)
+        value = jnp.clip(value, -limit, limit).astype(jnp.bfloat16)
+        out[:, span] = value
+        for j in range(copies.shape[0] // genes):
+            copies[genes * j : genes * j + genes, span] = value
 
 
 def residuals(counts, size_factors, gene_means, dispersions, block_order):
     genes, cells = counts.shape
-    place = lax.axis_index(("row", "col")).astype(jnp.int32)
+    place = lax.axis_index(AXES[:4]).astype(jnp.int32)
     smem, vmem = pl.BlockSpec(memory_space=pltpu.SMEM), pl.BlockSpec(memory_space=pltpu.VMEM)
     return pl.pallas_call(
         functools.partial(resid_kernel, math.sqrt(cells * NH)),
         in_specs=[smem, smem, vmem, vmem, vmem, vmem],
-        out_specs=vmem,
-        out_shape=jax.ShapeDtypeStruct((genes, cells), jnp.bfloat16),
+        out_specs=[vmem, vmem],
+        out_shape=[
+            jax.ShapeDtypeStruct((genes, cells), jnp.bfloat16),
+            jax.ShapeDtypeStruct((NX * genes, cells), jnp.bfloat16),
+        ],
         scratch_shapes=[pltpu.VMEM((128, 8), jnp.float32)],
     )(
         place[None],
@@ -114,10 +121,11 @@
     return jnp.sqrt(square - mean * mean + EPS)
 
 
-def tile_kernel(cells, count, parts, first, at, *refs):
+def tile_kernel(cells, count, first, at, *refs):
     refs = list(refs)
-    rows = [refs.pop(0) for _ in range(parts)]
-    pieces = [refs.pop(0) for _ in range(4 * count)]
+    rows = refs[:2]
+    pieces = refs[2 : 2 + 4 * count]
+    refs = refs[2 + 4 * count :]
     given = None if first else refs.pop(0)
     own, msg, cst = refs.pop(0), refs.pop(0), refs.pop(0)
     rst = refs.pop(0) if first else given
@@ -125,20 +133,13 @@
     half = own.shape[0]
 
     for i, p in enumerate(pieces):
-        place = 256 * (i // 4) + at[1 + i] * 64
+        place = 256 * (i // 4) + at[2 + i] * 64
         cbuf[pl.ds(pl.multiple_of(place, 64), 64), :] = p[...]
-    if parts == 1:
-        rbuf = rows[0]
-    else:
-        rbuf = refs[2]
-        for j, part in enumerate(rows):
-            for i in range(part.shape[0] // 64):
-                place = at[1 + 4 * count + 4 * j + i] * 64
-                rbuf[pl.ds(pl.multiple_of(place, 64), 64), :] = part[64 * i : 64 * i + 64, :]
 
     total = sums = squares = row_sums = row_squares = 0.0
     for k in range(0, cells, 1024):
-        r, c = rbuf[:, k : k + 1024], cbuf[:, k : k + 1024]
+        c = cbuf[:, k : k + 1024]
+        r = jnp.concatenate([part[:, k : k + 1024] for part in rows], axis=0)
         total += lax.dot_general(r, c, NT, preferred_element_type=jnp.float32)
         wide = c.astype(jnp.float32)
         sums += fold(wide)
@@ -147,7 +148,13 @@
             wide = r.astype(jnp.float32)
             row_sums += fold(wide)
             row_squares += fold(wide * wide)
-    acc[...] = total
+    for i in range(NX * NC):
+        core = at[1] if i < NX else 1 - at[1]
+        span = pl.ds(pl.multiple_of((NC * (i % NX) + core) * 64, 64), 64)
+        acc[span, :] = total[64 * i : 64 * i + 64, :]
+        if first:
+            refs[-2][span, :] = row_sums[64 * i : 64 * i + 64, :]
+            refs[-1][span, :] = row_squares[64 * i : 64 * i + 64, :]
 
     scale = 1.0 / cells
     mine = pl.multiple_of(at[0] * half, half)
@@ -155,9 +162,8 @@
     extra = []
     if first:
         rs, rq = refs[-2:]
-        rs[...], rq[...] = row_sums, row_squares
-        mean = jnp.sum(row_sums, axis=1, keepdims=True) * scale
-        dev = deviation(jnp.sum(row_squares, axis=1, keepdims=True) * scale, mean)
+        mean = jnp.sum(rs[...], axis=1, keepdims=True) * scale
+        dev = deviation(jnp.sum(rq[...], axis=1, keepdims=True) * scale, mean)
         lane = lax.broadcasted_iota(jnp.int32, rst.shape, 1)
         rst[...] = jnp.where(lane == 0, mean, dev)
         mean = lane_sums(rs[pl.ds(other, half), :]) * scale
@@ -179,7 +185,7 @@
         own[:, span] = acc[pl.ds(mine, half), span] * scale - rst[pl.ds(mine, half), 0:1] * mean
 
 
-VMEM_LIMIT = 32 * 1024 * 1024
+VMEM_LIMIT = 24 * 1024 * 1024
 VMEM = pl.BlockSpec(memory_space=pltpu.VMEM)
 SMEM = pl.BlockSpec(memory_space=pltpu.SMEM)
 
@@ -196,7 +202,7 @@
     )(jnp.stack(at).astype(jnp.int32), *args)
 
 
-def tiles(rows, sets, rstat, half_id, slots, places=()):
+def tiles(rows, sets, rstat, half_id, core, slots):
     n, cells = sum(part.shape[0] for part in rows), rows[0].shape[1]
     half, count, first = n // 2, len(sets), rstat is None
     outs = [
@@ -208,23 +214,26 @@
         pltpu.VMEM((256 * count, cells), jnp.bfloat16),
         pltpu.VMEM((n, 256 * count), jnp.float32),
     ]
-    if len(rows) > 1:
-        scratch.append(pltpu.VMEM((n, cells), jnp.bfloat16))
     if first:
         outs.append(((n, 128), jnp.float32))
         scratch += [pltpu.VMEM((n, 128), jnp.float32)] * 2
-    kernel = functools.partial(tile_kernel, cells, count, len(rows), first)
-    stat = [] if first else [rstat]
     return call(
-        kernel,
+        functools.partial(tile_kernel, cells, count, first),
         outs,
         scratch,
         2 * n * 256 * count * cells,
-        [half_id, *slots, *places],
+        [half_id, core, *slots],
         *rows,
         *[p for s in sets for p in s],
-        *stat,
-    )
+        *([] if first else [rstat]),
+    )
+
+
+def copies_kernel(at, top, bottom, out):
+    n = top.shape[0]
+    for i in range(NX):
+        out[2 * n * i : 2 * n * i + n, :] = top[...]
+        out[2 * n * i + n : 2 * n * i + 2 * n, :] = bottom[...]
 
 
 def merged(mean, mean2, dev, dev2):
@@ -288,45 +297,43 @@
 
 
 def local(counts, size_factors, gene_means, dispersions, block_order):
-    row, col, h = lax.axis_index("row"), lax.axis_index("col"), lax.axis_index("cell")
-    zl, y = row // NY, row % NY
-    x, c = col // NC, col % NC
-    a = residuals(counts, size_factors, gene_means, dispersions, block_order)
-    rows = lax.all_gather(a, "col", axis=0, tiled=True)
+    zl, y, c, h = [lax.axis_index(axis) for axis in ("z", "y", "core", "cell")]
     hold = lax.optimization_barrier
     up, down = {}, {}
-    z1, z3, far = move(a, zl=1), move(a, zl=3), move(a, y=2)
-    up[0], down[0] = move(a, y=1), move(a, y=-1)
-    a, z1, z3, far, up[0], down[0] = hold((a, z1, z3, far, up[0], down[0]))
-
-    z2 = move(a, zl=2)
+    a, copies = residuals(counts, size_factors, gene_means, dispersions, block_order)
+    half = a.shape[0] // 2
+
+    up[0], down[0], z1 = move(a, y=1), move(a, y=-1), move(a, z=1)
+    up[0], down[0], z1 = hold((up[0], down[0], z1))
+
+    rows = spread_x(copies)
+    z2 = move(z1, z=1)
+    far = move(up[0][:half], y=1), move(down[0][half:], y=-1)
+    a, rows, z1, z2, *far = hold((a, rows, z1, z2, *far))
+
+    (far,) = call(copies_kernel, [(copies.shape, a.dtype)], [], 1 << 20, [h], *far)
     up[1], down[1] = move(z1, y=1), move(z1, y=-1)
-    f1, f3 = move(far, x=1), move(far, x=-1)
-    z3, far, up[1], down[1], f1, f3 = hold((z3, far, up[1], down[1], f1, f3))
-
-    up[3], down[3] = move(z3, y=1), move(z3, y=-1)
-    f2 = move(far, x=2)
-    z2, up[3], down[3], f2 = hold((z2, up[3], down[3], f2))
-
-    up[2], down[2] = move(z2, y=1), move(z2, y=-1)
-    far_mine = jnp.concatenate([far, f1, f2, f3], axis=0)
-    far_theirs = move(far_mine, c=1)
-    z = [a, z1, z2, z3]
+    z3 = move(a, z=3)
+    rows = rows, move(rows, core=1)
+    z2, z3, up[1], down[1], *rows = hold((z2, z3, up[1], down[1], *rows))
 
     slots = [(y - 1) % NY, y, (y + 1) % NY, (y + 2) % NY]
     pieces = lambda k: (up[k], z[k], down[k], z[k])
-    own01, msg01, cst01, rstat = tiles([rows], [pieces(0), pieces(1)], None, h, slots * 2)
-    msg01 = move(msg01, h=1)
-    order = [(x - d) % NX * 2 for d in range(4)]
-    places = [o + c for o in order] + [o + 1 - c for o in order]
-    ownf, msgf, cstf, fstat = tiles(
-        [far_mine, far_theirs], [z], None, h, [jnp.int32(k) for k in range(4)], places
-    )
-    msgf = move(msgf, h=1)
-    own3, msg3, cst3 = tiles([rows], [pieces(3)], rstat, h, slots)
-    msg3 = move(msg3, h=1)
-    own2, msg2, cst2 = tiles([rows], [pieces(2)], rstat, h, slots)
-    msg2 = move(msg2, h=1)
+    z = [a, z1, z2, z3]
+    up[2], down[2] = move(z2, y=1), move(z2, y=-1)
+    own01, msg01, cst01, rstat = tiles(rows, [pieces(0), pieces(1)], None, h, c, slots * 2)
+    far = spread_x(far)
+    z3, up[2], down[2], far, msg01 = hold((z3, up[2], down[2], far, msg01))
+
+    up[3], down[3] = move(z3, y=1), move(z3, y=-1)
+    far = far, move(far, core=1)
+    msg01 = move(msg01, cell=1)
+    own2, msg2, cst2 = tiles(rows, [pieces(2)], rstat, h, c, slots)
+    msg2 = move(msg2, cell=1)
+    ownf, msgf, cstf, fstat = tiles(far, [z], None, h, c, [jnp.int32(k) for k in range(NZ)])
+    msgf = move(msgf, cell=1)
+    own3, msg3, cst3 = tiles(rows, [pieces(3)], rstat, h, c, slots)
+    msg3 = move(msg3, cell=1)
 
     half = ownf.shape[0]
     (back,) = call(
@@ -335,21 +342,22 @@
     back = move(back, y=2)
 
     (result,) = call(
-        functools.partial(final_kernel, ((0, 1), (3,), (2,))),
+        functools.partial(final_kernel, ((0, 1), (2,), (3,))),
         [((half, 8, 128), jnp.float32)],
         [],
         1 << 24,
-        [h, (y + 2) % NY] + [(zl - k) % ZL for k in range(ZL)],
-        *(rstat, back, own01, msg01, cst01, own3, msg3, cst3, own2, msg2, cst2),
+        [h, (y + 2) % NY] + [(zl - k) % NZ for k in range(NZ)],
+        *(rstat, back, own01, msg01, cst01, own2, msg2, cst2, own3, msg3, cst3),
     )
     return result.reshape(half, 1, 1024)
 
 
 def solution(mesh):
+    fine = Mesh(mesh.devices.reshape(DIMS), AXES)
     return jax.shard_map(
         local,
-        mesh=mesh,
-        in_specs=(P(("row", "col"), "cell"), P("cell"), P(), P(), P()),
-        out_specs=P(("row", "cell"), "col", None),
+        mesh=fine,
+        in_specs=(P(AXES[:4], "cell"), P("cell"), P(), P(), P()),
+        out_specs=P(("z", "y", "cell"), ("x", "core"), None),
         check_vma=False,
     )

time: 147 us -> 130 us (0.88)
  waiting for transfers between devices: 58.8 us -> 40.3 us
  between operations: 13.6 us -> 0.17 us
  starting transfers between devices: 35.5 us -> 44.7 us
  Pallas kernels: 24.8 us -> 28.8 us
    ppermute x21 -> x20, waiting for transfers between devices: 58.8 us -> 40.3 us  [move(): return lax.ppermute(value, AXES, pairs)]
    all_to_all x0 -> x2, starting transfers between devices: none -> 9.96 us  [spread_x(): return lax.all_to_all(copies, 'x', 0, 0, tiled=True)]
    pallas_call x6 -> x7, Pallas kernels: 22.2 us -> 25.4 us  [call(): pl.pallas_call(kernel, in_specs=[SMEM] + [VMEM] * len(args), out_specs=[V...]
    unnamed x45 -> x46, local copies, waits for them, and re-layouts: 11.4 us -> 14 us
    ppermute x21 -> x20, starting transfers between devices: 35.5 us -> 34.8 us  [move(): return lax.ppermute(value, AXES, pairs)]
  transfers between devices with their start and end apart: 22 -> 22, of which waited for: 8 -> 7; matrix products, arithmetic and copies ran while one was open for 3% -> 0% of each run, Pallas kernels for 13% -> 17%
where the time goes in v4:
time: 130 us; the launch traced here: 128 us
  starting transfers between devices  44.7 us (34%)
  waiting for transfers between devices  40.3 us (31%)
  Pallas kernels  28.8 us (22%)
  local copies, waits for them, and re-layouts  14.3 us (11%)
    ppermute x20, waiting for transfers between devices, move(): return lax.ppermute(value, AXES, pairs)  40.3 us
    ppermute x20, starting transfers between devices, move(): return lax.ppermute(value, AXES, pairs)  34.8 us
    pallas_call x7, Pallas kernels, call(): pl.pallas_call(kernel, in_specs=[SMEM] + [VMEM] * len(args), out_specs=[V...  25.4 us
    unnamed x46, local copies, waits for them, and re-layouts  14 us
    all_to_all x2, starting transfers between devices, spread_x(): return lax.all_to_all(copies, 'x', 0, 0, tiled=True)  9.96 us
    pallas_call x1, Pallas kernels, residuals(): pl.pallas_call(functools.partial(resid_kernel, math.sqrt(cells * NH)), in...  3.37 us
  transfers between devices with their start and end apart: 22, of which 7 were waited for; matrix products, arithmetic and copies ran while one was open for 0% of the time, Pallas kernels for 17%

profile of v4, /device:TPU:26, one launch (start us, length us, event | category | flops | bytes accessed | tf_op | source)
XLA Modules:
  0.0 128.4 jit_solution(7144276579573397218)
XLA Ops:
  0.0 3.4 %shard_map.55 = (bf16[64,4096]{1,0:T(8,128)(2,1)}, bf16[256,4096]{1,0:T(8,128)(2,1)}) custom-call(s32[1]{0:T(128)} %bitcast.10.place, s32[128]{0:T(128)} %order.1, s32[64,4096]{1,0:T(8,128)} %counts.1, f32[1,4096]{1,0:T(1,128)} %bitcast.27, f32[64,128]{1,0:T(8,128)} %bitcast.25, f32[64,128]{1,0:T(8,128)} %bitcast.26), custom_call_target="tpu_custom_call" | custom-call | tf_op jit(solution)/shard_map/pallas_call | solution.py:59
  3.4 5.0 %all-to-all-start = ((bf16[4,64,4096]{2,1,0:T(8,128)(2,1)}), bf16[4,64,4096]{2,1,0:T(8,128)(2,1)S(1)}, u32[]{:S(2)}, u32[]{:S(2)}) async-start(bf16[4,64,4096]{2,1,0:T(8,128)(2,1)} %bitcast.24), calls=%async_computation | async-start | bytes 4194304 | tf_op jit(solution)/shard_map/all_to_all | solution.py:31
  8.3 1.9 %collective-permute-start.2 = (bf16[64,4096]{1,0:T(8,128)(2,1)S(1)}, bf16[64,4096]{1,0:T(8,128)(2,1)S(1)}, u32[]{:S(2)}, u32[]{:S(2)}) collective-permute-start(bf16[64,4096]{1,0:T(8,128)(2,1)S(1)} %copy-done.1), channel_id=1, source_target_pairs={{0,64},{1,65},{2,66},{3,67},{4,68},{5,69},{6,70},{7,71},{8,72},{9,... | collective-permute-start | bytes 1572872 | tf_op jit(solution)/shard_map/ppermute | solution.py:27
  11.0 2.5 %collective-permute-start = (bf16[64,4096]{1,0:T(8,128)(2,1)S(1)}, bf16[64,4096]{1,0:T(8,128)(2,1)S(1)}, u32[]{:S(2)}, u32[]{:S(2)}) collective-permute-start(bf16[64,4096]{1,0:T(8,128)(2,1)S(1)} %copy-done.1), channel_id=1, source_target_pairs={{0,16},{1,17},{2,18},{3,19},{4,20},{5,21},{6,22},{7,23},{8,24},{9,... | collective-permute-start | bytes 1572872 | tf_op jit(solution)/shard_map/ppermute | solution.py:27
  13.5 10.8 %collective-permute-done.2.refs_7_.refs_9_.refs_3_ = bf16[64,4096]{1,0:T(8,128)(2,1)S(1)} collective-permute-done((bf16[64,4096]{1,0:T(8,128)(2,1)S(1)}, bf16[64,4096]{1,0:T(8,128)(2,1)S(1)}, u32[]{:S(2)}, u32[]{:S(2)}) %collective-permute-start.2) | collective-permute-done | bytes 524320 | tf_op jit(solution)/shard_map/ppermute | solution.py:27
  24.3 1.9 %collective-permute-start.3 = (bf16[64,4096]{1,0:T(8,128)(2,1)S(1)}, bf16[64,4096]{1,0:T(8,128)(2,1)}, u32[]{:S(2)}, u32[]{:S(2)}) collective-permute-start(bf16[64,4096]{1,0:T(8,128)(2,1)S(1)} %collective-permute-done.2.refs_7_.refs_9_.refs_3_), channel_id=1, source_target_pairs={{0,64},{1,65},{2,66},{3,67},{4,68},{5,69},{6,70},{7,71},{8,72},{9,... | collective-permute-start | bytes 1572872 | tf_op jit(solution)/shard_map/ppermute | solution.py:27
  26.4 3.2 %collective-permute-start.4 = (bf16[32,4096]{1,0:T(8,128)(2,1)S(1)}, bf16[32,4096]{1,0:T(8,128)(2,1)S(1)}, u32[]{:S(2)}, u32[]{:S(2)}) collective-permute-start(bf16[32,4096]{1,0:T(8,128)(2,1)S(1)} %slice.6), channel_id=1, source_target_pairs={{0,16},{1,17},{2,18},{3,19},{4,20},{5,21},{6,22},{7,23},{8,24},{9,... | collective-permute-start | bytes 786440 | tf_op jit(solution)/shard_map/ppermute | solution.py:27
  29.6 4.3 %collective-permute-done.5.bottom = bf16[32,4096]{1,0:T(8,128)(2,1)S(1)} collective-permute-done((bf16[32,4096]{1,0:T(8,128)(2,1)S(1)}, bf16[32,4096]{1,0:T(8,128)(2,1)S(1)}, u32[]{:S(2)}, u32[]{:S(2)}) %collective-permute-start.5) | collective-permute-done | bytes 262176 | tf_op jit(solution)/shard_map/ppermute | solution.py:27
  34.7 4.1 %collective-permute-done.3.refs_4_.refs_3_.refs_5_ = bf16[64,4096]{1,0:T(8,128)(2,1)} collective-permute-done((bf16[64,4096]{1,0:T(8,128)(2,1)S(1)}, bf16[64,4096]{1,0:T(8,128)(2,1)}, u32[]{:S(2)}, u32[]{:S(2)}) %collective-permute-start.3) | collective-permute-done | bytes 524320 | tf_op jit(solution)/shard_map/ppermute | solution.py:27
  39.9 1.4 %copy-done = bf16[256,4096]{1,0:T(8,128)(2,1)} copy-done((bf16[256,4096]{1,0:T(8,128)(2,1)}, bf16[256,4096]{1,0:T(8,128)(2,1)S(1)}, u32[]{:S(2)}) %copy-start) | copy-done | bytes 2097176
  41.3 5.0 %all-to-all-start.1 = ((bf16[4,64,4096]{2,1,0:T(8,128)(2,1)}), bf16[4,64,4096]{2,1,0:T(8,128)(2,1)}, u32[]{:S(2)}, u32[]{:S(2)}) async-start(bf16[4,64,4096]{2,1,0:T(8,128)(2,1)} %bitcast.23), calls=%async_computation.1 | async-start | bytes 4194304 | tf_op jit(solution)/shard_map/all_to_all | solution.py:31
  47.2 3.2 %collective-permute-start.7 = (bf16[64,4096]{1,0:T(8,128)(2,1)S(1)}, bf16[64,4096]{1,0:T(8,128)(2,1)S(1)}, u32[]{:S(2)}, u32[]{:S(2)}) collective-permute-start(bf16[64,4096]{1,0:T(8,128)(2,1)S(1)} %collective-permute-done.2.refs_7_.refs_9_.refs_3_), channel_id=1, source_target_pairs={{0,16},{1,17},{2,18},{3,19},{4,20},{5,21},{6,22},{7,23},{8,24},{9,... | collective-permute-start | bytes 1572872 | tf_op jit(solution)/shard_map/ppermute | solution.py:27
  50.4 9.9 %collective-permute-done.6.refs_5_.refs_3_ = bf16[64,4096]{1,0:T(8,128)(2,1)S(1)} collective-permute-done((bf16[64,4096]{1,0:T(8,128)(2,1)S(1)}, bf16[64,4096]{1,0:T(8,128)(2,1)S(1)}, u32[]{:S(2)}, u32[]{:S(2)}) %collective-permute-start.6) | collective-permute-done | bytes 524320 | tf_op jit(solution)/shard_map/ppermute | solution.py:27
  60.3 1.8 %collective-permute-done.8.refs_8_ = bf16[64,4096]{1,0:T(8,128)(2,1)S(1)} collective-permute-done((bf16[64,4096]{1,0:T(8,128)(2,1)S(1)}, bf16[64,4096]{1,0:T(8,128)(2,1)S(1)}, u32[]{:S(2)}, u32[]{:S(2)}) %collective-permute-start.8) | collective-permute-done | bytes 524320 | tf_op jit(solution)/shard_map/ppermute | solution.py:27
  63.8 3.2 %collective-permute-start.10 = (bf16[64,4096]{1,0:T(8,128)(2,1)}, bf16[64,4096]{1,0:T(8,128)(2,1)}, u32[]{:S(2)}, u32[]{:S(2)}) collective-permute-start(bf16[64,4096]{1,0:T(8,128)(2,1)} %collective-permute-done.3.refs_4_.refs_3_.refs_5_), channel_id=1, source_target_pairs={{0,16},{1,17},{2,18},{3,19},{4,20},{5,21},{6,22},{7,23},{8,24},{9,... | collective-permute-start | bytes 1572872 | tf_op jit(solution)/shard_map/ppermute | solution.py:27
  71.3 6.1 %shard_map.56 = (f32[256,512]{1,0:T(8,128)S(1)}, s16[544,256]{1,0:T(8,128)(2,1)S(1)}, f32[16,256]{1,0:T(8,128)S(1)}, f32[512,128]{1,0:T(8,128)S(1)}) custom-call(s32[10]{0:T(128)S(1)} %stack.76.at, bf16[256,4096]{1,0:T(8,128)(2,1)S(1)} %bitcast.20, bf16[256,4096]{1,0:T(8,128)(2,1)} %collective-permute-done.9.refs_1_, bf16[64,4096]{1,0:T(8,128)(2,1)S(1)} %copy-done.7, ...), custom_call_target="tpu_custom_call" | custom-call | flops 2147483648 | bytes 1048576 | tf_op jit(solution)/shard_map/pallas_call | solution.py:194
  79.6 3.2 %collective-permute-start.17 = (bf16[64,4096]{1,0:T(8,128)(2,1)}, bf16[64,4096]{1,0:T(8,128)(2,1)}, u32[]{:S(2)}, u32[]{:S(2)}) collective-permute-start(bf16[64,4096]{1,0:T(8,128)(2,1)} %copy-done.2), channel_id=1, source_target_pairs={{0,16},{1,17},{2,18},{3,19},{4,20},{5,21},{6,22},{7,23},{8,24},{9,... | collective-permute-start | bytes 1572872 | tf_op jit(solution)/shard_map/ppermute | solution.py:27
  83.0 5.8 %collective-permute-start.15 = (s16[544,256]{1,0:T(8,128)(2,1)}, s16[544,256]{1,0:T(8,128)(2,1)}, u32[]{:S(2)}, u32[]{:S(2)}) collective-permute-start(s16[544,256]{1,0:T(8,128)(2,1)} %copy-done.22), channel_id=1, source_target_pairs={{0,1},{1,0},{2,3},{3,2},{4,5},{5,4},{6,7},{7,6},{8,9},{9,8},{10,11... | collective-permute-start | bytes 835592 | tf_op jit(solution)/shard_map/ppermute | solution.py:27
  89.8 5.5 %shard_map.58 = (f32[256,256]{1,0:T(8,128)S(1)}, s16[272,256]{1,0:T(8,128)(2,1)S(1)}, f32[8,256]{1,0:T(8,128)S(1)}, f32[512,128]{1,0:T(8,128)S(1)}) custom-call(s32[6]{0:T(128)S(1)} %stack.77.at, bf16[256,4096]{1,0:T(8,128)(2,1)} %bitcast.17.refs_0_, bf16[256,4096]{1,0:T(8,128)(2,1)} %collective-permute-done.12.refs_1_, bf16[64,4096]{1,0:T(8,128)(2,1)S(1)} %copy-done.1, ...), custom_call_target="tpu_custom_call" | custom-call | flops 1073741824 | bytes 1048576 | tf_op jit(solution)/shard_map/pallas_call | solution.py:194
  96.6 4.9 %shard_map.60 = (f32[256,256]{1,0:T(8,128)S(1)}, s16[272,256]{1,0:T(8,128)(2,1)}, f32[8,256]{1,0:T(8,128)S(1)}) custom-call(s32[6]{0:T(128)S(1)} %stack.78.at, bf16[256,4096]{1,0:T(8,128)(2,1)S(1)} %bitcast.21, bf16[256,4096]{1,0:T(8,128)(2,1)} %collective-permute-done.9.refs_1_, bf16[64,4096]{1,0:T(8,128)(2,1)} %collective-permute-done.10.refs_2_, ...), custom_call_target="tpu_custom_call" | custom-call | flops 1073741824 | bytes 1048576 | tf_op jit(solution)/shard_map/pallas_call | solution.py:194
  101.5 5.0 %collective-permute-start.16 = (s16[272,256]{1,0:T(8,128)(2,1)}, s16[272,256]{1,0:T(8,128)(2,1)S(1)}, u32[]{:S(2)}, u32[]{:S(2)}) collective-permute-start(s16[272,256]{1,0:T(8,128)(2,1)} %get-tuple-element.71), channel_id=1, source_target_pairs={{0,1},{1,0},{2,3},{3,2},{4,5},{5,4},{6,7},{7,6},{8,9},{9,8},{10,11... | collective-permute-start | bytes 417800 | tf_op jit(solution)/shard_map/ppermute | solution.py:27
  107.1 4.6 %shard_map.61 = (f32[256,256]{1,0:T(8,128)S(1)}, s16[272,256]{1,0:T(8,128)(2,1)}, f32[8,256]{1,0:T(8,128)S(1)}) custom-call(s32[6]{0:T(128)S(1)} %copy-done.21, bf16[256,4096]{1,0:T(8,128)(2,1)S(1)} %bitcast.22, bf16[256,4096]{1,0:T(8,128)(2,1)} %collective-permute-done.9.refs_1_, bf16[64,4096]{1,0:T(8,128)(2,1)} %collective-permute-done.17.refs_2_, ...), custom_call_target="tpu_custom_call" | custom-call | flops 1073741824 | bytes 1048576 | tf_op jit(solution)/shard_map/pallas_call | solution.py:194
  114.6 8.6 %collective-permute-done.19.refs_7_ = s16[272,256]{1,0:T(8,128)(2,1)S(1)} collective-permute-done((s16[272,256]{1,0:T(8,128)(2,1)}, s16[272,256]{1,0:T(8,128)(2,1)S(1)}, u32[]{:S(2)}, u32[]{:S(2)}) %collective-permute-start.19) | collective-permute-done | bytes 139296 | tf_op jit(solution)/shard_map/ppermute | solution.py:27
  124.6 3.8 %shard_map.62 = f32[256,8,128]{2,1,0:T(8,128)} custom-call(s32[6]{0:T(128)S(1)} %stack.34.at, f32[512,128]{1,0:T(8,128)S(1)} %get-tuple-element.54.refs_6_.rst, s16[256,256]{1,0:T(8,128)(2,1)S(1)} %collective-permute-done.14.back, f32[256,512]{1,0:T(8,128)S(1)} %copy-done.9, s16[544,256]{1,0:T(8,128)(2,1)} %collective-permute-done.15.refs_1_, ...), custom_call_target="tpu_custom_call" | custom-call | flops 16777216 | bytes 1048576 | tf_op jit(solution)/shard_map/pallas_call | solution.py:194
  (80 shorter events, 19.2 us)
Async XLA Ops:
  3.4 35.4 %all-to-all-start = ((bf16[4,64,4096]{2,1,0:T(8,128)(2,1)}), bf16[4,64,4096]{2,1,0:T(8,128)(2,1)S(1)}, u32[]{:S(2)}, u32[]{:S(2)}) async-start(bf16[4,64,4096]{2,1,0:T(8,128)(2,1)} %bitcast.24), calls=%async_computation | async-start | bytes 4194304 | tf_op jit(solution)/shard_map/all_to_all | solution.py:31
  8.3 16.0 %collective-permute-start.2 = (bf16[64,4096]{1,0:T(8,128)(2,1)S(1)}, bf16[64,4096]{1,0:T(8,128)(2,1)S(1)}, u32[]{:S(2)}, u32[]{:S(2)}) collective-permute-start(bf16[64,4096]{1,0:T(8,128)(2,1)S(1)} %copy-done.1), channel_id=1, source_target_pairs={{0,64},{1,65},{2,66},{3,67},{4,68},{5,69},{6,70},{7,71},{8,72},{9,... | collective-permute-start | bytes 1572872 | tf_op jit(solution)/shard_map/ppermute | solution.py:27
  10.2 14.1 %collective-permute-start.1 = (bf16[64,4096]{1,0:T(8,128)(2,1)S(1)}, bf16[64,4096]{1,0:T(8,128)(2,1)S(1)}, u32[]{:S(2)}, u32[]{:S(2)}) collective-permute-start(bf16[64,4096]{1,0:T(8,128)(2,1)S(1)} %copy-done.1), channel_id=1, source_target_pairs={{0,48},{1,49},{2,50},{3,51},{4,52},{5,53},{6,54},{7,55},{8,56},{9,... | collective-permute-start | bytes 1572872 | tf_op jit(solution)/shard_map/ppermute | solution.py:27
  11.0 13.3 %collective-permute-start = (bf16[64,4096]{1,0:T(8,128)(2,1)S(1)}, bf16[64,4096]{1,0:T(8,128)(2,1)S(1)}, u32[]{:S(2)}, u32[]{:S(2)}) collective-permute-start(bf16[64,4096]{1,0:T(8,128)(2,1)S(1)} %copy-done.1), channel_id=1, source_target_pairs={{0,16},{1,17},{2,18},{3,19},{4,20},{5,21},{6,22},{7,23},{8,24},{9,... | collective-permute-start | bytes 1572872 | tf_op jit(solution)/shard_map/ppermute | solution.py:27
  24.3 14.5 %collective-permute-start.3 = (bf16[64,4096]{1,0:T(8,128)(2,1)S(1)}, bf16[64,4096]{1,0:T(8,128)(2,1)}, u32[]{:S(2)}, u32[]{:S(2)}) collective-permute-start(bf16[64,4096]{1,0:T(8,128)(2,1)S(1)} %collective-permute-done.2.refs_7_.refs_9_.refs_3_), channel_id=1, source_target_pairs={{0,64},{1,65},{2,66},{3,67},{4,68},{5,69},{6,70},{7,71},{8,72},{9,... | collective-permute-start | bytes 1572872 | tf_op jit(solution)/shard_map/ppermute | solution.py:27
  26.3 7.7 %collective-permute-start.5 = (bf16[32,4096]{1,0:T(8,128)(2,1)S(1)}, bf16[32,4096]{1,0:T(8,128)(2,1)S(1)}, u32[]{:S(2)}, u32[]{:S(2)}) collective-permute-start(bf16[32,4096]{1,0:T(8,128)(2,1)S(1)} %slice.7), channel_id=1, source_target_pairs={{0,48},{1,49},{2,50},{3,51},{4,52},{5,53},{6,54},{7,55},{8,56},{9,... | collective-permute-start | bytes 786440 | tf_op jit(solution)/shard_map/ppermute | solution.py:27
  26.4 7.6 %collective-permute-start.4 = (bf16[32,4096]{1,0:T(8,128)(2,1)S(1)}, bf16[32,4096]{1,0:T(8,128)(2,1)S(1)}, u32[]{:S(2)}, u32[]{:S(2)}) collective-permute-start(bf16[32,4096]{1,0:T(8,128)(2,1)S(1)} %slice.6), channel_id=1, source_target_pairs={{0,16},{1,17},{2,18},{3,19},{4,20},{5,21},{6,22},{7,23},{8,24},{9,... | collective-permute-start | bytes 786440 | tf_op jit(solution)/shard_map/ppermute | solution.py:27
  38.8 25.0 %collective-permute-start.9 = (bf16[256,4096]{1,0:T(8,128)(2,1)S(1)}, bf16[256,4096]{1,0:T(8,128)(2,1)}, u32[]{:S(2)}, u32[]{:S(2)}) collective-permute-start(bf16[256,4096]{1,0:T(8,128)(2,1)S(1)} %bitcast.19), channel_id=1, source_target_pairs={{0,2},{1,3},{2,0},{3,1},{4,6},{5,7},{6,4},{7,5},{8,10},{9,11},{10,... | collective-permute-start | bytes 6291464 | tf_op jit(solution)/shard_map/ppermute | solution.py:27
  41.3 38.2 %all-to-all-start.1 = ((bf16[4,64,4096]{2,1,0:T(8,128)(2,1)}), bf16[4,64,4096]{2,1,0:T(8,128)(2,1)}, u32[]{:S(2)}, u32[]{:S(2)}) async-start(bf16[4,64,4096]{2,1,0:T(8,128)(2,1)} %bitcast.23), calls=%async_computation.1 | async-start | bytes 4194304 | tf_op jit(solution)/shard_map/all_to_all | solution.py:31
  46.3 14.1 %collective-permute-start.6 = (bf16[64,4096]{1,0:T(8,128)(2,1)S(1)}, bf16[64,4096]{1,0:T(8,128)(2,1)S(1)}, u32[]{:S(2)}, u32[]{:S(2)}) collective-permute-start(bf16[64,4096]{1,0:T(8,128)(2,1)S(1)} %copy-done.1), channel_id=1, source_target_pairs={{0,192},{1,193},{2,194},{3,195},{4,196},{5,197},{6,198},{7,199},{8... | collective-permute-start | bytes 1572872 | tf_op jit(solution)/shard_map/ppermute | solution.py:27
  47.2 15.0 %collective-permute-start.8 = (bf16[64,4096]{1,0:T(8,128)(2,1)S(1)}, bf16[64,4096]{1,0:T(8,128)(2,1)S(1)}, u32[]{:S(2)}, u32[]{:S(2)}) collective-permute-start(bf16[64,4096]{1,0:T(8,128)(2,1)S(1)} %collective-permute-done.2.refs_7_.refs_9_.refs_3_), channel_id=1, source_target_pairs={{0,48},{1,49},{2,50},{3,51},{4,52},{5,53},{6,54},{7,55},{8,56},{9,... | collective-permute-start | bytes 1572872 | tf_op jit(solution)/shard_map/ppermute | solution.py:27
  47.2 15.8 %collective-permute-start.7 = (bf16[64,4096]{1,0:T(8,128)(2,1)S(1)}, bf16[64,4096]{1,0:T(8,128)(2,1)S(1)}, u32[]{:S(2)}, u32[]{:S(2)}) collective-permute-start(bf16[64,4096]{1,0:T(8,128)(2,1)S(1)} %collective-permute-done.2.refs_7_.refs_9_.refs_3_), channel_id=1, source_target_pairs={{0,16},{1,17},{2,18},{3,19},{4,20},{5,21},{6,22},{7,23},{8,24},{9,... | collective-permute-start | bytes 1572872 | tf_op jit(solution)/shard_map/ppermute | solution.py:27
  63.8 15.7 %collective-permute-start.11 = (bf16[64,4096]{1,0:T(8,128)(2,1)}, bf16[64,4096]{1,0:T(8,128)(2,1)}, u32[]{:S(2)}, u32[]{:S(2)}) collective-permute-start(bf16[64,4096]{1,0:T(8,128)(2,1)} %collective-permute-done.3.refs_4_.refs_3_.refs_5_), channel_id=1, source_target_pairs={{0,48},{1,49},{2,50},{3,51},{4,52},{5,53},{6,54},{7,55},{8,56},{9,... | collective-permute-start | bytes 1572872 | tf_op jit(solution)/shard_map/ppermute | solution.py:27
  63.8 15.7 %collective-permute-start.10 = (bf16[64,4096]{1,0:T(8,128)(2,1)}, bf16[64,4096]{1,0:T(8,128)(2,1)}, u32[]{:S(2)}, u32[]{:S(2)}) collective-permute-start(bf16[64,4096]{1,0:T(8,128)(2,1)} %collective-permute-done.3.refs_4_.refs_3_.refs_5_), channel_id=1, source_target_pairs={{0,16},{1,17},{2,18},{3,19},{4,20},{5,21},{6,22},{7,23},{8,24},{9,... | collective-permute-start | bytes 1572872 | tf_op jit(solution)/shard_map/ppermute | solution.py:27
  79.4 9.3 %collective-permute-start.12 = (bf16[256,4096]{1,0:T(8,128)(2,1)}, bf16[256,4096]{1,0:T(8,128)(2,1)}, u32[]{:S(2)}, u32[]{:S(2)}) collective-permute-start(bf16[256,4096]{1,0:T(8,128)(2,1)} %bitcast.17.refs_0_), channel_id=1, source_target_pairs={{0,2},{1,3},{2,0},{3,1},{4,6},{5,7},{6,4},{7,5},{8,10},{9,11},{10,... | collective-permute-start | bytes 6291464 | tf_op jit(solution)/shard_map/ppermute | solution.py:27
  79.5 26.9 %collective-permute-start.18 = (bf16[64,4096]{1,0:T(8,128)(2,1)}, bf16[64,4096]{1,0:T(8,128)(2,1)}, u32[]{:S(2)}, u32[]{:S(2)}) collective-permute-start(bf16[64,4096]{1,0:T(8,128)(2,1)} %copy-done.2), channel_id=1, source_target_pairs={{0,48},{1,49},{2,50},{3,51},{4,52},{5,53},{6,54},{7,55},{8,56},{9,... | collective-permute-start | bytes 1572872 | tf_op jit(solution)/shard_map/ppermute | solution.py:27
  79.6 26.8 %collective-permute-start.17 = (bf16[64,4096]{1,0:T(8,128)(2,1)}, bf16[64,4096]{1,0:T(8,128)(2,1)}, u32[]{:S(2)}, u32[]{:S(2)}) collective-permute-start(bf16[64,4096]{1,0:T(8,128)(2,1)} %copy-done.2), channel_id=1, source_target_pairs={{0,16},{1,17},{2,18},{3,19},{4,20},{5,21},{6,22},{7,23},{8,24},{9,... | collective-permute-start | bytes 1572872 | tf_op jit(solution)/shard_map/ppermute | solution.py:27
  82.9 13.7 %copy-start.20 = (s32[6]{0:T(128)}, s32[6]{0:T(128)S(1)}, u32[]{:S(2)}) copy-start(s32[6]{0:T(128)S(1)} %stack.78.at) | copy-start | bytes 76
  83.0 31.5 %collective-permute-start.15 = (s16[544,256]{1,0:T(8,128)(2,1)}, s16[544,256]{1,0:T(8,128)(2,1)}, u32[]{:S(2)}, u32[]{:S(2)}) collective-permute-start(s16[544,256]{1,0:T(8,128)(2,1)} %copy-done.22), channel_id=1, source_target_pairs={{0,1},{1,0},{2,3},{3,2},{4,5},{5,4},{6,7},{7,6},{8,9},{9,8},{10,11... | collective-permute-start | bytes 835592 | tf_op jit(solution)/shard_map/ppermute | solution.py:27
  95.3 17.3 %collective-permute-start.13 = (s16[272,256]{1,0:T(8,128)(2,1)S(1)}, s16[272,256]{1,0:T(8,128)(2,1)S(1)}, u32[]{:S(2)}, u32[]{:S(2)}) collective-permute-start(s16[272,256]{1,0:T(8,128)(2,1)S(1)} %get-tuple-element.62), channel_id=1, source_target_pairs={{0,1},{1,0},{2,3},{3,2},{4,5},{5,4},{6,7},{7,6},{8,9},{9,8},{10,11... | collective-permute-start | bytes 417800 | tf_op jit(solution)/shard_map/ppermute | solution.py:27
  101.5 21.7 %copy-start.9 = (f32[256,512]{1,0:T(8,128)S(1)}, f32[256,512]{1,0:T(8,128)}, u32[]{:S(2)}) copy-start(f32[256,512]{1,0:T(8,128)} %copy-done.8) | copy-start | bytes 1572868
  101.5 13.1 %collective-permute-start.16 = (s16[272,256]{1,0:T(8,128)(2,1)}, s16[272,256]{1,0:T(8,128)(2,1)S(1)}, u32[]{:S(2)}, u32[]{:S(2)}) collective-permute-start(s16[272,256]{1,0:T(8,128)(2,1)} %get-tuple-element.71), channel_id=1, source_target_pairs={{0,1},{1,0},{2,3},{3,2},{4,5},{5,4},{6,7},{7,6},{8,9},{9,8},{10,11... | collective-permute-start | bytes 417800 | tf_op jit(solution)/shard_map/ppermute | solution.py:27
  111.6 11.6 %collective-permute-start.19 = (s16[272,256]{1,0:T(8,128)(2,1)}, s16[272,256]{1,0:T(8,128)(2,1)S(1)}, u32[]{:S(2)}, u32[]{:S(2)}) collective-permute-start(s16[272,256]{1,0:T(8,128)(2,1)} %get-tuple-element.75), channel_id=1, source_target_pairs={{0,1},{1,0},{2,3},{3,2},{4,5},{5,4},{6,7},{7,6},{8,9},{9,8},{10,11... | collective-permute-start | bytes 417800 | tf_op jit(solution)/shard_map/ppermute | solution.py:27
  113.2 10.0 %collective-permute-start.14 = (s16[256,256]{1,0:T(8,128)(2,1)S(1)}, s16[256,256]{1,0:T(8,128)(2,1)S(1)}, u32[]{:S(2)}, u32[]{:S(2)}) collective-permute-start(s16[256,256]{1,0:T(8,128)(2,1)S(1)} %shard_map.59), channel_id=1, source_target_pairs={{0,32},{1,33},{2,34},{3,35},{4,36},{5,37},{6,38},{7,39},{8,40},{9,... | collective-permute-start | bytes 393224 | tf_op jit(solution)/shard_map/ppermute | solution.py:27
  (21 other events, 43.3 us)

commit v5 on v4

--- a/solution.py
+++ b/solution.py
@@ -48,7 +48,7 @@
         value = (counts[:, span].astype(jnp.float32) - expected) * scale
         value = jnp.clip(value, -limit, limit).astype(jnp.bfloat16)
         out[:, span] = value
-        for j in range(copies.shape[0] // genes):
+        for j in range(NX):
             copies[genes * j : genes * j + genes, span] = value
 
 
@@ -65,6 +65,7 @@
             jax.ShapeDtypeStruct((NX * genes, cells), jnp.bfloat16),
         ],
         scratch_shapes=[pltpu.VMEM((128, 8), jnp.float32)],
+        compiler_params=pltpu.CompilerParams(vmem_limit_bytes=VMEM_LIMIT),
     )(
         place[None],
         block_order,
@@ -121,25 +122,47 @@
     return jnp.sqrt(square - mean * mean + EPS)
 
 
-def tile_kernel(cells, count, first, at, *refs):
+def tile_kernel(cells, chunks, count, pieces, parts, first, export, at, *refs):
     refs = list(refs)
-    rows = refs[:2]
-    pieces = refs[2 : 2 + 4 * count]
-    refs = refs[2 + 4 * count :]
+    blocks = [refs.pop(0) for _ in range(pieces)]
+    rows = [refs.pop(0) for _ in range(1 + parts[-1][0] if parts else 1)]
     given = None if first else refs.pop(0)
     own, msg, cst = refs.pop(0), refs.pop(0), refs.pop(0)
     rst = refs.pop(0) if first else given
-    cbuf, acc = refs[:2]
+    ordered = refs.pop(0) if export else None
+    rbuf = refs.pop(0) if parts else rows[0]
+    cbuf, acc, sems = refs[:3]
     half = own.shape[0]
-
-    for i, p in enumerate(pieces):
-        place = 256 * (i // 4) + at[2 + i] * 64
-        cbuf[pl.ds(pl.multiple_of(place, 64), 64), :] = p[...]
-
+    width = cells // chunks
+    block_at = [pl.ds(pl.multiple_of(at[1 + i] * 32, 64), 64) for i in range(pieces)]
+
+    def copies(k):
+        cells_k = pl.ds(width * k, width)
+        pairs = [(p.at[:, cells_k], cbuf.at[span, cells_k]) for p, span in zip(blocks, block_at)]
+        for i, (ref, start, size) in enumerate(parts):
+            span = pl.ds(pl.multiple_of(at[1 + pieces + i] * 32, 32), size)
+            pairs.append((rows[ref].at[pl.ds(start, size), cells_k], rbuf.at[span, cells_k]))
+        made = [pltpu.make_async_copy(*pair, sems.at[k, i]) for i, pair in enumerate(pairs)]
+        for copy in made:
+            copy.start()
+        return made
+
+    flight = [copies(0), copies(1)] if parts else [[]] * chunks
+    if not parts:
+        for p, span in zip(blocks, block_at):
+            cbuf[span, :] = p[...]
+    if pieces < 4 * count:
+        for t in range(count):
+            span = pl.ds(pl.multiple_of(at[1 + pieces + len(parts) + t] * 32, 64), 64)
+            cbuf[span, :] = jnp.zeros((64, cells), cbuf.dtype)
     total = sums = squares = row_sums = row_squares = 0.0
-    for k in range(0, cells, 1024):
-        c = cbuf[:, k : k + 1024]
-        r = jnp.concatenate([part[:, k : k + 1024] for part in rows], axis=0)
+    for k in range(chunks):
+        for copy in flight[k]:
+            copy.wait()
+        if parts and k + 2 < chunks:
+            flight.append(copies(k + 2))
+        cells_k = slice(width * k, width * k + width)
+        r, c = rbuf[:, cells_k], cbuf[:, cells_k]
         total += lax.dot_general(r, c, NT, preferred_element_type=jnp.float32)
         wide = c.astype(jnp.float32)
         sums += fold(wide)
@@ -148,13 +171,13 @@
             wide = r.astype(jnp.float32)
             row_sums += fold(wide)
             row_squares += fold(wide * wide)
-    for i in range(NX * NC):
-        core = at[1] if i < NX else 1 - at[1]
-        span = pl.ds(pl.multiple_of((NC * (i % NX) + core) * 64, 64), 64)
-        acc[span, :] = total[64 * i : 64 * i + 64, :]
-        if first:
-            refs[-2][span, :] = row_sums[64 * i : 64 * i + 64, :]
-            refs[-1][span, :] = row_squares[64 * i : 64 * i + 64, :]
+    if export:
+        out = pltpu.make_async_copy(rbuf, ordered, sems.at[0, 0])
+        out.start()
+    acc[...] = total
+    if first:
+        refs[-2][...] = row_sums
+        refs[-1][...] = row_squares
 
     scale = 1.0 / cells
     mine = pl.multiple_of(at[0] * half, half)
@@ -183,57 +206,74 @@
         )
         msg[base + half : base + half + 16, :] = pack([*split(mean), *split(dev), *extra])
         own[:, span] = acc[pl.ds(mine, half), span] * scale - rst[pl.ds(mine, half), 0:1] * mean
-
-
-VMEM_LIMIT = 24 * 1024 * 1024
+    if export:
+        out.wait()
+
+
+VMEM_LIMIT = 60 * 1024 * 1024
 VMEM = pl.BlockSpec(memory_space=pltpu.VMEM)
 SMEM = pl.BlockSpec(memory_space=pltpu.SMEM)
-
-
-def call(kernel, outs, scratch, flops, at, *args):
+HBM = pl.BlockSpec(memory_space=pltpu.HBM)
+
+
+class From:
+    def __init__(self, table, first):
+        self.table, self.first = table, first
+
+    def __getitem__(self, i):
+        return self.table[self.first + i]
+
+
+def call(kernel, outs, scratch, flops, at, *args, places=None, out_places=None, limit=32 * 1024 * 1024):
+    table, first = at
     return pl.pallas_call(
-        kernel,
-        in_specs=[SMEM] + [VMEM] * len(args),
-        out_specs=[VMEM] * len(outs),
+        lambda table, *refs: kernel(From(table, first), *refs),
+        in_specs=[SMEM] + (places or [VMEM] * len(args)),
+        out_specs=out_places or [VMEM] * len(outs),
         out_shape=[jax.ShapeDtypeStruct(*o) for o in outs],
         scratch_shapes=scratch,
-        compiler_params=pltpu.CompilerParams(vmem_limit_bytes=VMEM_LIMIT),
+        compiler_params=pltpu.CompilerParams(vmem_limit_bytes=limit or VMEM_LIMIT),
         cost_estimate=pl.CostEstimate(flops=flops, bytes_accessed=1 << 20, transcendentals=0),
-    )(jnp.stack(at).astype(jnp.int32), *args)
-
-
-def tiles(rows, sets, rstat, half_id, core, slots):
+    )(table, *args)
+
+
+def tiles(rows, sets, rstat, at, empty=False, export=False):
+    rows, parts = rows
     n, cells = sum(part.shape[0] for part in rows), rows[0].shape[1]
-    half, count, first = n // 2, len(sets), rstat is None
+    half, count, first, chunks = n // 2, len(sets), rstat is None, 4
+    pieces = [p for s in sets for p in s]
     outs = [
         ((half, 256 * count), jnp.float32),
         (((half + 16) * count, 256), jnp.int16),
         ((8 * count, 256), jnp.float32),
     ]
-    scratch = [
+    out_places = [VMEM] * 3
+    scratch = [pltpu.VMEM((n, cells), jnp.bfloat16)] if parts else []
+    scratch += [
         pltpu.VMEM((256 * count, cells), jnp.bfloat16),
         pltpu.VMEM((n, 256 * count), jnp.float32),
+        pltpu.SemaphoreType.DMA((chunks, len(pieces) + len(parts))),
     ]
     if first:
         outs.append(((n, 128), jnp.float32))
+        out_places.append(VMEM)
         scratch += [pltpu.VMEM((n, 128), jnp.float32)] * 2
+    if export:
+        outs.append(((n, cells), jnp.bfloat16))
+        out_places.append(HBM)
     return call(
-        functools.partial(tile_kernel, cells, count, first),
+        functools.partial(tile_kernel, cells, chunks, count, len(pieces), parts, first, export),
         outs,
         scratch,
-        2 * n * 256 * count * cells,
-        [half_id, core, *slots],
+        int(1.15e9 * (2.5 + 1.5 * count + (3.5 if parts else 0))),
+        at,
+        *pieces,
         *rows,
-        *[p for s in sets for p in s],
         *([] if first else [rstat]),
-    )
-
-
-def copies_kernel(at, top, bottom, out):
-    n = top.shape[0]
-    for i in range(NX):
-        out[2 * n * i : 2 * n * i + n, :] = top[...]
-        out[2 * n * i + n : 2 * n * i + 2 * n, :] = bottom[...]
+        places=[HBM if parts else VMEM] * (len(rows) + len(pieces)) + ([] if first else [VMEM]),
+        out_places=out_places,
+        limit=VMEM_LIMIT if parts else 32 * 1024 * 1024,
+    )
 
 
 def merged(mean, mean2, dev, dev2):
@@ -297,57 +337,71 @@
 
 
 def local(counts, size_factors, gene_means, dispersions, block_order):
-    zl, y, c, h = [lax.axis_index(axis) for axis in ("z", "y", "core", "cell")]
+    zl, y, x, c, h = [lax.axis_index(axis) for axis in AXES]
     hold = lax.optimization_barrier
     up, down = {}, {}
+    near, last = [(y - 1) % NY * 2, y * 2, (y + 1) % NY * 2], (y + 2) % NY * 2
+    place = lambda at, core: 2 * (NC * (at % NX) + core)
+    row_places = [place(i, core) for core in (c, 1 - c) for i in range(NX)]
+    lists = [
+        [h, *near, *[8 + i for i in near]] + row_places + [last, 8 + last],
+        [h, *near, *[8 + i for i in near], last, 8 + last],
+        [h, *[2 * k for k in range(NZ)]]
+        + [place(x + d, core) for core in (c, 1 - c) for d in (0, -1, 1, 2)],
+        [h, (y + 2) % NY] + [(zl - k) % NZ for k in range(NZ)],
+    ]
+    table = jnp.stack([jnp.asarray(v, jnp.int32) for values in lists for v in values])
+    starts = np.cumsum([0] + [len(values) for values in lists]).tolist()
+    at_one, at_two, at_far, at_end = [(table, start) for start in starts[:4]]
+
     a, copies = residuals(counts, size_factors, gene_means, dispersions, block_order)
-    half = a.shape[0] // 2
-
-    up[0], down[0], z1 = move(a, y=1), move(a, y=-1), move(a, z=1)
-    up[0], down[0], z1 = hold((up[0], down[0], z1))
-
+
+    up[0], down[0], z1, far = move(a, y=1), move(a, y=-1), move(a, z=1), move(a, y=2)
+    z3 = move(a, z=3)
     rows = spread_x(copies)
-    z2 = move(z1, z=1)
-    far = move(up[0][:half], y=1), move(down[0][half:], y=-1)
-    a, rows, z1, z2, *far = hold((a, rows, z1, z2, *far))
-
-    (far,) = call(copies_kernel, [(copies.shape, a.dtype)], [], 1 << 20, [h], *far)
-    up[1], down[1] = move(z1, y=1), move(z1, y=-1)
-    z3 = move(a, z=3)
-    rows = rows, move(rows, core=1)
-    z2, z3, up[1], down[1], *rows = hold((z2, z3, up[1], down[1], *rows))
-
-    slots = [(y - 1) % NY, y, (y + 1) % NY, (y + 2) % NY]
-    pieces = lambda k: (up[k], z[k], down[k], z[k])
+    up[0], down[0], z1, z3, far = hold((up[0], down[0], z1, z3, far))
+
+    up[1], down[1], z2 = move(z1, y=1), move(z1, y=-1), move(z1, z=1)
+    far, far_c = hold((far, move(far, core=1)))
+    right, left = move(far, x=1), move(far, x=-1)
+    rows, z2, up[1], down[1], right, left = hold((rows, z2, up[1], down[1], right, left))
+
+    pieces = lambda k: (up[k], z[k], down[k])
+    up[2], down[2] = move(z2, y=1), move(z2, y=-1)
     z = [a, z1, z2, z3]
-    up[2], down[2] = move(z2, y=1), move(z2, y=-1)
-    own01, msg01, cst01, rstat = tiles(rows, [pieces(0), pieces(1)], None, h, c, slots * 2)
-    far = spread_x(far)
-    z3, up[2], down[2], far, msg01 = hold((z3, up[2], down[2], far, msg01))
-
+    rows_c = move(rows, core=1)
+    across = move(far, x=2)
+    rows = (rows, rows_c), [(i // NX, 64 * (i % NX), 64) for i in range(2 * NX)]
+    own01, msg01, cst01, rstat, ordered = tiles(
+        rows, [pieces(0), pieces(1)], None, at_one, True, True
+    )
+    z3, up[2], down[2], own01, across = hold((z3, up[2], down[2], own01, across))
+
+    z = [a, z1, z2, z3]
     up[3], down[3] = move(z3, y=1), move(z3, y=-1)
-    far = far, move(far, core=1)
+    across_c, right_c, left_c = move(across, core=1), move(right, core=1), move(left, core=1)
     msg01 = move(msg01, cell=1)
-    own2, msg2, cst2 = tiles(rows, [pieces(2)], rstat, h, c, slots)
-    msg2 = move(msg2, cell=1)
-    ownf, msgf, cstf, fstat = tiles(far, [z], None, h, c, [jnp.int32(k) for k in range(NZ)])
+    far = [far, right, left, across, far_c, right_c, left_c, across_c]
+    far = far, [(i, 0, part.shape[0]) for i, part in enumerate(far)]
+    ownf, msgf, cstf, fstat = tiles(far, [z], None, at_far)
+    up[3], down[3], ownf, msg01 = hold((up[3], down[3], ownf, msg01))
     msgf = move(msgf, cell=1)
-    own3, msg3, cst3 = tiles(rows, [pieces(3)], rstat, h, c, slots)
-    msg3 = move(msg3, cell=1)
+    own23, msg23, cst23 = tiles(([ordered], []), [pieces(2), pieces(3)], rstat, at_two, True)
+    msg23 = move(msg23, cell=1)
 
     half = ownf.shape[0]
     (back,) = call(
-        back_kernel, [((half, 256), jnp.int16)], [], 1 << 22, [h], ownf, msgf, cstf, fstat
+        back_kernel, [((half, 256), jnp.int16)], [], 1 << 33, at_end, ownf, msgf, cstf, fstat
     )
     back = move(back, y=2)
 
     (result,) = call(
-        functools.partial(final_kernel, ((0, 1), (2,), (3,))),
+        functools.partial(final_kernel, ((0, 1), (2, 3))),
         [((half, 8, 128), jnp.float32)],
         [],
         1 << 24,
-        [h, (y + 2) % NY] + [(zl - k) % NZ for k in range(NZ)],
-        *(rstat, back, own01, msg01, cst01, own2, msg2, cst2, own3, msg3, cst3),
+        at_end,
+        *(rstat, back, own01, msg01, cst01, own23, msg23, cst23),
     )
     return result.reshape(half, 1, 1024)
 

time: 130 us -> 125 us (0.962)
  local copies, waits for them, and re-layouts: 14.3 us -> 4.67 us
  waiting for transfers between devices: 40.3 us -> 48.3 us
  starting transfers between devices: 44.7 us -> 40.2 us
    unnamed x46 -> x36, local copies, waits for them, and re-layouts: 14 us -> 3.97 us
    ppermute x20 -> x24, waiting for transfers between devices: 40.3 us -> 48.3 us  [move(): return lax.ppermute(value, AXES, pairs)]
    all_to_all x2 -> x1, starting transfers between devices: 9.96 us -> 4.94 us  [spread_x(): return lax.all_to_all(copies, 'x', 0, 0, tiled=True)]
    pallas_call x7 -> x5, Pallas kernels: 25.4 us -> 26.6 us  [call(): pl.pallas_call(lambda table, *refs: kernel(From(table, first), *refs), in...]
    ppermute x20 -> x24, starting transfers between devices: 34.8 us -> 35.2 us  [move(): return lax.ppermute(value, AXES, pairs)]
  transfers between devices with their start and end apart: 22 -> 25, of which waited for: 7 -> 11; matrix products, arithmetic and copies ran while one was open for 0% -> 1% of each run, Pallas kernels for 17% -> 19%
where the time goes in v5:
time: 125 us; the launch traced here: 123 us
  waiting for transfers between devices  48.3 us (39%)
  starting transfers between devices  40.2 us (32%)
  Pallas kernels  30 us (24%)
  local copies, waits for them, and re-layouts  4.67 us (4%)
    ppermute x24, waiting for transfers between devices, move(): return lax.ppermute(value, AXES, pairs)  48.3 us
    ppermute x24, starting transfers between devices, move(): return lax.ppermute(value, AXES, pairs)  35.2 us
    pallas_call x5, Pallas kernels, call(): pl.pallas_call(lambda table, *refs: kernel(From(table, first), *refs), in...  26.6 us
    all_to_all x1, starting transfers between devices, spread_x(): return lax.all_to_all(copies, 'x', 0, 0, tiled=True)  4.94 us
    unnamed x36, local copies, waits for them, and re-layouts  3.97 us
    pallas_call x1, Pallas kernels, residuals(): pl.pallas_call(functools.partial(resid_kernel, math.sqrt(cells * NH)), in...  3.37 us
  transfers between devices with their start and end apart: 25, of which 11 were waited for; matrix products, arithmetic and copies ran while one was open for 1% of the time, Pallas kernels for 19%

profile of v5, /device:TPU:26, one launch (start us, length us, event | category | flops | bytes accessed | tf_op | source)
XLA Modules:
  0.0 123.5 jit_solution(12547631387760275226)
XLA Ops:
  0.0 3.4 %shard_map.55 = (bf16[64,4096]{1,0:T(8,128)(2,1)}, bf16[256,4096]{1,0:T(8,128)(2,1)}) custom-call(s32[1]{0:T(128)} %bitcast.30.place, s32[128]{0:T(128)} %order.1, s32[64,4096]{1,0:T(8,128)} %counts.1, f32[1,4096]{1,0:T(1,128)} %bitcast.40, f32[64,128]{1,0:T(8,128)} %bitcast.38, f32[64,128]{1,0:T(8,128)} %bitcast.39), custom_call_target="tpu_custom_call" | custom-call | tf_op jit(solution)/shard_map/pallas_call | solution.py:59
  3.6 1.8 %collective-permute-start.1 = (bf16[64,4096]{1,0:T(8,128)(2,1)}, bf16[64,4096]{1,0:T(8,128)(2,1)S(1)}, u32[]{:S(2)}, u32[]{:S(2)}) collective-permute-start(bf16[64,4096]{1,0:T(8,128)(2,1)} %get-tuple-element.41.refs_1_.refs_0_), channel_id=1, source_target_pairs={{0,48},{1,49},{2,50},{3,51},{4,52},{5,53},{6,54},{7,55},{8,56},{9,... | collective-permute-start | bytes 1572872 | tf_op jit(solution)/shard_map/ppermute | solution.py:27
  5.4 1.9 %collective-permute-start.2 = (bf16[64,4096]{1,0:T(8,128)(2,1)}, bf16[64,4096]{1,0:T(8,128)(2,1)S(1)}, u32[]{:S(2)}, u32[]{:S(2)}) collective-permute-start(bf16[64,4096]{1,0:T(8,128)(2,1)} %get-tuple-element.41.refs_1_.refs_0_), channel_id=1, source_target_pairs={{0,64},{1,65},{2,66},{3,67},{4,68},{5,69},{6,70},{7,71},{8,72},{9,... | collective-permute-start | bytes 1572872 | tf_op jit(solution)/shard_map/ppermute | solution.py:27
  7.3 2.7 %collective-permute-start.3 = (bf16[64,4096]{1,0:T(8,128)(2,1)}, bf16[64,4096]{1,0:T(8,128)(2,1)}, u32[]{:S(2)}, u32[]{:S(2)}) collective-permute-start(bf16[64,4096]{1,0:T(8,128)(2,1)} %get-tuple-element.41.refs_1_.refs_0_), channel_id=1, source_target_pairs={{0,192},{1,193},{2,194},{3,195},{4,196},{5,197},{6,198},{7,199},{8... | collective-permute-start | bytes 1572872 | tf_op jit(solution)/shard_map/ppermute | solution.py:27
  11.3 4.9 %all-to-all-start = ((bf16[4,64,4096]{2,1,0:T(8,128)(2,1)}), bf16[4,64,4096]{2,1,0:T(8,128)(2,1)}, u32[]{:S(2)}, u32[]{:S(2)}) async-start(bf16[4,64,4096]{2,1,0:T(8,128)(2,1)} %bitcast.37), calls=%async_computation | async-start | bytes 4194304 | tf_op jit(solution)/shard_map/all_to_all | solution.py:31
  16.2 2.2 %collective-permute-done.refs_0_ = bf16[64,4096]{1,0:T(8,128)(2,1)S(1)} collective-permute-done((bf16[64,4096]{1,0:T(8,128)(2,1)}, bf16[64,4096]{1,0:T(8,128)(2,1)S(1)}, u32[]{:S(2)}, u32[]{:S(2)}) %collective-permute-start) | collective-permute-done | bytes 524320 | tf_op jit(solution)/shard_map/ppermute | solution.py:27
  18.4 11.3 %collective-permute-done.1.refs_2_ = bf16[64,4096]{1,0:T(8,128)(2,1)S(1)} collective-permute-done((bf16[64,4096]{1,0:T(8,128)(2,1)}, bf16[64,4096]{1,0:T(8,128)(2,1)S(1)}, u32[]{:S(2)}, u32[]{:S(2)}) %collective-permute-start.1) | collective-permute-done | bytes 524320 | tf_op jit(solution)/shard_map/ppermute | solution.py:27
  29.7 2.2 %collective-permute-done.3.refs_3_.refs_4_ = bf16[64,4096]{1,0:T(8,128)(2,1)} collective-permute-done((bf16[64,4096]{1,0:T(8,128)(2,1)}, bf16[64,4096]{1,0:T(8,128)(2,1)}, u32[]{:S(2)}, u32[]{:S(2)}) %collective-permute-start.3) | collective-permute-done | bytes 524320 | tf_op jit(solution)/shard_map/ppermute | solution.py:27
  31.9 1.7 %collective-permute-start.5 = (bf16[64,4096]{1,0:T(8,128)(2,1)S(1)}, bf16[64,4096]{1,0:T(8,128)(2,1)S(1)}, u32[]{:S(2)}, u32[]{:S(2)}) collective-permute-start(bf16[64,4096]{1,0:T(8,128)(2,1)S(1)} %collective-permute-done.2.refs_4_.refs_1_), channel_id=1, source_target_pairs={{0,64},{1,65},{2,66},{3,67},{4,68},{5,69},{6,70},{7,71},{8,72},{9,... | collective-permute-start | bytes 1572872 | tf_op jit(solution)/shard_map/ppermute | solution.py:27
  37.7 10.4 %collective-permute-done.5.refs_2_.refs_1_ = bf16[64,4096]{1,0:T(8,128)(2,1)S(1)} collective-permute-done((bf16[64,4096]{1,0:T(8,128)(2,1)S(1)}, bf16[64,4096]{1,0:T(8,128)(2,1)S(1)}, u32[]{:S(2)}, u32[]{:S(2)}) %collective-permute-start.5) | collective-permute-done | bytes 524320 | tf_op jit(solution)/shard_map/ppermute | solution.py:27
  48.1 2.0 %collective-permute-done.7.refs_5_ = bf16[64,4096]{1,0:T(8,128)(2,1)S(1)} collective-permute-done((bf16[64,4096]{1,0:T(8,128)(2,1)S(1)}, bf16[64,4096]{1,0:T(8,128)(2,1)S(1)}, u32[]{:S(2)}, u32[]{:S(2)}) %collective-permute-start.7) | collective-permute-done | bytes 524320 | tf_op jit(solution)/shard_map/ppermute | solution.py:27
  52.6 2.1 %collective-permute-start.14 = (bf16[64,4096]{1,0:T(8,128)(2,1)}, bf16[64,4096]{1,0:T(8,128)(2,1)}, u32[]{:S(2)}, u32[]{:S(2)}) collective-permute-start(bf16[64,4096]{1,0:T(8,128)(2,1)} %collective-permute-done.4.refs_4_), channel_id=1, source_target_pairs={{0,8},{1,9},{2,10},{3,11},{4,12},{5,13},{6,14},{7,15},{8,0},{9,1},... | collective-permute-start | bytes 1572872 | tf_op jit(solution)/shard_map/ppermute | solution.py:27
  54.7 2.2 %collective-permute-start.12 = (bf16[64,4096]{1,0:T(8,128)(2,1)S(1)}, bf16[64,4096]{1,0:T(8,128)(2,1)S(1)}, u32[]{:S(2)}, u32[]{:S(2)}) collective-permute-start(bf16[64,4096]{1,0:T(8,128)(2,1)S(1)} %collective-permute-done.5.refs_2_.refs_1_), channel_id=1, source_target_pairs={{0,16},{1,17},{2,18},{3,19},{4,20},{5,21},{6,22},{7,23},{8,24},{9,... | collective-permute-start | bytes 1572872 | tf_op jit(solution)/shard_map/ppermute | solution.py:27
  58.3 9.2 %shard_map.56 = (f32[256,512]{1,0:T(8,128)}, s16[544,256]{1,0:T(8,128)(2,1)}, f32[16,256]{1,0:T(8,128)}, f32[512,128]{1,0:T(8,128)}, bf16[512,4096]{1,0:T(8,128)(2,1)}) custom-call(s32[45]{0:T(128)} %stack.134.table, bf16[64,4096]{1,0:T(8,128)(2,1)} %copy-done.13, bf16[64,4096]{1,0:T(8,128)(2,1)} %get-tuple-element.41.refs_1_.refs_0_, ...), custom_call_target="tpu_custom_call" | custom-call | flops 10350000128 | bytes 1048576 | tf_op jit(solution)/shard_map/pallas_call | solution.py:229
  68.6 3.1 %collective-permute-done.13.refs_2_ = bf16[64,4096]{1,0:T(8,128)(2,1)S(1)} collective-permute-done((bf16[64,4096]{1,0:T(8,128)(2,1)S(1)}, bf16[64,4096]{1,0:T(8,128)(2,1)S(1)}, u32[]{:S(2)}, u32[]{:S(2)}) %collective-permute-start.13) | collective-permute-done | bytes 524320 | tf_op jit(solution)/shard_map/ppermute | solution.py:27
  71.9 1.7 %collective-permute-start.16 = (bf16[64,4096]{1,0:T(8,128)(2,1)}, bf16[64,4096]{1,0:T(8,128)(2,1)S(1)}, u32[]{:S(2)}, u32[]{:S(2)}) collective-permute-start(bf16[64,4096]{1,0:T(8,128)(2,1)} %collective-permute-done.3.refs_3_.refs_4_), channel_id=1, source_target_pairs={{0,48},{1,49},{2,50},{3,51},{4,52},{5,53},{6,54},{7,55},{8,56},{9,... | collective-permute-start | bytes 1572872 | tf_op jit(solution)/shard_map/ppermute | solution.py:27
  73.7 6.4 %collective-permute-start.20 = (s16[544,256]{1,0:T(8,128)(2,1)}, s16[544,256]{1,0:T(8,128)(2,1)S(1)}, u32[]{:S(2)}, u32[]{:S(2)}) collective-permute-start(s16[544,256]{1,0:T(8,128)(2,1)} %get-tuple-element.61), channel_id=1, source_target_pairs={{0,1},{1,0},{2,3},{3,2},{4,5},{5,4},{6,7},{7,6},{8,9},{9,8},{10,11... | collective-permute-start | bytes 835592 | tf_op jit(solution)/shard_map/ppermute | solution.py:27
  81.0 7.6 %shard_map.57 = (f32[256,256]{1,0:T(8,128)}, s16[272,256]{1,0:T(8,128)(2,1)}, f32[8,256]{1,0:T(8,128)}, f32[512,128]{1,0:T(8,128)}) custom-call(s32[45]{0:T(128)} %stack.134.table, bf16[64,4096]{1,0:T(8,128)(2,1)} %get-tuple-element.41.refs_1_.refs_0_, bf16[64,4096]{1,0:T(8,128)(2,1)} %copy-done.11, bf16[64,4096]{1,0:T(8,128)(2,1)} %copy-done.4, ...), custom_call_target="tpu_custom_call" | custom-call | flops 8625000448 | bytes 1048576 | tf_op jit(solution)/shard_map/pallas_call | solution.py:229
  89.1 8.1 %collective-permute-start.21 = (s16[272,256]{1,0:T(8,128)(2,1)}, s16[272,256]{1,0:T(8,128)(2,1)S(1)}, u32[]{:S(2)}, u32[]{:S(2)}) collective-permute-start(s16[272,256]{1,0:T(8,128)(2,1)} %get-tuple-element.63), channel_id=1, source_target_pairs={{0,1},{1,0},{2,3},{3,2},{4,5},{5,4},{6,7},{7,6},{8,9},{9,8},{10,11... | collective-permute-start | bytes 417800 | tf_op jit(solution)/shard_map/ppermute | solution.py:27
  97.2 2.2 %copy-done.6 = bf16[512,4096]{1,0:T(8,128)(2,1)S(1)} copy-done((bf16[512,4096]{1,0:T(8,128)(2,1)S(1)}, bf16[512,4096]{1,0:T(8,128)(2,1)}, u32[]{:S(2)}) %copy-start.6) | copy-done | bytes 4194328
  99.4 5.4 %shard_map.59 = (f32[256,512]{1,0:T(8,128)S(1)}, s16[544,256]{1,0:T(8,128)(2,1)S(1)}, f32[16,256]{1,0:T(8,128)S(1)}) custom-call(s32[45]{0:T(128)S(1)} %copy-done.3, bf16[64,4096]{1,0:T(8,128)(2,1)S(1)} %collective-permute-done.12.refs_0_, bf16[64,4096]{1,0:T(8,128)(2,1)S(1)} %copy-done.5, bf16[64,4096]{1,0:T(8,128)(2,1)S(1)} %collective-permute-done.13.refs_2_, ...), custom_call_target="tpu_custom_call" | custom-call | flops 6325000192 | bytes 1048576 | tf_op jit(solution)/shard_map/pallas_call | solution.py:229
  106.2 6.5 %collective-permute-done.22.refs_1_ = s16[256,256]{1,0:T(8,128)(2,1)S(1)} collective-permute-done((s16[256,256]{1,0:T(8,128)(2,1)S(1)}, s16[256,256]{1,0:T(8,128)(2,1)S(1)}, u32[]{:S(2)}, u32[]{:S(2)}) %collective-permute-start.22) | collective-permute-done | bytes 131104 | tf_op jit(solution)/shard_map/ppermute | solution.py:27
  112.7 7.5 %collective-permute-done.23.refs_6_ = s16[544,256]{1,0:T(8,128)(2,1)S(1)} collective-permute-done((s16[544,256]{1,0:T(8,128)(2,1)S(1)}, s16[544,256]{1,0:T(8,128)(2,1)S(1)}, u32[]{:S(2)}, u32[]{:S(2)}) %collective-permute-start.23) | collective-permute-done | bytes 278560 | tf_op jit(solution)/shard_map/ppermute | solution.py:27
  120.1 3.3 %shard_map.60 = f32[256,8,128]{2,1,0:T(8,128)} custom-call(s32[45]{0:T(128)S(1)} %copy-done.3, f32[512,128]{1,0:T(8,128)S(1)} %copy-done.1, s16[256,256]{1,0:T(8,128)(2,1)S(1)} %collective-permute-done.22.refs_1_, f32[256,512]{1,0:T(8,128)S(1)} %copy-done, s16[544,256]{1,0:T(8,128)(2,1)S(1)} %collective-permute-done.20.refs_3_, f32[16,256]{1,0:T(8,128)S(1)} %copy-done.2, ...), custom_call_target="tpu_custom_call" | custom-call | flops 16777216 | bytes 1048576 | tf_op jit(solution)/shard_map/pallas_call | solution.py:229
  (69 shorter events, 13.5 us)
Async XLA Ops:
  3.4 15.0 %collective-permute-start = (bf16[64,4096]{1,0:T(8,128)(2,1)}, bf16[64,4096]{1,0:T(8,128)(2,1)S(1)}, u32[]{:S(2)}, u32[]{:S(2)}) collective-permute-start(bf16[64,4096]{1,0:T(8,128)(2,1)} %get-tuple-element.41.refs_1_.refs_0_), channel_id=1, source_target_pairs={{0,16},{1,17},{2,18},{3,19},{4,20},{5,21},{6,22},{7,23},{8,24},{9,... | collective-permute-start | bytes 1572872 | tf_op jit(solution)/shard_map/ppermute | solution.py:27
  3.6 26.1 %collective-permute-start.1 = (bf16[64,4096]{1,0:T(8,128)(2,1)}, bf16[64,4096]{1,0:T(8,128)(2,1)S(1)}, u32[]{:S(2)}, u32[]{:S(2)}) collective-permute-start(bf16[64,4096]{1,0:T(8,128)(2,1)} %get-tuple-element.41.refs_1_.refs_0_), channel_id=1, source_target_pairs={{0,48},{1,49},{2,50},{3,51},{4,52},{5,53},{6,54},{7,55},{8,56},{9,... | collective-permute-start | bytes 1572872 | tf_op jit(solution)/shard_map/ppermute | solution.py:27
  5.4 24.3 %collective-permute-start.2 = (bf16[64,4096]{1,0:T(8,128)(2,1)}, bf16[64,4096]{1,0:T(8,128)(2,1)S(1)}, u32[]{:S(2)}, u32[]{:S(2)}) collective-permute-start(bf16[64,4096]{1,0:T(8,128)(2,1)} %get-tuple-element.41.refs_1_.refs_0_), channel_id=1, source_target_pairs={{0,64},{1,65},{2,66},{3,67},{4,68},{5,69},{6,70},{7,71},{8,72},{9,... | collective-permute-start | bytes 1572872 | tf_op jit(solution)/shard_map/ppermute | solution.py:27
  7.3 24.6 %collective-permute-start.3 = (bf16[64,4096]{1,0:T(8,128)(2,1)}, bf16[64,4096]{1,0:T(8,128)(2,1)}, u32[]{:S(2)}, u32[]{:S(2)}) collective-permute-start(bf16[64,4096]{1,0:T(8,128)(2,1)} %get-tuple-element.41.refs_1_.refs_0_), channel_id=1, source_target_pairs={{0,192},{1,193},{2,194},{3,195},{4,196},{5,197},{6,198},{7,199},{8... | collective-permute-start | bytes 1572872 | tf_op jit(solution)/shard_map/ppermute | solution.py:27
  10.0 21.9 %collective-permute-start.4 = (bf16[64,4096]{1,0:T(8,128)(2,1)}, bf16[64,4096]{1,0:T(8,128)(2,1)}, u32[]{:S(2)}, u32[]{:S(2)}) collective-permute-start(bf16[64,4096]{1,0:T(8,128)(2,1)} %get-tuple-element.41.refs_1_.refs_0_), channel_id=1, source_target_pairs={{0,32},{1,33},{2,34},{3,35},{4,36},{5,37},{6,38},{7,39},{8,40},{9,... | collective-permute-start | bytes 1572872 | tf_op jit(solution)/shard_map/ppermute | solution.py:27
  11.3 40.3 %all-to-all-start = ((bf16[4,64,4096]{2,1,0:T(8,128)(2,1)}), bf16[4,64,4096]{2,1,0:T(8,128)(2,1)}, u32[]{:S(2)}, u32[]{:S(2)}) async-start(bf16[4,64,4096]{2,1,0:T(8,128)(2,1)} %bitcast.37), calls=%async_computation | async-start | bytes 4194304 | tf_op jit(solution)/shard_map/all_to_all | solution.py:31
  31.9 16.1 %collective-permute-start.5 = (bf16[64,4096]{1,0:T(8,128)(2,1)S(1)}, bf16[64,4096]{1,0:T(8,128)(2,1)S(1)}, u32[]{:S(2)}, u32[]{:S(2)}) collective-permute-start(bf16[64,4096]{1,0:T(8,128)(2,1)S(1)} %collective-permute-done.2.refs_4_.refs_1_), channel_id=1, source_target_pairs={{0,64},{1,65},{2,66},{3,67},{4,68},{5,69},{6,70},{7,71},{8,72},{9,... | collective-permute-start | bytes 1572872 | tf_op jit(solution)/shard_map/ppermute | solution.py:27
  33.6 14.4 %collective-permute-start.6 = (bf16[64,4096]{1,0:T(8,128)(2,1)S(1)}, bf16[64,4096]{1,0:T(8,128)(2,1)S(1)}, u32[]{:S(2)}, u32[]{:S(2)}) collective-permute-start(bf16[64,4096]{1,0:T(8,128)(2,1)S(1)} %collective-permute-done.2.refs_4_.refs_1_), channel_id=1, source_target_pairs={{0,16},{1,17},{2,18},{3,19},{4,20},{5,21},{6,22},{7,23},{8,24},{9,... | collective-permute-start | bytes 1572872 | tf_op jit(solution)/shard_map/ppermute | solution.py:27
  35.1 14.9 %collective-permute-start.7 = (bf16[64,4096]{1,0:T(8,128)(2,1)S(1)}, bf16[64,4096]{1,0:T(8,128)(2,1)S(1)}, u32[]{:S(2)}, u32[]{:S(2)}) collective-permute-start(bf16[64,4096]{1,0:T(8,128)(2,1)S(1)} %collective-permute-done.2.refs_4_.refs_1_), channel_id=1, source_target_pairs={{0,48},{1,49},{2,50},{3,51},{4,52},{5,53},{6,54},{7,55},{8,56},{9,... | collective-permute-start | bytes 1572872 | tf_op jit(solution)/shard_map/ppermute | solution.py:27
  35.7 15.9 %collective-permute-start.10 = (bf16[64,4096]{1,0:T(8,128)(2,1)}, bf16[64,4096]{1,0:T(8,128)(2,1)}, u32[]{:S(2)}, u32[]{:S(2)}) collective-permute-start(bf16[64,4096]{1,0:T(8,128)(2,1)} %collective-permute-done.4.refs_4_), channel_id=1, source_target_pairs={{0,12},{1,13},{2,14},{3,15},{4,0},{5,1},{6,2},{7,3},{8,4},{9,5},{1... | collective-permute-start | bytes 1572872 | tf_op jit(solution)/shard_map/ppermute | solution.py:27
  36.2 15.4 %collective-permute-start.9 = (bf16[64,4096]{1,0:T(8,128)(2,1)}, bf16[64,4096]{1,0:T(8,128)(2,1)}, u32[]{:S(2)}, u32[]{:S(2)}) collective-permute-start(bf16[64,4096]{1,0:T(8,128)(2,1)} %collective-permute-done.4.refs_4_), channel_id=1, source_target_pairs={{0,4},{1,5},{2,6},{3,7},{4,8},{5,9},{6,10},{7,11},{8,12},{9,13},{1... | collective-permute-start | bytes 1572872 | tf_op jit(solution)/shard_map/ppermute | solution.py:27
  51.6 5.2 %collective-permute-start.11 = (bf16[256,4096]{1,0:T(8,128)(2,1)}, bf16[256,4096]{1,0:T(8,128)(2,1)S(1)}, u32[]{:S(2)}, u32[]{:S(2)}) collective-permute-start(bf16[256,4096]{1,0:T(8,128)(2,1)} %bitcast.35.refs_6_), channel_id=1, source_target_pairs={{0,2},{1,3},{2,0},{3,1},{4,6},{5,7},{6,4},{7,5},{8,10},{9,11},{10,... | collective-permute-start | bytes 6291464 | tf_op jit(solution)/shard_map/ppermute | solution.py:27
  52.6 16.0 %collective-permute-start.14 = (bf16[64,4096]{1,0:T(8,128)(2,1)}, bf16[64,4096]{1,0:T(8,128)(2,1)}, u32[]{:S(2)}, u32[]{:S(2)}) collective-permute-start(bf16[64,4096]{1,0:T(8,128)(2,1)} %collective-permute-done.4.refs_4_), channel_id=1, source_target_pairs={{0,8},{1,9},{2,10},{3,11},{4,12},{5,13},{6,14},{7,15},{8,0},{9,1},... | collective-permute-start | bytes 1572872 | tf_op jit(solution)/shard_map/ppermute | solution.py:27
  54.7 13.9 %collective-permute-start.12 = (bf16[64,4096]{1,0:T(8,128)(2,1)S(1)}, bf16[64,4096]{1,0:T(8,128)(2,1)S(1)}, u32[]{:S(2)}, u32[]{:S(2)}) collective-permute-start(bf16[64,4096]{1,0:T(8,128)(2,1)S(1)} %collective-permute-done.5.refs_2_.refs_1_), channel_id=1, source_target_pairs={{0,16},{1,17},{2,18},{3,19},{4,20},{5,21},{6,22},{7,23},{8,24},{9,... | collective-permute-start | bytes 1572872 | tf_op jit(solution)/shard_map/ppermute | solution.py:27
  56.9 14.8 %collective-permute-start.13 = (bf16[64,4096]{1,0:T(8,128)(2,1)S(1)}, bf16[64,4096]{1,0:T(8,128)(2,1)S(1)}, u32[]{:S(2)}, u32[]{:S(2)}) collective-permute-start(bf16[64,4096]{1,0:T(8,128)(2,1)S(1)} %collective-permute-done.5.refs_2_.refs_1_), channel_id=1, source_target_pairs={{0,48},{1,49},{2,50},{3,51},{4,52},{5,53},{6,54},{7,55},{8,56},{9,... | collective-permute-start | bytes 1572872 | tf_op jit(solution)/shard_map/ppermute | solution.py:27
  56.9 16.8 %collective-permute-start.17 = (bf16[64,4096]{1,0:T(8,128)(2,1)}, bf16[64,4096]{1,0:T(8,128)(2,1)}, u32[]{:S(2)}, u32[]{:S(2)}) collective-permute-start(bf16[64,4096]{1,0:T(8,128)(2,1)} %collective-permute-done.9.refs_5_), channel_id=1, source_target_pairs={{0,2},{1,3},{2,0},{3,1},{4,6},{5,7},{6,4},{7,5},{8,10},{9,11},{10,... | collective-permute-start | bytes 1572872 | tf_op jit(solution)/shard_map/ppermute | solution.py:27
  56.9 23.2 %collective-permute-start.18 = (bf16[64,4096]{1,0:T(8,128)(2,1)}, bf16[64,4096]{1,0:T(8,128)(2,1)}, u32[]{:S(2)}, u32[]{:S(2)}) collective-permute-start(bf16[64,4096]{1,0:T(8,128)(2,1)} %collective-permute-done.10.refs_6_), channel_id=1, source_target_pairs={{0,2},{1,3},{2,0},{3,1},{4,6},{5,7},{6,4},{7,5},{8,10},{9,11},{10,... | collective-permute-start | bytes 1572872 | tf_op jit(solution)/shard_map/ppermute | solution.py:27
  71.7 8.5 %collective-permute-start.19 = (bf16[64,4096]{1,0:T(8,128)(2,1)}, bf16[64,4096]{1,0:T(8,128)(2,1)S(1)}, u32[]{:S(2)}, u32[]{:S(2)}) collective-permute-start(bf16[64,4096]{1,0:T(8,128)(2,1)} %collective-permute-done.14.refs_7_), channel_id=1, source_target_pairs={{0,2},{1,3},{2,0},{3,1},{4,6},{5,7},{6,4},{7,5},{8,10},{9,11},{10,... | collective-permute-start | bytes 1572872 | tf_op jit(solution)/shard_map/ppermute | solution.py:27
  71.7 17.5 %collective-permute-start.15 = (bf16[64,4096]{1,0:T(8,128)(2,1)}, bf16[64,4096]{1,0:T(8,128)(2,1)S(1)}, u32[]{:S(2)}, u32[]{:S(2)}) collective-permute-start(bf16[64,4096]{1,0:T(8,128)(2,1)} %collective-permute-done.3.refs_3_.refs_4_), channel_id=1, source_target_pairs={{0,16},{1,17},{2,18},{3,19},{4,20},{5,21},{6,22},{7,23},{8,24},{9,... | collective-permute-start | bytes 1572872 | tf_op jit(solution)/shard_map/ppermute | solution.py:27
  71.9 17.2 %collective-permute-start.16 = (bf16[64,4096]{1,0:T(8,128)(2,1)}, bf16[64,4096]{1,0:T(8,128)(2,1)S(1)}, u32[]{:S(2)}, u32[]{:S(2)}) collective-permute-start(bf16[64,4096]{1,0:T(8,128)(2,1)} %collective-permute-done.3.refs_3_.refs_4_), channel_id=1, source_target_pairs={{0,48},{1,49},{2,50},{3,51},{4,52},{5,53},{6,54},{7,55},{8,56},{9,... | collective-permute-start | bytes 1572872 | tf_op jit(solution)/shard_map/ppermute | solution.py:27
  73.7 15.4 %collective-permute-start.20 = (s16[544,256]{1,0:T(8,128)(2,1)}, s16[544,256]{1,0:T(8,128)(2,1)S(1)}, u32[]{:S(2)}, u32[]{:S(2)}) collective-permute-start(s16[544,256]{1,0:T(8,128)(2,1)} %get-tuple-element.61), channel_id=1, source_target_pairs={{0,1},{1,0},{2,3},{3,2},{4,5},{5,4},{6,7},{7,6},{8,9},{9,8},{10,11... | collective-permute-start | bytes 835592 | tf_op jit(solution)/shard_map/ppermute | solution.py:27
  89.1 15.8 %collective-permute-start.21 = (s16[272,256]{1,0:T(8,128)(2,1)}, s16[272,256]{1,0:T(8,128)(2,1)S(1)}, u32[]{:S(2)}, u32[]{:S(2)}) collective-permute-start(s16[272,256]{1,0:T(8,128)(2,1)} %get-tuple-element.63), channel_id=1, source_target_pairs={{0,1},{1,0},{2,3},{3,2},{4,5},{5,4},{6,7},{7,6},{8,9},{9,8},{10,11... | collective-permute-start | bytes 417800 | tf_op jit(solution)/shard_map/ppermute | solution.py:27
  104.8 15.3 %collective-permute-start.23 = (s16[544,256]{1,0:T(8,128)(2,1)S(1)}, s16[544,256]{1,0:T(8,128)(2,1)S(1)}, u32[]{:S(2)}, u32[]{:S(2)}) collective-permute-start(s16[544,256]{1,0:T(8,128)(2,1)S(1)} %get-tuple-element.75), channel_id=1, source_target_pairs={{0,1},{1,0},{2,3},{3,2},{4,5},{5,4},{6,7},{7,6},{8,9},{9,8},{10,11... | collective-permute-start | bytes 835592 | tf_op jit(solution)/shard_map/ppermute | solution.py:27
  106.1 6.6 %collective-permute-start.22 = (s16[256,256]{1,0:T(8,128)(2,1)S(1)}, s16[256,256]{1,0:T(8,128)(2,1)S(1)}, u32[]{:S(2)}, u32[]{:S(2)}) collective-permute-start(s16[256,256]{1,0:T(8,128)(2,1)S(1)} %shard_map.58), channel_id=1, source_target_pairs={{0,32},{1,33},{2,34},{3,35},{4,36},{5,37},{6,38},{7,39},{8,40},{9,... | collective-permute-start | bytes 393224 | tf_op jit(solution)/shard_map/ppermute | solution.py:27
  (19 other events, 221.9 us)

commit v6 on v5

--- a/solution.py
+++ b/solution.py
@@ -122,7 +122,7 @@
     return jnp.sqrt(square - mean * mean + EPS)
 
 
-def tile_kernel(cells, chunks, count, pieces, parts, first, export, at, *refs):
+def tile_kernel(cells, chunks, pieces, parts, first, export, at, *refs):
     refs = list(refs)
     blocks = [refs.pop(0) for _ in range(pieces)]
     rows = [refs.pop(0) for _ in range(1 + parts[-1][0] if parts else 1)]
@@ -134,13 +134,13 @@
     cbuf, acc, sems = refs[:3]
     half = own.shape[0]
     width = cells // chunks
-    block_at = [pl.ds(pl.multiple_of(at[1 + i] * 32, 64), 64) for i in range(pieces)]
+    block_at = [pl.ds(64 * i, 64) for i in range(pieces)]
 
     def copies(k):
         cells_k = pl.ds(width * k, width)
         pairs = [(p.at[:, cells_k], cbuf.at[span, cells_k]) for p, span in zip(blocks, block_at)]
         for i, (ref, start, size) in enumerate(parts):
-            span = pl.ds(pl.multiple_of(at[1 + pieces + i] * 32, 32), size)
+            span = pl.ds(pl.multiple_of(at[1 + i] * 32, 32), size)
             pairs.append((rows[ref].at[pl.ds(start, size), cells_k], rbuf.at[span, cells_k]))
         made = [pltpu.make_async_copy(*pair, sems.at[k, i]) for i, pair in enumerate(pairs)]
         for copy in made:
@@ -151,10 +151,9 @@
     if not parts:
         for p, span in zip(blocks, block_at):
             cbuf[span, :] = p[...]
-    if pieces < 4 * count:
-        for t in range(count):
-            span = pl.ds(pl.multiple_of(at[1 + pieces + len(parts) + t] * 32, 64), 64)
-            cbuf[span, :] = jnp.zeros((64, cells), cbuf.dtype)
+    used = 64 * pieces
+    if used < cbuf.shape[0]:
+        cbuf[used:, :] = jnp.zeros((cbuf.shape[0] - used, cells), cbuf.dtype)
     total = sums = squares = row_sums = row_squares = 0.0
     for k in range(chunks):
         for copy in flight[k]:
@@ -192,20 +191,14 @@
         mean = lane_sums(rs[pl.ds(other, half), :]) * scale
         dev = deviation(lane_sums(rq[pl.ds(other, half), :]) * scale, mean)
         extra = [*split(mean), *split(dev)]
-    means, devs = lane_sums(sums) * scale, lane_sums(squares) * scale
-    devs = deviation(devs, means)
-    for t in range(count):
-        span = slice(256 * t, 256 * t + 256)
-        mean, dev = means[:, span], devs[:, span]
-        row = lax.broadcasted_iota(jnp.int32, (8, 256), 0)
-        cst[8 * t : 8 * t + 8, :] = jnp.where(row == 0, mean, dev)
-        cov = acc[pl.ds(other, half), span] * scale - rst[pl.ds(other, half), 0:1] * mean
-        base = (half + 16) * t
-        msg[base : base + half, :] = encode(
-            cov * ((1.0 / rst[pl.ds(other, half), 1:2]) * (1.0 / dev))
-        )
-        msg[base + half : base + half + 16, :] = pack([*split(mean), *split(dev), *extra])
-        own[:, span] = acc[pl.ds(mine, half), span] * scale - rst[pl.ds(mine, half), 0:1] * mean
+    mean = lane_sums(sums) * scale
+    dev = deviation(lane_sums(squares) * scale, mean)
+    row = lax.broadcasted_iota(jnp.int32, cst.shape, 0)
+    cst[...] = jnp.where(row == 0, mean, dev)
+    cov = acc[pl.ds(other, half), :] * scale - rst[pl.ds(other, half), 0:1] * mean
+    msg[0:half, :] = encode(cov * ((1.0 / rst[pl.ds(other, half), 1:2]) * (1.0 / dev)))
+    msg[half:, :] = pack([*split(mean), *split(dev), *extra])
+    own[...] = acc[pl.ds(mine, half), :] * scale - rst[pl.ds(mine, half), 0:1] * mean
     if export:
         out.wait()
 
@@ -237,21 +230,17 @@
     )(table, *args)
 
 
-def tiles(rows, sets, rstat, at, empty=False, export=False):
+def tiles(rows, pieces, rstat, at, export=False, limit=None):
     rows, parts = rows
     n, cells = sum(part.shape[0] for part in rows), rows[0].shape[1]
-    half, count, first, chunks = n // 2, len(sets), rstat is None, 4
-    pieces = [p for s in sets for p in s]
-    outs = [
-        ((half, 256 * count), jnp.float32),
-        (((half + 16) * count, 256), jnp.int16),
-        ((8 * count, 256), jnp.float32),
-    ]
+    half, first, chunks = n // 2, rstat is None, 4
+    wide = -(-len(pieces) // 2) * 128
+    outs = [((half, wide), jnp.float32), ((half + 16, wide), jnp.int16), ((8, wide), jnp.float32)]
     out_places = [VMEM] * 3
     scratch = [pltpu.VMEM((n, cells), jnp.bfloat16)] if parts else []
     scratch += [
-        pltpu.VMEM((256 * count, cells), jnp.bfloat16),
-        pltpu.VMEM((n, 256 * count), jnp.float32),
+        pltpu.VMEM((wide, cells), jnp.bfloat16),
+        pltpu.VMEM((n, wide), jnp.float32),
         pltpu.SemaphoreType.DMA((chunks, len(pieces) + len(parts))),
     ]
     if first:
@@ -262,17 +251,17 @@
         outs.append(((n, cells), jnp.bfloat16))
         out_places.append(HBM)
     return call(
-        functools.partial(tile_kernel, cells, chunks, count, len(pieces), parts, first, export),
+        functools.partial(tile_kernel, cells, chunks, len(pieces), parts, first, export),
         outs,
         scratch,
-        int(1.15e9 * (2.5 + 1.5 * count + (3.5 if parts else 0))),
+        int(1.15e9 * (2.5 + wide / 170 + (3.5 if parts else 0))),
         at,
         *pieces,
         *rows,
         *([] if first else [rstat]),
         places=[HBM if parts else VMEM] * (len(rows) + len(pieces)) + ([] if first else [VMEM]),
         out_places=out_places,
-        limit=VMEM_LIMIT if parts else 32 * 1024 * 1024,
+        limit=limit or (VMEM_LIMIT if parts else 32 * 1024 * 1024),
     )
 
 
@@ -315,78 +304,74 @@
 
 def final_kernel(groups, at, rst, back, *refs):
     out = refs[-1]
-    slot = lax.broadcasted_iota(jnp.int32, (1, 256), 1) // 64
     half = back.shape[0]
-    rows = half + 16
-    factors = row_factors(rst, refs[1][half:rows, :], at[0])
+    factors = row_factors(rst, refs[1][half:, :], at[0])
     far_all = decode(back[...])
+    lane = lax.broadcasted_iota(jnp.int32, (1, 128), 1) // 64
     for g, ids in enumerate(groups):
         own, msg, cst = refs[3 * g : 3 * g + 3]
+        values = joined(own[...], msg[...], cst[...], factors)
         for t, k in enumerate(ids):
-            value = joined(
-                own[:, 256 * t : 256 * t + 256],
-                msg[rows * t : rows * t + rows, :],
-                cst[8 * t : 8 * t + 8, :],
-                factors,
-            )
-            piece = far_all[:, 64 * k : 64 * k + 64]
-            far = jnp.concatenate([piece] * 4, axis=1)
-            value = jnp.where(slot == at[1], far, value)
-            out[:, at[2 + k] * 2, :] = value[:, 0:128]
-            out[:, at[2 + k] * 2 + 1, :] = value[:, 128:256]
+            blocks = [values[:, 192 * t + 64 * i : 192 * t + 64 * i + 64] for i in range(3)]
+            blocks.append(far_all[:, 64 * k : 64 * k + 64])
+            twice = [jnp.concatenate([block, block], axis=1) for block in blocks]
+            for i in range(2):
+                which = (lane + (2 * i + 1 + NY - at[1])) % NY
+                value = twice[3]
+                for source in range(3):
+                    value = jnp.where(which == source, twice[source], value)
+                out[:, at[2 + k] * 2 + i, :] = value
 
 
 def local(counts, size_factors, gene_means, dispersions, block_order):
     zl, y, x, c, h = [lax.axis_index(axis) for axis in AXES]
     hold = lax.optimization_barrier
     up, down = {}, {}
-    near, last = [(y - 1) % NY * 2, y * 2, (y + 1) % NY * 2], (y + 2) % NY * 2
     place = lambda at, core: 2 * (NC * (at % NX) + core)
-    row_places = [place(i, core) for core in (c, 1 - c) for i in range(NX)]
     lists = [
-        [h, *near, *[8 + i for i in near]] + row_places + [last, 8 + last],
-        [h, *near, *[8 + i for i in near], last, 8 + last],
-        [h, *[2 * k for k in range(NZ)]]
-        + [place(x + d, core) for core in (c, 1 - c) for d in (0, -1, 1, 2)],
-        [h, (y + 2) % NY] + [(zl - k) % NZ for k in range(NZ)],
+        [h] + [place(i, core) for core in (c, 1 - c) for i in range(NX)],
+        [h] + [place(x + d, core) for core in (c, 1 - c) for d in (0, -1, 1, 2)],
+        [h, y] + [(zl - k) % NZ for k in range(NZ)],
     ]
     table = jnp.stack([jnp.asarray(v, jnp.int32) for values in lists for v in values])
     starts = np.cumsum([0] + [len(values) for values in lists]).tolist()
-    at_one, at_two, at_far, at_end = [(table, start) for start in starts[:4]]
 
     a, copies = residuals(counts, size_factors, gene_means, dispersions, block_order)
 
-    up[0], down[0], z1, far = move(a, y=1), move(a, y=-1), move(a, z=1), move(a, y=2)
-    z3 = move(a, z=3)
+    far, z1 = move(a, y=2), move(a, z=1)
     rows = spread_x(copies)
-    up[0], down[0], z1, z3, far = hold((up[0], down[0], z1, z3, far))
-
-    up[1], down[1], z2 = move(z1, y=1), move(z1, y=-1), move(z1, z=1)
-    far, far_c = hold((far, move(far, core=1)))
+    a, far, z1, table = hold((a, far, z1, table))
+    at_near, at_far, at_end = [(table, start) for start in starts[:3]]
+
+    up[0], down[0], z2 = move(a, y=1), move(a, y=-1), move(z1, z=1)
     right, left = move(far, x=1), move(far, x=-1)
-    rows, z2, up[1], down[1], right, left = hold((rows, z2, up[1], down[1], right, left))
-
-    pieces = lambda k: (up[k], z[k], down[k])
+    a, rows, z2, up[0], down[0], right, left = hold((a, rows, z2, up[0], down[0], right, left))
+
+    pieces = lambda k: [up[k], z[k], down[k]]
+    up[1], down[1], z3 = move(z1, y=1), move(z1, y=-1), move(a, z=3)
+    z = [a, z1, z2, z3]
+    across, rows_c = move(far, x=2), move(rows, core=1)
+    rows = (rows, rows_c), [(i // NX, 64 * (i % NX), 64) for i in range(2 * NX)]
+    own0, msg0, cst0, rstat, ordered = tiles(rows, pieces(0) + [a], None, at_near, True)
+    z3, up[1], down[1], far, right, left, across, own0 = hold(
+        (z3, up[1], down[1], far, right, left, across, own0)
+    )
+
+    z = [a, z1, z2, z3]
     up[2], down[2] = move(z2, y=1), move(z2, y=-1)
-    z = [a, z1, z2, z3]
-    rows_c = move(rows, core=1)
-    across = move(far, x=2)
-    rows = (rows, rows_c), [(i // NX, 64 * (i % NX), 64) for i in range(2 * NX)]
-    own01, msg01, cst01, rstat, ordered = tiles(
-        rows, [pieces(0), pieces(1)], None, at_one, True, True
-    )
-    z3, up[2], down[2], own01, across = hold((z3, up[2], down[2], own01, across))
+    far = jnp.concatenate([far, right, left, across], axis=0)
+    far_c = move(far, core=1)
+    msg0 = move(msg0, cell=1)
+    own1, msg1, cst1 = tiles(rows, pieces(1), rstat, at_near)
+    z3, up[2], down[2], msg0, own1, far, far_c = hold((z3, up[2], down[2], msg0, own1, far, far_c))
 
     z = [a, z1, z2, z3]
     up[3], down[3] = move(z3, y=1), move(z3, y=-1)
-    across_c, right_c, left_c = move(across, core=1), move(right, core=1), move(left, core=1)
-    msg01 = move(msg01, cell=1)
-    far = [far, right, left, across, far_c, right_c, left_c, across_c]
-    far = far, [(i, 0, part.shape[0]) for i, part in enumerate(far)]
-    ownf, msgf, cstf, fstat = tiles(far, [z], None, at_far)
-    up[3], down[3], ownf, msg01 = hold((up[3], down[3], ownf, msg01))
+    msg1 = move(msg1, cell=1)
+    ownf, msgf, cstf, fstat = tiles(((far, far_c), rows[1]), z, None, at_far, limit=48 * 1024 * 1024)
+    up[3], down[3], ownf = hold((up[3], down[3], ownf))
     msgf = move(msgf, cell=1)
-    own23, msg23, cst23 = tiles(([ordered], []), [pieces(2), pieces(3)], rstat, at_two, True)
+    own23, msg23, cst23 = tiles(([ordered], []), pieces(2) + pieces(3), rstat, at_near)
     msg23 = move(msg23, cell=1)
 
     half = ownf.shape[0]
@@ -396,12 +381,12 @@
     back = move(back, y=2)
 
     (result,) = call(
-        functools.partial(final_kernel, ((0, 1), (2, 3))),
+        functools.partial(final_kernel, ((0,), (1,), (2, 3))),
         [((half, 8, 128), jnp.float32)],
         [],
         1 << 24,
         at_end,
-        *(rstat, back, own01, msg01, cst01, own23, msg23, cst23),
+        *(rstat, back, own0, msg0, cst0, own1, msg1, cst1, own23, msg23, cst23),
     )
     return result.reshape(half, 1, 1024)
 

time: 125 us -> 123 us (0.984)
  the two profiles are of different devices: /device:TPU:26 before, /device:TPU:32 now
where the time goes in v6:
time: 123 us
  starting transfers between devices  48.7 us (40%)
  waiting for transfers between devices  35.8 us (29%)
  Pallas kernels  34.2 us (28%)
  local copies, waits for them, and re-layouts  3.81 us (3%)
    ppermute x22, starting transfers between devices, move(): return lax.ppermute(value, AXES, pairs)  44.1 us
    ppermute x22, waiting for transfers between devices, move(): return lax.ppermute(value, AXES, pairs)  35.8 us
    pallas_call x6, Pallas kernels, call(): pl.pallas_call(lambda table, *refs: kernel(From(table, first), *refs), in...  30.8 us
    all_to_all x1, starting transfers between devices, spread_x(): return lax.all_to_all(copies, 'x', 0, 0, tiled=True)  4.58 us
    pallas_call x1, Pallas kernels, residuals(): pl.pallas_call(functools.partial(resid_kernel, math.sqrt(cells * NH)), in...  3.36 us
    unnamed x43, local copies, waits for them, and re-layouts  3.12 us
  transfers between devices with their start and end apart: 23, of which 10 were waited for; matrix products, arithmetic and copies ran while one was open for 1% of the time, Pallas kernels for 22%

profile of v6, /device:TPU:32, one launch (start us, length us, event | category | flops | bytes accessed | tf_op | source)
XLA Modules:
  0.0 122.8 jit_solution(14109455865701040526)
XLA Ops:
  0.0 3.4 %shard_map.55 = (bf16[64,4096]{1,0:T(8,128)(2,1)}, bf16[256,4096]{1,0:T(8,128)(2,1)}) custom-call(s32[1]{0:T(128)} %bitcast.place, s32[128]{0:T(128)} %order.1, s32[64,4096]{1,0:T(8,128)} %counts.1, f32[1,4096]{1,0:T(1,128)} %bitcast.32, f32[64,128]{1,0:T(8,128)} %bitcast.30, f32[64,128]{1,0:T(8,128)} %bitcast.31), custom_call_target="tpu_custom_call" | custom-call | tf_op jit(solution)/shard_map/pallas_call | solution.py:59
  3.4 4.6 %all-to-all-start = ((bf16[4,64,4096]{2,1,0:T(8,128)(2,1)}), bf16[4,64,4096]{2,1,0:T(8,128)(2,1)}, u32[]{:S(2)}, u32[]{:S(2)}) async-start(bf16[4,64,4096]{2,1,0:T(8,128)(2,1)} %bitcast.29), calls=%async_computation | async-start | bytes 4194304 | tf_op jit(solution)/shard_map/all_to_all | solution.py:31
  8.0 3.3 %collective-permute-start = (bf16[64,4096]{1,0:T(8,128)(2,1)S(1)}, bf16[64,4096]{1,0:T(8,128)(2,1)S(1)}, u32[]{:S(2)}, u32[]{:S(2)}) collective-permute-start(bf16[64,4096]{1,0:T(8,128)(2,1)S(1)} %copy-done.6), channel_id=1, source_target_pairs={{0,32},{1,33},{2,34},{3,35},{4,36},{5,37},{6,38},{7,39},{8,40},{9,... | collective-permute-start | bytes 1572872 | tf_op jit(solution)/shard_map/ppermute | solution.py:27
  11.3 1.9 %collective-permute-start.1 = (bf16[64,4096]{1,0:T(8,128)(2,1)S(1)}, bf16[64,4096]{1,0:T(8,128)(2,1)S(1)}, u32[]{:S(2)}, u32[]{:S(2)}) collective-permute-start(bf16[64,4096]{1,0:T(8,128)(2,1)S(1)} %copy-done.6), channel_id=1, source_target_pairs={{0,64},{1,65},{2,66},{3,67},{4,68},{5,69},{6,70},{7,71},{8,72},{9,... | collective-permute-start | bytes 1572872 | tf_op jit(solution)/shard_map/ppermute | solution.py:27
  13.8 9.4 %collective-permute-done = bf16[64,4096]{1,0:T(8,128)(2,1)S(1)} collective-permute-done((bf16[64,4096]{1,0:T(8,128)(2,1)S(1)}, bf16[64,4096]{1,0:T(8,128)(2,1)S(1)}, u32[]{:S(2)}, u32[]{:S(2)}) %collective-permute-start) | collective-permute-done | bytes 524320 | tf_op jit(solution)/shard_map/ppermute | solution.py:27
  24.6 1.9 %collective-permute-start.2 = (bf16[64,4096]{1,0:T(8,128)(2,1)S(1)}, bf16[64,4096]{1,0:T(8,128)(2,1)S(1)}, u32[]{:S(2)}, u32[]{:S(2)}) collective-permute-start(bf16[64,4096]{1,0:T(8,128)(2,1)S(1)} %collective-permute-done.1.refs_1_), channel_id=1, source_target_pairs={{0,64},{1,65},{2,66},{3,67},{4,68},{5,69},{6,70},{7,71},{8,72},{9,... | collective-permute-start | bytes 1572872 | tf_op jit(solution)/shard_map/ppermute | solution.py:27
  27.2 2.6 %collective-permute-start.4 = (bf16[64,4096]{1,0:T(8,128)(2,1)S(1)}, bf16[64,4096]{1,0:T(8,128)(2,1)S(1)}, u32[]{:S(2)}, u32[]{:S(2)}) collective-permute-start(bf16[64,4096]{1,0:T(8,128)(2,1)S(1)} %copy-done.6), channel_id=1, source_target_pairs={{0,48},{1,49},{2,50},{3,51},{4,52},{5,53},{6,54},{7,55},{8,56},{9,... | collective-permute-start | bytes 1572872 | tf_op jit(solution)/shard_map/ppermute | solution.py:27
  33.0 5.8 %collective-permute-done.2.refs_2_.refs_1_ = bf16[64,4096]{1,0:T(8,128)(2,1)S(1)} collective-permute-done((bf16[64,4096]{1,0:T(8,128)(2,1)S(1)}, bf16[64,4096]{1,0:T(8,128)(2,1)S(1)}, u32[]{:S(2)}, u32[]{:S(2)}) %collective-permute-start.2) | collective-permute-done | bytes 524320 | tf_op jit(solution)/shard_map/ppermute | solution.py:27
  40.1 5.7 %collective-permute-done.5 = bf16[64,4096]{1,0:T(8,128)(2,1)S(1)} collective-permute-done((bf16[64,4096]{1,0:T(8,128)(2,1)S(1)}, bf16[64,4096]{1,0:T(8,128)(2,1)S(1)}, u32[]{:S(2)}, u32[]{:S(2)}) %collective-permute-start.5) | collective-permute-done | bytes 524320 | tf_op jit(solution)/shard_map/ppermute | solution.py:27
  50.4 7.8 %shard_map.56 = (f32[256,256]{1,0:T(8,128)}, s16[272,256]{1,0:T(8,128)(2,1)}, f32[8,256]{1,0:T(8,128)}, f32[512,128]{1,0:T(8,128)}, bf16[512,4096]{1,0:T(8,128)(2,1)}) custom-call(s32[24]{0:T(128)} %stack.93.table, bf16[64,4096]{1,0:T(8,128)(2,1)} %copy-done.17, bf16[64,4096]{1,0:T(8,128)(2,1)} %get-tuple-element.58.refs_1_.refs_3_.refs_0_, ...), custom_call_target="tpu_custom_call" | custom-call | flops 8631764992 | bytes 1048576 | tf_op jit(solution)/shard_map/pallas_call | solution.py:222
  58.3 3.3 %collective-permute-done.9.refs_0_ = bf16[64,4096]{1,0:T(8,128)(2,1)} collective-permute-done((bf16[64,4096]{1,0:T(8,128)(2,1)S(1)}, bf16[64,4096]{1,0:T(8,128)(2,1)}, u32[]{:S(2)}, u32[]{:S(2)}) %collective-permute-start.9) | collective-permute-done | bytes 524320 | tf_op jit(solution)/shard_map/ppermute | solution.py:27
  61.6 2.8 %collective-permute-done.11 = bf16[64,4096]{1,0:T(8,128)(2,1)S(1)} collective-permute-done((bf16[64,4096]{1,0:T(8,128)(2,1)S(1)}, bf16[64,4096]{1,0:T(8,128)(2,1)S(1)}, u32[]{:S(2)}, u32[]{:S(2)}) %collective-permute-start.11) | collective-permute-done | bytes 524320 | tf_op jit(solution)/shard_map/ppermute | solution.py:27
  68.1 2.9 %collective-permute-start.13 = (bf16[64,4096]{1,0:T(8,128)(2,1)S(1)}, bf16[64,4096]{1,0:T(8,128)(2,1)}, u32[]{:S(2)}, u32[]{:S(2)}) collective-permute-start(bf16[64,4096]{1,0:T(8,128)(2,1)S(1)} %collective-permute-done.2.refs_2_.refs_1_), channel_id=1, source_target_pairs={{0,48},{1,49},{2,50},{3,51},{4,52},{5,53},{6,54},{7,55},{8,56},{9,... | collective-permute-start | bytes 1572872 | tf_op jit(solution)/shard_map/ppermute | solution.py:27
  71.0 6.3 %collective-permute-start.14 = (s16[272,256]{1,0:T(8,128)(2,1)S(1)}, s16[272,256]{1,0:T(8,128)(2,1)S(1)}, u32[]{:S(2)}, u32[]{:S(2)}) collective-permute-start(s16[272,256]{1,0:T(8,128)(2,1)S(1)} %copy-done.19), channel_id=1, source_target_pairs={{0,1},{1,0},{2,3},{3,2},{4,5},{5,4},{6,7},{7,6},{8,9},{9,8},{10,11... | collective-permute-start | bytes 417800 | tf_op jit(solution)/shard_map/ppermute | solution.py:27
  77.3 6.7 %shard_map.57 = (f32[256,256]{1,0:T(8,128)}, s16[272,256]{1,0:T(8,128)(2,1)}, f32[8,256]{1,0:T(8,128)}) custom-call(s32[24]{0:T(128)} %stack.93.table, bf16[64,4096]{1,0:T(8,128)(2,1)} %collective-permute-done.9.refs_0_, bf16[64,4096]{1,0:T(8,128)(2,1)} %copy-done.8, bf16[64,4096]{1,0:T(8,128)(2,1)} %collective-permute-done.10.refs_2_, ...), custom_call_target="tpu_custom_call" | custom-call | flops 8631764992 | bytes 1048576 | tf_op jit(solution)/shard_map/pallas_call | solution.py:222
  84.2 3.2 %collective-permute-start.17 = (bf16[64,4096]{1,0:T(8,128)(2,1)}, bf16[64,4096]{1,0:T(8,128)(2,1)S(1)}, u32[]{:S(2)}, u32[]{:S(2)}) collective-permute-start(bf16[64,4096]{1,0:T(8,128)(2,1)} %collective-permute-done.8.refs_3_.refs_4_), channel_id=1, source_target_pairs={{0,48},{1,49},{2,50},{3,51},{4,52},{5,53},{6,54},{7,55},{8,56},{9,... | collective-permute-start | bytes 1572872 | tf_op jit(solution)/shard_map/ppermute | solution.py:27
  87.5 7.0 %shard_map.58 = (f32[256,256]{1,0:T(8,128)S(1)}, s16[272,256]{1,0:T(8,128)(2,1)S(1)}, f32[8,256]{1,0:T(8,128)S(1)}, f32[512,128]{1,0:T(8,128)S(1)}) custom-call(s32[24]{0:T(128)S(1)} %copy-done.5, bf16[64,4096]{1,0:T(8,128)(2,1)S(1)} %copy-done.7, bf16[64,4096]{1,0:T(8,128)(2,1)S(1)} %copy-done.9, ...), custom_call_target="tpu_custom_call" | custom-call | flops 8631764992 | bytes 1048576 | tf_op jit(solution)/shard_map/pallas_call | solution.py:222
  94.5 6.0 %collective-permute-start.18 = (s16[272,256]{1,0:T(8,128)(2,1)S(1)}, s16[272,256]{1,0:T(8,128)(2,1)S(1)}, u32[]{:S(2)}, u32[]{:S(2)}) collective-permute-start(s16[272,256]{1,0:T(8,128)(2,1)S(1)} %get-tuple-element.80), channel_id=1, source_target_pairs={{0,1},{1,0},{2,3},{3,2},{4,5},{5,4},{6,7},{7,6},{8,9},{9,8},{10,11... | collective-permute-start | bytes 417800 | tf_op jit(solution)/shard_map/ppermute | solution.py:27
  100.5 4.9 %shard_map.60 = (f32[256,384]{1,0:T(8,128)S(1)}, s16[272,384]{1,0:T(8,128)(2,1)S(1)}, f32[8,384]{1,0:T(8,128)S(1)}) custom-call(s32[24]{0:T(128)S(1)} %copy-done.5, bf16[64,4096]{1,0:T(8,128)(2,1)} %collective-permute-done.12.refs_0_, bf16[64,4096]{1,0:T(8,128)(2,1)S(1)} %collective-permute-done.2.refs_2_.refs_1_, ...), custom_call_target="tpu_custom_call" | custom-call | flops 5472647168 | bytes 1048576 | tf_op jit(solution)/shard_map/pallas_call | solution.py:222
  105.4 4.3 %collective-permute-start.21 = (s16[272,384]{1,0:T(8,128)(2,1)S(1)}, s16[272,384]{1,0:T(8,128)(2,1)S(1)}, u32[]{:S(2)}, u32[]{:S(2)}) collective-permute-start(s16[272,384]{1,0:T(8,128)(2,1)S(1)} %get-tuple-element.95), channel_id=1, source_target_pairs={{0,1},{1,0},{2,3},{3,2},{4,5},{5,4},{6,7},{7,6},{8,9},{9,8},{10,11... | collective-permute-start | bytes 626696 | tf_op jit(solution)/shard_map/ppermute | solution.py:27
  110.8 2.6 %collective-permute-start.19 = (s16[256,256]{1,0:T(8,128)(2,1)S(1)}, s16[256,256]{1,0:T(8,128)(2,1)S(1)}, u32[]{:S(2)}, u32[]{:S(2)}) collective-permute-start(s16[256,256]{1,0:T(8,128)(2,1)S(1)} %shard_map.59), channel_id=1, source_target_pairs={{0,32},{1,33},{2,34},{3,35},{4,36},{5,37},{6,38},{7,39},{8,40},{9,... | collective-permute-start | bytes 393224 | tf_op jit(solution)/shard_map/ppermute | solution.py:27
  113.4 3.9 %collective-permute-done.19.refs_1_ = s16[256,256]{1,0:T(8,128)(2,1)S(1)} collective-permute-done((s16[256,256]{1,0:T(8,128)(2,1)S(1)}, s16[256,256]{1,0:T(8,128)(2,1)S(1)}, u32[]{:S(2)}, u32[]{:S(2)}) %collective-permute-start.19) | collective-permute-done | bytes 131104 | tf_op jit(solution)/shard_map/ppermute | solution.py:27
  117.4 2.0 %collective-permute-done.21.refs_9_ = s16[272,384]{1,0:T(8,128)(2,1)S(1)} collective-permute-done((s16[272,384]{1,0:T(8,128)(2,1)S(1)}, s16[272,384]{1,0:T(8,128)(2,1)S(1)}, u32[]{:S(2)}, u32[]{:S(2)}) %collective-permute-start.21) | collective-permute-done | bytes 208928 | tf_op jit(solution)/shard_map/ppermute | solution.py:27
  119.4 3.4 %shard_map.61 = f32[256,8,128]{2,1,0:T(8,128)} custom-call(s32[24]{0:T(128)S(1)} %copy-done.5, f32[512,128]{1,0:T(8,128)S(1)} %copy-done.1, s16[256,256]{1,0:T(8,128)(2,1)S(1)} %collective-permute-done.19.refs_1_, f32[256,256]{1,0:T(8,128)S(1)} %copy-done, s16[272,256]{1,0:T(8,128)(2,1)S(1)} %collective-permute-done.14.refs_3_, f32[8,256]{1,0:T(8,128)S(1)} %copy-done.3, ...), custom_call_target="tpu_custom_call" | custom-call | flops 16777216 | bytes 1048576 | tf_op jit(solution)/shard_map/pallas_call | solution.py:222
  (74 shorter events, 16.8 us)
Async XLA Ops:
  3.4 42.4 %all-to-all-start = ((bf16[4,64,4096]{2,1,0:T(8,128)(2,1)}), bf16[4,64,4096]{2,1,0:T(8,128)(2,1)}, u32[]{:S(2)}, u32[]{:S(2)}) async-start(bf16[4,64,4096]{2,1,0:T(8,128)(2,1)} %bitcast.29), calls=%async_computation | async-start | bytes 4194304 | tf_op jit(solution)/shard_map/all_to_all | solution.py:31
  8.0 15.3 %collective-permute-start = (bf16[64,4096]{1,0:T(8,128)(2,1)S(1)}, bf16[64,4096]{1,0:T(8,128)(2,1)S(1)}, u32[]{:S(2)}, u32[]{:S(2)}) collective-permute-start(bf16[64,4096]{1,0:T(8,128)(2,1)S(1)} %copy-done.6), channel_id=1, source_target_pairs={{0,32},{1,33},{2,34},{3,35},{4,36},{5,37},{6,38},{7,39},{8,40},{9,... | collective-permute-start | bytes 1572872 | tf_op jit(solution)/shard_map/ppermute | solution.py:27
  11.3 13.4 %collective-permute-start.1 = (bf16[64,4096]{1,0:T(8,128)(2,1)S(1)}, bf16[64,4096]{1,0:T(8,128)(2,1)S(1)}, u32[]{:S(2)}, u32[]{:S(2)}) collective-permute-start(bf16[64,4096]{1,0:T(8,128)(2,1)S(1)} %copy-done.6), channel_id=1, source_target_pairs={{0,64},{1,65},{2,66},{3,67},{4,68},{5,69},{6,70},{7,71},{8,72},{9,... | collective-permute-start | bytes 1572872 | tf_op jit(solution)/shard_map/ppermute | solution.py:27
  23.2 35.0 %copy-start.11 = (bf16[64,4096]{1,0:T(8,128)(2,1)}, bf16[64,4096]{1,0:T(8,128)(2,1)S(1)}, u32[]{:S(2)}) copy-start(bf16[64,4096]{1,0:T(8,128)(2,1)S(1)} %collective-permute-done) | copy-start | bytes 1572868
  24.6 14.1 %collective-permute-start.2 = (bf16[64,4096]{1,0:T(8,128)(2,1)S(1)}, bf16[64,4096]{1,0:T(8,128)(2,1)S(1)}, u32[]{:S(2)}, u32[]{:S(2)}) collective-permute-start(bf16[64,4096]{1,0:T(8,128)(2,1)S(1)} %collective-permute-done.1.refs_1_), channel_id=1, source_target_pairs={{0,64},{1,65},{2,66},{3,67},{4,68},{5,69},{6,70},{7,71},{8,72},{9,... | collective-permute-start | bytes 1572872 | tf_op jit(solution)/shard_map/ppermute | solution.py:27
  26.6 13.5 %collective-permute-start.3 = (bf16[64,4096]{1,0:T(8,128)(2,1)S(1)}, bf16[64,4096]{1,0:T(8,128)(2,1)S(1)}, u32[]{:S(2)}, u32[]{:S(2)}) collective-permute-start(bf16[64,4096]{1,0:T(8,128)(2,1)S(1)} %copy-done.6), channel_id=1, source_target_pairs={{0,16},{1,17},{2,18},{3,19},{4,20},{5,21},{6,22},{7,23},{8,24},{9,... | collective-permute-start | bytes 1572872 | tf_op jit(solution)/shard_map/ppermute | solution.py:27
  27.2 12.8 %collective-permute-start.4 = (bf16[64,4096]{1,0:T(8,128)(2,1)S(1)}, bf16[64,4096]{1,0:T(8,128)(2,1)S(1)}, u32[]{:S(2)}, u32[]{:S(2)}) collective-permute-start(bf16[64,4096]{1,0:T(8,128)(2,1)S(1)} %copy-done.6), channel_id=1, source_target_pairs={{0,48},{1,49},{2,50},{3,51},{4,52},{5,53},{6,54},{7,55},{8,56},{9,... | collective-permute-start | bytes 1572872 | tf_op jit(solution)/shard_map/ppermute | solution.py:27
  29.8 16.0 %collective-permute-start.5 = (bf16[64,4096]{1,0:T(8,128)(2,1)S(1)}, bf16[64,4096]{1,0:T(8,128)(2,1)S(1)}, u32[]{:S(2)}, u32[]{:S(2)}) collective-permute-start(bf16[64,4096]{1,0:T(8,128)(2,1)S(1)} %collective-permute-done), channel_id=1, source_target_pairs={{0,4},{1,5},{2,6},{3,7},{4,8},{5,9},{6,10},{7,11},{8,12},{9,13},{1... | collective-permute-start | bytes 1572872 | tf_op jit(solution)/shard_map/ppermute | solution.py:27
  31.4 14.4 %collective-permute-start.6 = (bf16[64,4096]{1,0:T(8,128)(2,1)S(1)}, bf16[64,4096]{1,0:T(8,128)(2,1)S(1)}, u32[]{:S(2)}, u32[]{:S(2)}) collective-permute-start(bf16[64,4096]{1,0:T(8,128)(2,1)S(1)} %collective-permute-done), channel_id=1, source_target_pairs={{0,12},{1,13},{2,14},{3,15},{4,0},{5,1},{6,2},{7,3},{8,4},{9,5},{1... | collective-permute-start | bytes 1572872 | tf_op jit(solution)/shard_map/ppermute | solution.py:27
  45.8 4.6 %collective-permute-start.7 = (bf16[256,4096]{1,0:T(8,128)(2,1)}, bf16[256,4096]{1,0:T(8,128)(2,1)}, u32[]{:S(2)}, u32[]{:S(2)}) collective-permute-start(bf16[256,4096]{1,0:T(8,128)(2,1)} %bitcast.27.refs_4_.refs_3_), channel_id=1, source_target_pairs={{0,2},{1,3},{2,0},{3,1},{4,6},{5,7},{6,4},{7,5},{8,10},{9,11},{10,... | collective-permute-start | bytes 6291464 | tf_op jit(solution)/shard_map/ppermute | solution.py:27
  45.9 15.7 %collective-permute-start.9 = (bf16[64,4096]{1,0:T(8,128)(2,1)S(1)}, bf16[64,4096]{1,0:T(8,128)(2,1)}, u32[]{:S(2)}, u32[]{:S(2)}) collective-permute-start(bf16[64,4096]{1,0:T(8,128)(2,1)S(1)} %collective-permute-done.1.refs_1_), channel_id=1, source_target_pairs={{0,16},{1,17},{2,18},{3,19},{4,20},{5,21},{6,22},{7,23},{8,24},{9,... | collective-permute-start | bytes 1572872 | tf_op jit(solution)/shard_map/ppermute | solution.py:27
  47.5 14.1 %collective-permute-start.10 = (bf16[64,4096]{1,0:T(8,128)(2,1)S(1)}, bf16[64,4096]{1,0:T(8,128)(2,1)}, u32[]{:S(2)}, u32[]{:S(2)}) collective-permute-start(bf16[64,4096]{1,0:T(8,128)(2,1)S(1)} %collective-permute-done.1.refs_1_), channel_id=1, source_target_pairs={{0,48},{1,49},{2,50},{3,51},{4,52},{5,53},{6,54},{7,55},{8,56},{9,... | collective-permute-start | bytes 1572872 | tf_op jit(solution)/shard_map/ppermute | solution.py:27
  49.2 15.3 %collective-permute-start.11 = (bf16[64,4096]{1,0:T(8,128)(2,1)S(1)}, bf16[64,4096]{1,0:T(8,128)(2,1)S(1)}, u32[]{:S(2)}, u32[]{:S(2)}) collective-permute-start(bf16[64,4096]{1,0:T(8,128)(2,1)S(1)} %collective-permute-done), channel_id=1, source_target_pairs={{0,8},{1,9},{2,10},{3,11},{4,12},{5,13},{6,14},{7,15},{8,0},{9,1},... | collective-permute-start | bytes 1572872 | tf_op jit(solution)/shard_map/ppermute | solution.py:27
  50.3 14.2 %collective-permute-start.8 = (bf16[64,4096]{1,0:T(8,128)(2,1)S(1)}, bf16[64,4096]{1,0:T(8,128)(2,1)}, u32[]{:S(2)}, u32[]{:S(2)}) collective-permute-start(bf16[64,4096]{1,0:T(8,128)(2,1)S(1)} %copy-done.6), channel_id=1, source_target_pairs={{0,192},{1,193},{2,194},{3,195},{4,196},{5,197},{6,198},{7,199},{8... | collective-permute-start | bytes 1572872 | tf_op jit(solution)/shard_map/ppermute | solution.py:27
  67.6 16.5 %collective-permute-start.15 = (bf16[256,4096]{1,0:T(8,128)(2,1)S(1)}, bf16[256,4096]{1,0:T(8,128)(2,1)}, u32[]{:S(2)}, u32[]{:S(2)}) collective-permute-start(bf16[256,4096]{1,0:T(8,128)(2,1)S(1)} %constant_dynamic-update-slice_fusion.refs_4_), channel_id=1, source_target_pairs={{0,2},{1,3},{2,0},{3,1},{4,6},{5,7},{6,4},{7,5},{8,10},{9,11},{10,... | collective-permute-start | bytes 6291464 | tf_op jit(solution)/shard_map/ppermute | solution.py:27
  67.7 16.4 %collective-permute-start.12 = (bf16[64,4096]{1,0:T(8,128)(2,1)S(1)}, bf16[64,4096]{1,0:T(8,128)(2,1)}, u32[]{:S(2)}, u32[]{:S(2)}) collective-permute-start(bf16[64,4096]{1,0:T(8,128)(2,1)S(1)} %collective-permute-done.2.refs_2_.refs_1_), channel_id=1, source_target_pairs={{0,16},{1,17},{2,18},{3,19},{4,20},{5,21},{6,22},{7,23},{8,24},{9,... | collective-permute-start | bytes 1572872 | tf_op jit(solution)/shard_map/ppermute | solution.py:27
  68.1 16.0 %collective-permute-start.13 = (bf16[64,4096]{1,0:T(8,128)(2,1)S(1)}, bf16[64,4096]{1,0:T(8,128)(2,1)}, u32[]{:S(2)}, u32[]{:S(2)}) collective-permute-start(bf16[64,4096]{1,0:T(8,128)(2,1)S(1)} %collective-permute-done.2.refs_2_.refs_1_), channel_id=1, source_target_pairs={{0,48},{1,49},{2,50},{3,51},{4,52},{5,53},{6,54},{7,55},{8,56},{9,... | collective-permute-start | bytes 1572872 | tf_op jit(solution)/shard_map/ppermute | solution.py:27
  71.0 13.1 %collective-permute-start.14 = (s16[272,256]{1,0:T(8,128)(2,1)S(1)}, s16[272,256]{1,0:T(8,128)(2,1)S(1)}, u32[]{:S(2)}, u32[]{:S(2)}) collective-permute-start(s16[272,256]{1,0:T(8,128)(2,1)S(1)} %copy-done.19), channel_id=1, source_target_pairs={{0,1},{1,0},{2,3},{3,2},{4,5},{5,4},{6,7},{7,6},{8,9},{9,8},{10,11... | collective-permute-start | bytes 417800 | tf_op jit(solution)/shard_map/ppermute | solution.py:27
  84.0 29.5 %collective-permute-start.20 = (s16[272,256]{1,0:T(8,128)(2,1)}, s16[272,256]{1,0:T(8,128)(2,1)S(1)}, u32[]{:S(2)}, u32[]{:S(2)}) collective-permute-start(s16[272,256]{1,0:T(8,128)(2,1)} %get-tuple-element.87), channel_id=1, source_target_pairs={{0,1},{1,0},{2,3},{3,2},{4,5},{5,4},{6,7},{7,6},{8,9},{9,8},{10,11... | collective-permute-start | bytes 417800 | tf_op jit(solution)/shard_map/ppermute | solution.py:27
  84.2 16.3 %collective-permute-start.16 = (bf16[64,4096]{1,0:T(8,128)(2,1)}, bf16[64,4096]{1,0:T(8,128)(2,1)S(1)}, u32[]{:S(2)}, u32[]{:S(2)}) collective-permute-start(bf16[64,4096]{1,0:T(8,128)(2,1)} %collective-permute-done.8.refs_3_.refs_4_), channel_id=1, source_target_pairs={{0,16},{1,17},{2,18},{3,19},{4,20},{5,21},{6,22},{7,23},{8,24},{9,... | collective-permute-start | bytes 1572872 | tf_op jit(solution)/shard_map/ppermute | solution.py:27
  84.2 16.2 %collective-permute-start.17 = (bf16[64,4096]{1,0:T(8,128)(2,1)}, bf16[64,4096]{1,0:T(8,128)(2,1)S(1)}, u32[]{:S(2)}, u32[]{:S(2)}) collective-permute-start(bf16[64,4096]{1,0:T(8,128)(2,1)} %collective-permute-done.8.refs_3_.refs_4_), channel_id=1, source_target_pairs={{0,48},{1,49},{2,50},{3,51},{4,52},{5,53},{6,54},{7,55},{8,56},{9,... | collective-permute-start | bytes 1572872 | tf_op jit(solution)/shard_map/ppermute | solution.py:27
  94.5 15.2 %collective-permute-start.18 = (s16[272,256]{1,0:T(8,128)(2,1)S(1)}, s16[272,256]{1,0:T(8,128)(2,1)S(1)}, u32[]{:S(2)}, u32[]{:S(2)}) collective-permute-start(s16[272,256]{1,0:T(8,128)(2,1)S(1)} %get-tuple-element.80), channel_id=1, source_target_pairs={{0,1},{1,0},{2,3},{3,2},{4,5},{5,4},{6,7},{7,6},{8,9},{9,8},{10,11... | collective-permute-start | bytes 417800 | tf_op jit(solution)/shard_map/ppermute | solution.py:27
  105.4 14.1 %collective-permute-start.21 = (s16[272,384]{1,0:T(8,128)(2,1)S(1)}, s16[272,384]{1,0:T(8,128)(2,1)S(1)}, u32[]{:S(2)}, u32[]{:S(2)}) collective-permute-start(s16[272,384]{1,0:T(8,128)(2,1)S(1)} %get-tuple-element.95), channel_id=1, source_target_pairs={{0,1},{1,0},{2,3},{3,2},{4,5},{5,4},{6,7},{7,6},{8,9},{9,8},{10,11... | collective-permute-start | bytes 626696 | tf_op jit(solution)/shard_map/ppermute | solution.py:27
  110.8 6.6 %collective-permute-start.19 = (s16[256,256]{1,0:T(8,128)(2,1)S(1)}, s16[256,256]{1,0:T(8,128)(2,1)S(1)}, u32[]{:S(2)}, u32[]{:S(2)}) collective-permute-start(s16[256,256]{1,0:T(8,128)(2,1)S(1)} %shard_map.59), channel_id=1, source_target_pairs={{0,32},{1,33},{2,34},{3,35},{4,36},{5,37},{6,38},{7,39},{8,40},{9,... | collective-permute-start | bytes 393224 | tf_op jit(solution)/shard_map/ppermute | solution.py:27
  (19 other events, 191.4 us)

commit v7 on v6

--- a/solution.py
+++ b/solution.py
@@ -191,6 +191,9 @@
         mean = lane_sums(rs[pl.ds(other, half), :]) * scale
         dev = deviation(lane_sums(rq[pl.ds(other, half), :]) * scale, mean)
         extra = [*split(mean), *split(dev)]
+        spare = msg.shape[1] - half
+        if spare:
+            extra = [jnp.concatenate([e, jnp.zeros((1, spare), jnp.float32)], axis=1) for e in extra]
     mean = lane_sums(sums) * scale
     dev = deviation(lane_sums(squares) * scale, mean)
     row = lax.broadcasted_iota(jnp.int32, cst.shape, 0)
@@ -278,6 +281,7 @@
 
 def row_factors(rst, block, half_id):
     mean2, dev2 = received(block, 4)
+    mean2, dev2 = mean2[:, : rst.shape[0] // 2], dev2[:, : rst.shape[0] // 2]
     index = lax.broadcasted_iota(jnp.int32, (8, mean2.shape[1]), 0)
     flip = jnp.where(index == 0, mean2, dev2).T
     half = flip.shape[0]
@@ -338,37 +342,34 @@
 
     a, copies = residuals(counts, size_factors, gene_means, dispersions, block_order)
 
-    far, z1 = move(a, y=2), move(a, z=1)
+    up[0], down[0], z1, far = move(a, y=1), move(a, y=-1), move(a, z=1), move(a, y=2)
+    z3 = move(a, z=3)
     rows = spread_x(copies)
-    a, far, z1, table = hold((a, far, z1, table))
+    up[0], down[0], z1, z3, far, table = hold((up[0], down[0], z1, z3, far, table))
     at_near, at_far, at_end = [(table, start) for start in starts[:3]]
 
-    up[0], down[0], z2 = move(a, y=1), move(a, y=-1), move(z1, z=1)
+    up[1], down[1], z2 = move(z1, y=1), move(z1, y=-1), move(z1, z=1)
+    far, far_c = hold((far, move(far, core=1)))
     right, left = move(far, x=1), move(far, x=-1)
-    a, rows, z2, up[0], down[0], right, left = hold((a, rows, z2, up[0], down[0], right, left))
+    rows, z2, up[1], down[1], right, left = hold((rows, z2, up[1], down[1], right, left))
 
     pieces = lambda k: [up[k], z[k], down[k]]
-    up[1], down[1], z3 = move(z1, y=1), move(z1, y=-1), move(a, z=3)
-    z = [a, z1, z2, z3]
-    across, rows_c = move(far, x=2), move(rows, core=1)
-    rows = (rows, rows_c), [(i // NX, 64 * (i % NX), 64) for i in range(2 * NX)]
-    own0, msg0, cst0, rstat, ordered = tiles(rows, pieces(0) + [a], None, at_near, True)
-    z3, up[1], down[1], far, right, left, across, own0 = hold(
-        (z3, up[1], down[1], far, right, left, across, own0)
-    )
-
     z = [a, z1, z2, z3]
     up[2], down[2] = move(z2, y=1), move(z2, y=-1)
-    far = jnp.concatenate([far, right, left, across], axis=0)
-    far_c = move(far, core=1)
-    msg0 = move(msg0, cell=1)
-    own1, msg1, cst1 = tiles(rows, pieces(1), rstat, at_near)
-    z3, up[2], down[2], msg0, own1, far, far_c = hold((z3, up[2], down[2], msg0, own1, far, far_c))
+    rows_c, across = move(rows, core=1), move(far, x=2)
+    rows = (rows, rows_c), [(i // NX, 64 * (i % NX), 64) for i in range(2 * NX)]
+    own01, msg01, cst01, rstat, ordered = tiles(
+        rows, pieces(0) + pieces(1), None, at_near, True
+    )
+    z3, up[2], down[2], own01, across = hold((z3, up[2], down[2], own01, across))
 
     z = [a, z1, z2, z3]
     up[3], down[3] = move(z3, y=1), move(z3, y=-1)
-    msg1 = move(msg1, cell=1)
-    ownf, msgf, cstf, fstat = tiles(((far, far_c), rows[1]), z, None, at_far, limit=48 * 1024 * 1024)
+    across_c, right_c, left_c = move(across, core=1), move(right, core=1), move(left, core=1)
+    msg01 = move(msg01, cell=1)
+    far = [far, right, left, across, far_c, right_c, left_c, across_c]
+    far = far, [(i, 0, 64) for i in range(len(far))]
+    ownf, msgf, cstf, fstat = tiles(far, z, None, at_far, limit=48 * 1024 * 1024)
     up[3], down[3], ownf = hold((up[3], down[3], ownf))
     msgf = move(msgf, cell=1)
     own23, msg23, cst23 = tiles(([ordered], []), pieces(2) + pieces(3), rstat, at_near)
@@ -381,12 +382,12 @@
     back = move(back, y=2)
 
     (result,) = call(
-        functools.partial(final_kernel, ((0,), (1,), (2, 3))),
+        functools.partial(final_kernel, ((0, 1), (2, 3))),
         [((half, 8, 128), jnp.float32)],
         [],
         1 << 24,
         at_end,
-        *(rstat, back, own0, msg0, cst0, own1, msg1, cst1, own23, msg23, cst23),
+        *(rstat, back, own01, msg01, cst01, own23, msg23, cst23),
     )
     return result.reshape(half, 1, 1024)
 

time: 123 us -> 116 us (0.943)
  the two profiles are of different devices: /device:TPU:32 before, /device:TPU:26 now
where the time goes in v7:
time: 116 us; the launch traced here: 115 us
  waiting for transfers between devices  46.3 us (40%)
  starting transfers between devices  37.9 us (33%)
  Pallas kernels  28.4 us (24%)
  local copies, waits for them, and re-layouts  2.56 us (2%)
    ppermute x24, waiting for transfers between devices, move(): return lax.ppermute(value, AXES, pairs)  46.3 us
    ppermute x24, starting transfers between devices, move(): return lax.ppermute(value, AXES, pairs)  32.9 us
    pallas_call x5, Pallas kernels, call(): pl.pallas_call(lambda table, *refs: kernel(From(table, first), *refs), in...  25 us
    all_to_all x1, starting transfers between devices, spread_x(): return lax.all_to_all(copies, 'x', 0, 0, tiled=True)  4.94 us
    pallas_call x1, Pallas kernels, residuals(): pl.pallas_call(functools.partial(resid_kernel, math.sqrt(cells * NH)), in...  3.39 us
  transfers between devices with their start and end apart: 25, of which 12 were waited for; matrix products, arithmetic and copies ran while one was open for 1% of the time, Pallas kernels for 19%

profile of v7, /device:TPU:26, one launch (start us, length us, event | category | flops | bytes accessed | tf_op | source)
XLA Modules:
  0.0 115.3 jit_solution(9824047108034695851)
XLA Ops:
  0.0 3.4 %shard_map.55 = (bf16[64,4096]{1,0:T(8,128)(2,1)}, bf16[256,4096]{1,0:T(8,128)(2,1)}) custom-call(s32[1]{0:T(128)} %bitcast.place, s32[128]{0:T(128)} %order.1, s32[64,4096]{1,0:T(8,128)} %counts.1, f32[1,4096]{1,0:T(1,128)} %bitcast.32, f32[64,128]{1,0:T(8,128)} %bitcast.30, f32[64,128]{1,0:T(8,128)} %bitcast.31), custom_call_target="tpu_custom_call" | custom-call | tf_op jit(solution)/shard_map/pallas_call | solution.py:59
  3.6 1.8 %collective-permute-start.1 = (bf16[64,4096]{1,0:T(8,128)(2,1)}, bf16[64,4096]{1,0:T(8,128)(2,1)S(1)}, u32[]{:S(2)}, u32[]{:S(2)}) collective-permute-start(bf16[64,4096]{1,0:T(8,128)(2,1)} %get-tuple-element.41.refs_1_.refs_0_), channel_id=1, source_target_pairs={{0,48},{1,49},{2,50},{3,51},{4,52},{5,53},{6,54},{7,55},{8,56},{9,... | collective-permute-start | bytes 1572872 | tf_op jit(solution)/shard_map/ppermute | solution.py:27
  5.4 1.9 %collective-permute-start.2 = (bf16[64,4096]{1,0:T(8,128)(2,1)}, bf16[64,4096]{1,0:T(8,128)(2,1)S(1)}, u32[]{:S(2)}, u32[]{:S(2)}) collective-permute-start(bf16[64,4096]{1,0:T(8,128)(2,1)} %get-tuple-element.41.refs_1_.refs_0_), channel_id=1, source_target_pairs={{0,64},{1,65},{2,66},{3,67},{4,68},{5,69},{6,70},{7,71},{8,72},{9,... | collective-permute-start | bytes 1572872 | tf_op jit(solution)/shard_map/ppermute | solution.py:27
  7.3 2.7 %collective-permute-start.3 = (bf16[64,4096]{1,0:T(8,128)(2,1)}, bf16[64,4096]{1,0:T(8,128)(2,1)S(1)}, u32[]{:S(2)}, u32[]{:S(2)}) collective-permute-start(bf16[64,4096]{1,0:T(8,128)(2,1)} %get-tuple-element.41.refs_1_.refs_0_), channel_id=1, source_target_pairs={{0,192},{1,193},{2,194},{3,195},{4,196},{5,197},{6,198},{7,199},{8... | collective-permute-start | bytes 1572872 | tf_op jit(solution)/shard_map/ppermute | solution.py:27
  11.3 4.9 %all-to-all-start = ((bf16[4,64,4096]{2,1,0:T(8,128)(2,1)}), bf16[4,64,4096]{2,1,0:T(8,128)(2,1)}, u32[]{:S(2)}, u32[]{:S(2)}) async-start(bf16[4,64,4096]{2,1,0:T(8,128)(2,1)} %bitcast.29), calls=%async_computation | async-start | bytes 4194304 | tf_op jit(solution)/shard_map/all_to_all | solution.py:31
  16.9 1.5 %collective-permute-done.refs_0_ = bf16[64,4096]{1,0:T(8,128)(2,1)S(1)} collective-permute-done((bf16[64,4096]{1,0:T(8,128)(2,1)}, bf16[64,4096]{1,0:T(8,128)(2,1)S(1)}, u32[]{:S(2)}, u32[]{:S(2)}) %collective-permute-start) | collective-permute-done | bytes 524320 | tf_op jit(solution)/shard_map/ppermute | solution.py:27
  18.4 11.3 %collective-permute-done.1.refs_2_ = bf16[64,4096]{1,0:T(8,128)(2,1)S(1)} collective-permute-done((bf16[64,4096]{1,0:T(8,128)(2,1)}, bf16[64,4096]{1,0:T(8,128)(2,1)S(1)}, u32[]{:S(2)}, u32[]{:S(2)}) %collective-permute-start.1) | collective-permute-done | bytes 524320 | tf_op jit(solution)/shard_map/ppermute | solution.py:27
  29.7 2.1 %collective-permute-done.3.refs_3_.refs_4_ = bf16[64,4096]{1,0:T(8,128)(2,1)S(1)} collective-permute-done((bf16[64,4096]{1,0:T(8,128)(2,1)}, bf16[64,4096]{1,0:T(8,128)(2,1)S(1)}, u32[]{:S(2)}, u32[]{:S(2)}) %collective-permute-start.3) | collective-permute-done | bytes 524320 | tf_op jit(solution)/shard_map/ppermute | solution.py:27
  31.9 1.8 %collective-permute-start.5 = (bf16[64,4096]{1,0:T(8,128)(2,1)S(1)}, bf16[64,4096]{1,0:T(8,128)(2,1)S(1)}, u32[]{:S(2)}, u32[]{:S(2)}) collective-permute-start(bf16[64,4096]{1,0:T(8,128)(2,1)S(1)} %collective-permute-done.2.refs_4_.refs_1_), channel_id=1, source_target_pairs={{0,64},{1,65},{2,66},{3,67},{4,68},{5,69},{6,70},{7,71},{8,72},{9,... | collective-permute-start | bytes 1572872 | tf_op jit(solution)/shard_map/ppermute | solution.py:27
  37.8 10.3 %collective-permute-done.5.refs_2_.refs_1_ = bf16[64,4096]{1,0:T(8,128)(2,1)S(1)} collective-permute-done((bf16[64,4096]{1,0:T(8,128)(2,1)S(1)}, bf16[64,4096]{1,0:T(8,128)(2,1)S(1)}, u32[]{:S(2)}, u32[]{:S(2)}) %collective-permute-start.5) | collective-permute-done | bytes 524320 | tf_op jit(solution)/shard_map/ppermute | solution.py:27
  48.1 2.0 %collective-permute-done.7.refs_5_ = bf16[64,4096]{1,0:T(8,128)(2,1)S(1)} collective-permute-done((bf16[64,4096]{1,0:T(8,128)(2,1)S(1)}, bf16[64,4096]{1,0:T(8,128)(2,1)S(1)}, u32[]{:S(2)}, u32[]{:S(2)}) %collective-permute-start.7) | collective-permute-done | bytes 524320 | tf_op jit(solution)/shard_map/ppermute | solution.py:27
  51.6 2.2 %collective-permute-start.14 = (bf16[64,4096]{1,0:T(8,128)(2,1)S(1)}, bf16[64,4096]{1,0:T(8,128)(2,1)}, u32[]{:S(2)}, u32[]{:S(2)}) collective-permute-start(bf16[64,4096]{1,0:T(8,128)(2,1)S(1)} %collective-permute-done.4.refs_4_), channel_id=1, source_target_pairs={{0,8},{1,9},{2,10},{3,11},{4,12},{5,13},{6,14},{7,15},{8,0},{9,1},... | collective-permute-start | bytes 1572872 | tf_op jit(solution)/shard_map/ppermute | solution.py:27
  53.8 2.2 %collective-permute-start.12 = (bf16[64,4096]{1,0:T(8,128)(2,1)S(1)}, bf16[64,4096]{1,0:T(8,128)(2,1)}, u32[]{:S(2)}, u32[]{:S(2)}) collective-permute-start(bf16[64,4096]{1,0:T(8,128)(2,1)S(1)} %collective-permute-done.5.refs_2_.refs_1_), channel_id=1, source_target_pairs={{0,16},{1,17},{2,18},{3,19},{4,20},{5,21},{6,22},{7,23},{8,24},{9,... | collective-permute-start | bytes 1572872 | tf_op jit(solution)/shard_map/ppermute | solution.py:27
  56.5 8.6 %shard_map.56 = (f32[256,384]{1,0:T(8,128)}, s16[272,384]{1,0:T(8,128)(2,1)}, f32[8,384]{1,0:T(8,128)}, f32[512,128]{1,0:T(8,128)}, bf16[512,4096]{1,0:T(8,128)(2,1)}) custom-call(s32[24]{0:T(128)} %stack.93.table, bf16[64,4096]{1,0:T(8,128)(2,1)} %copy-done.8, bf16[64,4096]{1,0:T(8,128)(2,1)} %get-tuple-element.41.refs_1_.refs_0_, ...), custom_call_target="tpu_custom_call" | custom-call | flops 9497647104 | bytes 1048576 | tf_op jit(solution)/shard_map/pallas_call | solution.py:225
  65.1 2.5 %collective-permute-done.14.refs_7_ = bf16[64,4096]{1,0:T(8,128)(2,1)} collective-permute-done((bf16[64,4096]{1,0:T(8,128)(2,1)S(1)}, bf16[64,4096]{1,0:T(8,128)(2,1)}, u32[]{:S(2)}, u32[]{:S(2)}) %collective-permute-start.14) | collective-permute-done | bytes 524320 | tf_op jit(solution)/shard_map/ppermute | solution.py:27
  67.9 3.1 %collective-permute-done.13.refs_2_ = bf16[64,4096]{1,0:T(8,128)(2,1)} collective-permute-done((bf16[64,4096]{1,0:T(8,128)(2,1)S(1)}, bf16[64,4096]{1,0:T(8,128)(2,1)}, u32[]{:S(2)}, u32[]{:S(2)}) %collective-permute-start.13) | collective-permute-done | bytes 524320 | tf_op jit(solution)/shard_map/ppermute | solution.py:27
  71.3 1.7 %collective-permute-start.16 = (bf16[64,4096]{1,0:T(8,128)(2,1)S(1)}, bf16[64,4096]{1,0:T(8,128)(2,1)S(1)}, u32[]{:S(2)}, u32[]{:S(2)}) collective-permute-start(bf16[64,4096]{1,0:T(8,128)(2,1)S(1)} %collective-permute-done.3.refs_3_.refs_4_), channel_id=1, source_target_pairs={{0,48},{1,49},{2,50},{3,51},{4,52},{5,53},{6,54},{7,55},{8,56},{9,... | collective-permute-start | bytes 1572872 | tf_op jit(solution)/shard_map/ppermute | solution.py:27
  73.0 6.1 %collective-permute-start.22 = (s16[272,384]{1,0:T(8,128)(2,1)}, s16[272,384]{1,0:T(8,128)(2,1)S(1)}, u32[]{:S(2)}, u32[]{:S(2)}) collective-permute-start(s16[272,384]{1,0:T(8,128)(2,1)} %get-tuple-element.67), channel_id=1, source_target_pairs={{0,1},{1,0},{2,3},{3,2},{4,5},{5,4},{6,7},{7,6},{8,9},{9,8},{10,11... | collective-permute-start | bytes 626696 | tf_op jit(solution)/shard_map/ppermute | solution.py:27
  81.0 7.3 %shard_map.57 = (f32[256,256]{1,0:T(8,128)S(1)}, s16[272,256]{1,0:T(8,128)(2,1)S(1)}, f32[8,256]{1,0:T(8,128)S(1)}, f32[512,128]{1,0:T(8,128)S(1)}) custom-call(s32[24]{0:T(128)S(1)} %copy-done.3, bf16[64,4096]{1,0:T(8,128)(2,1)S(1)} %copy-done.4, bf16[64,4096]{1,0:T(8,128)(2,1)S(1)} %copy-done.6, ...), custom_call_target="tpu_custom_call" | custom-call | flops 8631764992 | bytes 1048576 | tf_op jit(solution)/shard_map/pallas_call | solution.py:225
  88.4 4.3 %collective-permute-start.20 = (s16[272,256]{1,0:T(8,128)(2,1)S(1)}, s16[272,256]{1,0:T(8,128)(2,1)S(1)}, u32[]{:S(2)}, u32[]{:S(2)}) collective-permute-start(s16[272,256]{1,0:T(8,128)(2,1)S(1)} %get-tuple-element.63), channel_id=1, source_target_pairs={{0,1},{1,0},{2,3},{3,2},{4,5},{5,4},{6,7},{7,6},{8,9},{9,8},{10,11... | collective-permute-start | bytes 417800 | tf_op jit(solution)/shard_map/ppermute | solution.py:27
  92.7 4.7 %shard_map.59 = (f32[256,384]{1,0:T(8,128)S(1)}, s16[272,384]{1,0:T(8,128)(2,1)S(1)}, f32[8,384]{1,0:T(8,128)S(1)}) custom-call(s32[24]{0:T(128)S(1)} %copy-done.3, bf16[64,4096]{1,0:T(8,128)(2,1)} %collective-permute-done.12.refs_0_, bf16[64,4096]{1,0:T(8,128)(2,1)S(1)} %collective-permute-done.5.refs_2_.refs_1_, ...), custom_call_target="tpu_custom_call" | custom-call | flops 5472647168 | bytes 1048576 | tf_op jit(solution)/shard_map/pallas_call | solution.py:225
  97.4 1.8 %collective-permute-start.23 = (s16[272,384]{1,0:T(8,128)(2,1)S(1)}, s16[272,384]{1,0:T(8,128)(2,1)S(1)}, u32[]{:S(2)}, u32[]{:S(2)}) collective-permute-start(s16[272,384]{1,0:T(8,128)(2,1)S(1)} %get-tuple-element.75), channel_id=1, source_target_pairs={{0,1},{1,0},{2,3},{3,2},{4,5},{5,4},{6,7},{7,6},{8,9},{9,8},{10,11... | collective-permute-start | bytes 626696 | tf_op jit(solution)/shard_map/ppermute | solution.py:27
  101.8 10.2 %collective-permute-done.23.refs_6_ = s16[272,384]{1,0:T(8,128)(2,1)S(1)} collective-permute-done((s16[272,384]{1,0:T(8,128)(2,1)S(1)}, s16[272,384]{1,0:T(8,128)(2,1)S(1)}, u32[]{:S(2)}, u32[]{:S(2)}) %collective-permute-start.23) | collective-permute-done | bytes 208928 | tf_op jit(solution)/shard_map/ppermute | solution.py:27
  112.1 3.3 %shard_map.60 = f32[256,8,128]{2,1,0:T(8,128)} custom-call(s32[24]{0:T(128)S(1)} %copy-done.3, f32[512,128]{1,0:T(8,128)S(1)} %copy-done.1, s16[256,256]{1,0:T(8,128)(2,1)S(1)} %collective-permute-done.21.refs_1_, f32[256,384]{1,0:T(8,128)S(1)} %copy-done, s16[272,384]{1,0:T(8,128)(2,1)S(1)} %collective-permute-done.22.refs_3_, f32[8,384]{1,0:T(8,128)S(1)} %copy-done.2, ...), custom_call_target="tpu_custom_call" | custom-call | flops 16777216 | bytes 1048576 | tf_op jit(solution)/shard_map/pallas_call | solution.py:225
  (59 shorter events, 13.5 us)
Async XLA Ops:
  3.4 15.0 %collective-permute-start = (bf16[64,4096]{1,0:T(8,128)(2,1)}, bf16[64,4096]{1,0:T(8,128)(2,1)S(1)}, u32[]{:S(2)}, u32[]{:S(2)}) collective-permute-start(bf16[64,4096]{1,0:T(8,128)(2,1)} %get-tuple-element.41.refs_1_.refs_0_), channel_id=1, source_target_pairs={{0,16},{1,17},{2,18},{3,19},{4,20},{5,21},{6,22},{7,23},{8,24},{9,... | collective-permute-start | bytes 1572872 | tf_op jit(solution)/shard_map/ppermute | solution.py:27
  3.6 26.1 %collective-permute-start.1 = (bf16[64,4096]{1,0:T(8,128)(2,1)}, bf16[64,4096]{1,0:T(8,128)(2,1)S(1)}, u32[]{:S(2)}, u32[]{:S(2)}) collective-permute-start(bf16[64,4096]{1,0:T(8,128)(2,1)} %get-tuple-element.41.refs_1_.refs_0_), channel_id=1, source_target_pairs={{0,48},{1,49},{2,50},{3,51},{4,52},{5,53},{6,54},{7,55},{8,56},{9,... | collective-permute-start | bytes 1572872 | tf_op jit(solution)/shard_map/ppermute | solution.py:27
  5.4 24.3 %collective-permute-start.2 = (bf16[64,4096]{1,0:T(8,128)(2,1)}, bf16[64,4096]{1,0:T(8,128)(2,1)S(1)}, u32[]{:S(2)}, u32[]{:S(2)}) collective-permute-start(bf16[64,4096]{1,0:T(8,128)(2,1)} %get-tuple-element.41.refs_1_.refs_0_), channel_id=1, source_target_pairs={{0,64},{1,65},{2,66},{3,67},{4,68},{5,69},{6,70},{7,71},{8,72},{9,... | collective-permute-start | bytes 1572872 | tf_op jit(solution)/shard_map/ppermute | solution.py:27
  7.3 24.5 %collective-permute-start.3 = (bf16[64,4096]{1,0:T(8,128)(2,1)}, bf16[64,4096]{1,0:T(8,128)(2,1)S(1)}, u32[]{:S(2)}, u32[]{:S(2)}) collective-permute-start(bf16[64,4096]{1,0:T(8,128)(2,1)} %get-tuple-element.41.refs_1_.refs_0_), channel_id=1, source_target_pairs={{0,192},{1,193},{2,194},{3,195},{4,196},{5,197},{6,198},{7,199},{8... | collective-permute-start | bytes 1572872 | tf_op jit(solution)/shard_map/ppermute | solution.py:27
  10.0 21.8 %collective-permute-start.4 = (bf16[64,4096]{1,0:T(8,128)(2,1)}, bf16[64,4096]{1,0:T(8,128)(2,1)S(1)}, u32[]{:S(2)}, u32[]{:S(2)}) collective-permute-start(bf16[64,4096]{1,0:T(8,128)(2,1)} %get-tuple-element.41.refs_1_.refs_0_), channel_id=1, source_target_pairs={{0,32},{1,33},{2,34},{3,35},{4,36},{5,37},{6,38},{7,39},{8,40},{9,... | collective-permute-start | bytes 1572872 | tf_op jit(solution)/shard_map/ppermute | solution.py:27
  11.3 40.2 %all-to-all-start = ((bf16[4,64,4096]{2,1,0:T(8,128)(2,1)}), bf16[4,64,4096]{2,1,0:T(8,128)(2,1)}, u32[]{:S(2)}, u32[]{:S(2)}) async-start(bf16[4,64,4096]{2,1,0:T(8,128)(2,1)} %bitcast.29), calls=%async_computation | async-start | bytes 4194304 | tf_op jit(solution)/shard_map/all_to_all | solution.py:31
  31.9 16.1 %collective-permute-start.5 = (bf16[64,4096]{1,0:T(8,128)(2,1)S(1)}, bf16[64,4096]{1,0:T(8,128)(2,1)S(1)}, u32[]{:S(2)}, u32[]{:S(2)}) collective-permute-start(bf16[64,4096]{1,0:T(8,128)(2,1)S(1)} %collective-permute-done.2.refs_4_.refs_1_), channel_id=1, source_target_pairs={{0,64},{1,65},{2,66},{3,67},{4,68},{5,69},{6,70},{7,71},{8,72},{9,... | collective-permute-start | bytes 1572872 | tf_op jit(solution)/shard_map/ppermute | solution.py:27
  33.7 14.4 %collective-permute-start.6 = (bf16[64,4096]{1,0:T(8,128)(2,1)S(1)}, bf16[64,4096]{1,0:T(8,128)(2,1)S(1)}, u32[]{:S(2)}, u32[]{:S(2)}) collective-permute-start(bf16[64,4096]{1,0:T(8,128)(2,1)S(1)} %collective-permute-done.2.refs_4_.refs_1_), channel_id=1, source_target_pairs={{0,16},{1,17},{2,18},{3,19},{4,20},{5,21},{6,22},{7,23},{8,24},{9,... | collective-permute-start | bytes 1572872 | tf_op jit(solution)/shard_map/ppermute | solution.py:27
  35.2 14.8 %collective-permute-start.7 = (bf16[64,4096]{1,0:T(8,128)(2,1)S(1)}, bf16[64,4096]{1,0:T(8,128)(2,1)S(1)}, u32[]{:S(2)}, u32[]{:S(2)}) collective-permute-start(bf16[64,4096]{1,0:T(8,128)(2,1)S(1)} %collective-permute-done.2.refs_4_.refs_1_), channel_id=1, source_target_pairs={{0,48},{1,49},{2,50},{3,51},{4,52},{5,53},{6,54},{7,55},{8,56},{9,... | collective-permute-start | bytes 1572872 | tf_op jit(solution)/shard_map/ppermute | solution.py:27
  35.7 15.8 %collective-permute-start.10 = (bf16[64,4096]{1,0:T(8,128)(2,1)S(1)}, bf16[64,4096]{1,0:T(8,128)(2,1)S(1)}, u32[]{:S(2)}, u32[]{:S(2)}) collective-permute-start(bf16[64,4096]{1,0:T(8,128)(2,1)S(1)} %collective-permute-done.4.refs_4_), channel_id=1, source_target_pairs={{0,12},{1,13},{2,14},{3,15},{4,0},{5,1},{6,2},{7,3},{8,4},{9,5},{1... | collective-permute-start | bytes 1572872 | tf_op jit(solution)/shard_map/ppermute | solution.py:27
  36.3 15.2 %collective-permute-start.9 = (bf16[64,4096]{1,0:T(8,128)(2,1)S(1)}, bf16[64,4096]{1,0:T(8,128)(2,1)}, u32[]{:S(2)}, u32[]{:S(2)}) collective-permute-start(bf16[64,4096]{1,0:T(8,128)(2,1)S(1)} %collective-permute-done.4.refs_4_), channel_id=1, source_target_pairs={{0,4},{1,5},{2,6},{3,7},{4,8},{5,9},{6,10},{7,11},{8,12},{9,13},{1... | collective-permute-start | bytes 1572872 | tf_op jit(solution)/shard_map/ppermute | solution.py:27
  51.5 4.6 %collective-permute-start.11 = (bf16[256,4096]{1,0:T(8,128)(2,1)}, bf16[256,4096]{1,0:T(8,128)(2,1)}, u32[]{:S(2)}, u32[]{:S(2)}) collective-permute-start(bf16[256,4096]{1,0:T(8,128)(2,1)} %bitcast.27.refs_6_), channel_id=1, source_target_pairs={{0,2},{1,3},{2,0},{3,1},{4,6},{5,7},{6,4},{7,5},{8,10},{9,11},{10,... | collective-permute-start | bytes 6291464 | tf_op jit(solution)/shard_map/ppermute | solution.py:27
  51.6 16.0 %collective-permute-start.14 = (bf16[64,4096]{1,0:T(8,128)(2,1)S(1)}, bf16[64,4096]{1,0:T(8,128)(2,1)}, u32[]{:S(2)}, u32[]{:S(2)}) collective-permute-start(bf16[64,4096]{1,0:T(8,128)(2,1)S(1)} %collective-permute-done.4.refs_4_), channel_id=1, source_target_pairs={{0,8},{1,9},{2,10},{3,11},{4,12},{5,13},{6,14},{7,15},{8,0},{9,1},... | collective-permute-start | bytes 1572872 | tf_op jit(solution)/shard_map/ppermute | solution.py:27
  53.8 14.1 %collective-permute-start.12 = (bf16[64,4096]{1,0:T(8,128)(2,1)S(1)}, bf16[64,4096]{1,0:T(8,128)(2,1)}, u32[]{:S(2)}, u32[]{:S(2)}) collective-permute-start(bf16[64,4096]{1,0:T(8,128)(2,1)S(1)} %collective-permute-done.5.refs_2_.refs_1_), channel_id=1, source_target_pairs={{0,16},{1,17},{2,18},{3,19},{4,20},{5,21},{6,22},{7,23},{8,24},{9,... | collective-permute-start | bytes 1572872 | tf_op jit(solution)/shard_map/ppermute | solution.py:27
  56.0 15.0 %collective-permute-start.13 = (bf16[64,4096]{1,0:T(8,128)(2,1)S(1)}, bf16[64,4096]{1,0:T(8,128)(2,1)}, u32[]{:S(2)}, u32[]{:S(2)}) collective-permute-start(bf16[64,4096]{1,0:T(8,128)(2,1)S(1)} %collective-permute-done.5.refs_2_.refs_1_), channel_id=1, source_target_pairs={{0,48},{1,49},{2,50},{3,51},{4,52},{5,53},{6,54},{7,55},{8,56},{9,... | collective-permute-start | bytes 1572872 | tf_op jit(solution)/shard_map/ppermute | solution.py:27
  56.0 17.0 %collective-permute-start.17 = (bf16[64,4096]{1,0:T(8,128)(2,1)}, bf16[64,4096]{1,0:T(8,128)(2,1)}, u32[]{:S(2)}, u32[]{:S(2)}) collective-permute-start(bf16[64,4096]{1,0:T(8,128)(2,1)} %collective-permute-done.9.refs_5_), channel_id=1, source_target_pairs={{0,2},{1,3},{2,0},{3,1},{4,6},{5,7},{6,4},{7,5},{8,10},{9,11},{10,... | collective-permute-start | bytes 1572872 | tf_op jit(solution)/shard_map/ppermute | solution.py:27
  56.1 23.0 %collective-permute-start.18 = (bf16[64,4096]{1,0:T(8,128)(2,1)S(1)}, bf16[64,4096]{1,0:T(8,128)(2,1)}, u32[]{:S(2)}, u32[]{:S(2)}) collective-permute-start(bf16[64,4096]{1,0:T(8,128)(2,1)S(1)} %collective-permute-done.10.refs_6_), channel_id=1, source_target_pairs={{0,2},{1,3},{2,0},{3,1},{4,6},{5,7},{6,4},{7,5},{8,10},{9,11},{10,... | collective-permute-start | bytes 1572872 | tf_op jit(solution)/shard_map/ppermute | solution.py:27
  71.0 8.1 %collective-permute-start.19 = (bf16[64,4096]{1,0:T(8,128)(2,1)}, bf16[64,4096]{1,0:T(8,128)(2,1)S(1)}, u32[]{:S(2)}, u32[]{:S(2)}) collective-permute-start(bf16[64,4096]{1,0:T(8,128)(2,1)} %collective-permute-done.14.refs_7_), channel_id=1, source_target_pairs={{0,2},{1,3},{2,0},{3,1},{4,6},{5,7},{6,4},{7,5},{8,10},{9,11},{10,... | collective-permute-start | bytes 1572872 | tf_op jit(solution)/shard_map/ppermute | solution.py:27
  71.0 17.3 %collective-permute-start.15 = (bf16[64,4096]{1,0:T(8,128)(2,1)S(1)}, bf16[64,4096]{1,0:T(8,128)(2,1)S(1)}, u32[]{:S(2)}, u32[]{:S(2)}) collective-permute-start(bf16[64,4096]{1,0:T(8,128)(2,1)S(1)} %collective-permute-done.3.refs_3_.refs_4_), channel_id=1, source_target_pairs={{0,16},{1,17},{2,18},{3,19},{4,20},{5,21},{6,22},{7,23},{8,24},{9,... | collective-permute-start | bytes 1572872 | tf_op jit(solution)/shard_map/ppermute | solution.py:27
  71.3 17.1 %collective-permute-start.16 = (bf16[64,4096]{1,0:T(8,128)(2,1)S(1)}, bf16[64,4096]{1,0:T(8,128)(2,1)S(1)}, u32[]{:S(2)}, u32[]{:S(2)}) collective-permute-start(bf16[64,4096]{1,0:T(8,128)(2,1)S(1)} %collective-permute-done.3.refs_3_.refs_4_), channel_id=1, source_target_pairs={{0,48},{1,49},{2,50},{3,51},{4,52},{5,53},{6,54},{7,55},{8,56},{9,... | collective-permute-start | bytes 1572872 | tf_op jit(solution)/shard_map/ppermute | solution.py:27
  73.0 28.8 %collective-permute-start.22 = (s16[272,384]{1,0:T(8,128)(2,1)}, s16[272,384]{1,0:T(8,128)(2,1)S(1)}, u32[]{:S(2)}, u32[]{:S(2)}) collective-permute-start(s16[272,384]{1,0:T(8,128)(2,1)} %get-tuple-element.67), channel_id=1, source_target_pairs={{0,1},{1,0},{2,3},{3,2},{4,5},{5,4},{6,7},{7,6},{8,9},{9,8},{10,11... | collective-permute-start | bytes 626696 | tf_op jit(solution)/shard_map/ppermute | solution.py:27
  88.4 12.3 %collective-permute-start.20 = (s16[272,256]{1,0:T(8,128)(2,1)S(1)}, s16[272,256]{1,0:T(8,128)(2,1)S(1)}, u32[]{:S(2)}, u32[]{:S(2)}) collective-permute-start(s16[272,256]{1,0:T(8,128)(2,1)S(1)} %get-tuple-element.63), channel_id=1, source_target_pairs={{0,1},{1,0},{2,3},{3,2},{4,5},{5,4},{6,7},{7,6},{8,9},{9,8},{10,11... | collective-permute-start | bytes 417800 | tf_op jit(solution)/shard_map/ppermute | solution.py:27
  97.4 14.7 %collective-permute-start.23 = (s16[272,384]{1,0:T(8,128)(2,1)S(1)}, s16[272,384]{1,0:T(8,128)(2,1)S(1)}, u32[]{:S(2)}, u32[]{:S(2)}) collective-permute-start(s16[272,384]{1,0:T(8,128)(2,1)S(1)} %get-tuple-element.75), channel_id=1, source_target_pairs={{0,1},{1,0},{2,3},{3,2},{4,5},{5,4},{6,7},{7,6},{8,9},{9,8},{10,11... | collective-permute-start | bytes 626696 | tf_op jit(solution)/shard_map/ppermute | solution.py:27
  101.7 10.3 %collective-permute-start.21 = (s16[256,256]{1,0:T(8,128)(2,1)S(1)}, s16[256,256]{1,0:T(8,128)(2,1)S(1)}, u32[]{:S(2)}, u32[]{:S(2)}) collective-permute-start(s16[256,256]{1,0:T(8,128)(2,1)S(1)} %shard_map.58), channel_id=1, source_target_pairs={{0,32},{1,33},{2,34},{3,35},{4,36},{5,37},{6,38},{7,39},{8,40},{9,... | collective-permute-start | bytes 393224 | tf_op jit(solution)/shard_map/ppermute | solution.py:27
  (14 other events, 163.9 us)

commit v8 on v7

--- a/solution.py
+++ b/solution.py
@@ -343,15 +343,15 @@
     a, copies = residuals(counts, size_factors, gene_means, dispersions, block_order)
 
     up[0], down[0], z1, far = move(a, y=1), move(a, y=-1), move(a, z=1), move(a, y=2)
-    z3 = move(a, z=3)
     rows = spread_x(copies)
-    up[0], down[0], z1, z3, far, table = hold((up[0], down[0], z1, z3, far, table))
+    a, up[0], down[0], z1, far, table = hold((a, up[0], down[0], z1, far, table))
     at_near, at_far, at_end = [(table, start) for start in starts[:3]]
 
     up[1], down[1], z2 = move(z1, y=1), move(z1, y=-1), move(z1, z=1)
     far, far_c = hold((far, move(far, core=1)))
     right, left = move(far, x=1), move(far, x=-1)
-    rows, z2, up[1], down[1], right, left = hold((rows, z2, up[1], down[1], right, left))
+    a, rows, z2, up[1], down[1], right, left = hold((a, rows, z2, up[1], down[1], right, left))
+    z3 = move(a, z=3)
 
     pieces = lambda k: [up[k], z[k], down[k]]
     z = [a, z1, z2, z3]

time: 116 us -> 116 us (level); the launches traced: 115 us -> 114 us
  waiting for transfers between devices: 46.3 us -> 39.7 us
  starting transfers between devices: 37.9 us -> 40.6 us
  local copies, waits for them, and re-layouts: 2.56 us -> 4.92 us
    ppermute x24, waiting for transfers between devices: 46.3 us -> 39.7 us  [move(): return lax.ppermute(value, AXES, pairs)]
    ppermute x24, starting transfers between devices: 32.9 us -> 35.5 us  [move(): return lax.ppermute(value, AXES, pairs)]
    unnamed x26 -> x30, local copies, waits for them, and re-layouts: 1.87 us -> 4.29 us
  transfers between devices with their start and end apart: 25 -> 25, of which waited for: 12 -> 8; matrix products, arithmetic and copies ran while one was open for 1% -> 1% of each run, Pallas kernels for 19% -> 19%
where the time goes in v8:
time: 116 us; the launch traced here: 114 us
  starting transfers between devices  40.6 us (35%)
  waiting for transfers between devices  39.7 us (34%)
  Pallas kernels  28.5 us (25%)
  local copies, waits for them, and re-layouts  4.92 us (4%)
    ppermute x24, waiting for transfers between devices, move(): return lax.ppermute(value, AXES, pairs)  39.7 us
    ppermute x24, starting transfers between devices, move(): return lax.ppermute(value, AXES, pairs)  35.5 us
    pallas_call x5, Pallas kernels, call(): pl.pallas_call(lambda table, *refs: kernel(From(table, first), *refs), in...  25.1 us
    all_to_all x1, starting transfers between devices, spread_x(): return lax.all_to_all(copies, 'x', 0, 0, tiled=True)  5.07 us
    unnamed x30, local copies, waits for them, and re-layouts  4.29 us
    pallas_call x1, Pallas kernels, residuals(): pl.pallas_call(functools.partial(resid_kernel, math.sqrt(cells * NH)), in...  3.38 us
  transfers between devices with their start and end apart: 25, of which 8 were waited for; matrix products, arithmetic and copies ran while one was open for 1% of the time, Pallas kernels for 19%

profile of v8, /device:TPU:26, one launch (start us, length us, event | category | flops | bytes accessed | tf_op | source)
XLA Modules:
  0.0 113.8 jit_solution(14465612306098684244)
XLA Ops:
  0.0 3.4 %shard_map.55 = (bf16[64,4096]{1,0:T(8,128)(2,1)}, bf16[256,4096]{1,0:T(8,128)(2,1)}) custom-call(s32[1]{0:T(128)} %bitcast.place, s32[128]{0:T(128)} %order.1, s32[64,4096]{1,0:T(8,128)} %counts.1, f32[1,4096]{1,0:T(1,128)} %bitcast.32, f32[64,128]{1,0:T(8,128)} %bitcast.30, f32[64,128]{1,0:T(8,128)} %bitcast.31), custom_call_target="tpu_custom_call" | custom-call | tf_op jit(solution)/shard_map/pallas_call | solution.py:59
  3.6 1.8 %collective-permute-start.1 = (bf16[64,4096]{1,0:T(8,128)(2,1)}, bf16[64,4096]{1,0:T(8,128)(2,1)S(1)}, u32[]{:S(2)}, u32[]{:S(2)}) collective-permute-start(bf16[64,4096]{1,0:T(8,128)(2,1)} %get-tuple-element.50.refs_1_.refs_0_), channel_id=1, source_target_pairs={{0,48},{1,49},{2,50},{3,51},{4,52},{5,53},{6,54},{7,55},{8,56},{9,... | collective-permute-start | bytes 1572872 | tf_op jit(solution)/shard_map/ppermute | solution.py:27
  5.4 1.9 %collective-permute-start.2 = (bf16[64,4096]{1,0:T(8,128)(2,1)}, bf16[64,4096]{1,0:T(8,128)(2,1)S(1)}, u32[]{:S(2)}, u32[]{:S(2)}) collective-permute-start(bf16[64,4096]{1,0:T(8,128)(2,1)} %get-tuple-element.50.refs_1_.refs_0_), channel_id=1, source_target_pairs={{0,64},{1,65},{2,66},{3,67},{4,68},{5,69},{6,70},{7,71},{8,72},{9,... | collective-permute-start | bytes 1572872 | tf_op jit(solution)/shard_map/ppermute | solution.py:27
  7.3 1.2 %collective-permute-start.3 = (bf16[64,4096]{1,0:T(8,128)(2,1)}, bf16[64,4096]{1,0:T(8,128)(2,1)S(1)}, u32[]{:S(2)}, u32[]{:S(2)}) collective-permute-start(bf16[64,4096]{1,0:T(8,128)(2,1)} %get-tuple-element.50.refs_1_.refs_0_), channel_id=1, source_target_pairs={{0,32},{1,33},{2,34},{3,35},{4,36},{5,37},{6,38},{7,39},{8,40},{9,... | collective-permute-start | bytes 1572872 | tf_op jit(solution)/shard_map/ppermute | solution.py:27
  8.6 5.1 %all-to-all-start = ((bf16[4,64,4096]{2,1,0:T(8,128)(2,1)}), bf16[4,64,4096]{2,1,0:T(8,128)(2,1)}, u32[]{:S(2)}, u32[]{:S(2)}) async-start(bf16[4,64,4096]{2,1,0:T(8,128)(2,1)} %bitcast.29), calls=%async_computation | async-start | bytes 4194304 | tf_op jit(solution)/shard_map/all_to_all | solution.py:31
  14.3 4.1 %collective-permute-done.refs_0_ = bf16[64,4096]{1,0:T(8,128)(2,1)S(1)} collective-permute-done((bf16[64,4096]{1,0:T(8,128)(2,1)}, bf16[64,4096]{1,0:T(8,128)(2,1)S(1)}, u32[]{:S(2)}, u32[]{:S(2)}) %collective-permute-start) | collective-permute-done | bytes 524320 | tf_op jit(solution)/shard_map/ppermute | solution.py:27
  18.4 11.3 %collective-permute-done.1.refs_2_ = bf16[64,4096]{1,0:T(8,128)(2,1)S(1)} collective-permute-done((bf16[64,4096]{1,0:T(8,128)(2,1)}, bf16[64,4096]{1,0:T(8,128)(2,1)S(1)}, u32[]{:S(2)}, u32[]{:S(2)}) %collective-permute-start.1) | collective-permute-done | bytes 524320 | tf_op jit(solution)/shard_map/ppermute | solution.py:27
  30.6 2.0 %collective-permute-start.4 = (bf16[64,4096]{1,0:T(8,128)(2,1)S(1)}, bf16[64,4096]{1,0:T(8,128)(2,1)S(1)}, u32[]{:S(2)}, u32[]{:S(2)}) collective-permute-start(bf16[64,4096]{1,0:T(8,128)(2,1)S(1)} %collective-permute-done.2.refs_4_.refs_1_), channel_id=1, source_target_pairs={{0,64},{1,65},{2,66},{3,67},{4,68},{5,69},{6,70},{7,71},{8,72},{9,... | collective-permute-start | bytes 1572872 | tf_op jit(solution)/shard_map/ppermute | solution.py:27
  33.1 1.6 %collective-permute-start.6 = (bf16[64,4096]{1,0:T(8,128)(2,1)S(1)}, bf16[64,4096]{1,0:T(8,128)(2,1)S(1)}, u32[]{:S(2)}, u32[]{:S(2)}) collective-permute-start(bf16[64,4096]{1,0:T(8,128)(2,1)S(1)} %collective-permute-done.2.refs_4_.refs_1_), channel_id=1, source_target_pairs={{0,48},{1,49},{2,50},{3,51},{4,52},{5,53},{6,54},{7,55},{8,56},{9,... | collective-permute-start | bytes 1572872 | tf_op jit(solution)/shard_map/ppermute | solution.py:27
  34.7 1.5 %collective-permute-start.8 = (bf16[64,4096]{1,0:T(8,128)(2,1)S(1)}, bf16[64,4096]{1,0:T(8,128)(2,1)S(1)}, u32[]{:S(2)}, u32[]{:S(2)}) collective-permute-start(bf16[64,4096]{1,0:T(8,128)(2,1)S(1)} %collective-permute-done.3.refs_4_), channel_id=1, source_target_pairs={{0,4},{1,5},{2,6},{3,7},{4,8},{5,9},{6,10},{7,11},{8,12},{9,13},{1... | collective-permute-start | bytes 1572872 | tf_op jit(solution)/shard_map/ppermute | solution.py:27
  36.7 11.2 %collective-permute-done.4.refs_2_.refs_1_ = bf16[64,4096]{1,0:T(8,128)(2,1)S(1)} collective-permute-done((bf16[64,4096]{1,0:T(8,128)(2,1)S(1)}, bf16[64,4096]{1,0:T(8,128)(2,1)S(1)}, u32[]{:S(2)}, u32[]{:S(2)}) %collective-permute-start.4) | collective-permute-done | bytes 524320 | tf_op jit(solution)/shard_map/ppermute | solution.py:27
  49.5 2.4 %collective-permute-start.14 = (bf16[64,4096]{1,0:T(8,128)(2,1)S(1)}, bf16[64,4096]{1,0:T(8,128)(2,1)}, u32[]{:S(2)}, u32[]{:S(2)}) collective-permute-start(bf16[64,4096]{1,0:T(8,128)(2,1)S(1)} %collective-permute-done.3.refs_4_), channel_id=1, source_target_pairs={{0,8},{1,9},{2,10},{3,11},{4,12},{5,13},{6,14},{7,15},{8,0},{9,1},... | collective-permute-start | bytes 1572872 | tf_op jit(solution)/shard_map/ppermute | solution.py:27
  51.9 1.7 %collective-permute-start.12 = (bf16[64,4096]{1,0:T(8,128)(2,1)S(1)}, bf16[64,4096]{1,0:T(8,128)(2,1)}, u32[]{:S(2)}, u32[]{:S(2)}) collective-permute-start(bf16[64,4096]{1,0:T(8,128)(2,1)S(1)} %collective-permute-done.4.refs_2_.refs_1_), channel_id=1, source_target_pairs={{0,16},{1,17},{2,18},{3,19},{4,20},{5,21},{6,22},{7,23},{8,24},{9,... | collective-permute-start | bytes 1572872 | tf_op jit(solution)/shard_map/ppermute | solution.py:27
  53.9 3.0 %collective-permute-start.11 = (bf16[64,4096]{1,0:T(8,128)(2,1)S(1)}, bf16[64,4096]{1,0:T(8,128)(2,1)}, u32[]{:S(2)}, u32[]{:S(2)}) collective-permute-start(bf16[64,4096]{1,0:T(8,128)(2,1)S(1)} %copy-done.4), channel_id=1, source_target_pairs={{0,192},{1,193},{2,194},{3,195},{4,196},{5,197},{6,198},{7,199},{8... | collective-permute-start | bytes 1572872 | tf_op jit(solution)/shard_map/ppermute | solution.py:27
  57.0 8.6 %shard_map.56 = (f32[256,384]{1,0:T(8,128)}, s16[272,384]{1,0:T(8,128)(2,1)}, f32[8,384]{1,0:T(8,128)}, f32[512,128]{1,0:T(8,128)}, bf16[512,4096]{1,0:T(8,128)(2,1)}) custom-call(s32[24]{0:T(128)} %stack.93.table, bf16[64,4096]{1,0:T(8,128)(2,1)} %copy-done.9, bf16[64,4096]{1,0:T(8,128)(2,1)} %get-tuple-element.50.refs_1_.refs_0_, ...), custom_call_target="tpu_custom_call" | custom-call | flops 9497647104 | bytes 1048576 | tf_op jit(solution)/shard_map/pallas_call | solution.py:225
  66.2 1.7 %collective-permute-done.11.refs_3_.refs_4_ = bf16[64,4096]{1,0:T(8,128)(2,1)} collective-permute-done((bf16[64,4096]{1,0:T(8,128)(2,1)S(1)}, bf16[64,4096]{1,0:T(8,128)(2,1)}, u32[]{:S(2)}, u32[]{:S(2)}) %collective-permute-start.11) | collective-permute-done | bytes 524320 | tf_op jit(solution)/shard_map/ppermute | solution.py:27
  68.7 2.3 %collective-permute-start.15 = (bf16[64,4096]{1,0:T(8,128)(2,1)}, bf16[64,4096]{1,0:T(8,128)(2,1)S(1)}, u32[]{:S(2)}, u32[]{:S(2)}) collective-permute-start(bf16[64,4096]{1,0:T(8,128)(2,1)} %collective-permute-done.11.refs_3_.refs_4_), channel_id=1, source_target_pairs={{0,16},{1,17},{2,18},{3,19},{4,20},{5,21},{6,22},{7,23},{8,24},{9,... | collective-permute-start | bytes 1572872 | tf_op jit(solution)/shard_map/ppermute | solution.py:27
  70.9 6.4 %collective-permute-start.22 = (s16[272,384]{1,0:T(8,128)(2,1)}, s16[272,384]{1,0:T(8,128)(2,1)S(1)}, u32[]{:S(2)}, u32[]{:S(2)}) collective-permute-start(s16[272,384]{1,0:T(8,128)(2,1)} %get-tuple-element.69), channel_id=1, source_target_pairs={{0,1},{1,0},{2,3},{3,2},{4,5},{5,4},{6,7},{7,6},{8,9},{9,8},{10,11... | collective-permute-start | bytes 626696 | tf_op jit(solution)/shard_map/ppermute | solution.py:27
  80.0 7.3 %shard_map.57 = (f32[256,256]{1,0:T(8,128)S(1)}, s16[272,256]{1,0:T(8,128)(2,1)S(1)}, f32[8,256]{1,0:T(8,128)S(1)}, f32[512,128]{1,0:T(8,128)S(1)}) custom-call(s32[24]{0:T(128)S(1)} %copy-done.3, bf16[64,4096]{1,0:T(8,128)(2,1)S(1)} %copy-done.5, bf16[64,4096]{1,0:T(8,128)(2,1)S(1)} %copy-done.7, ...), custom_call_target="tpu_custom_call" | custom-call | flops 8631764992 | bytes 1048576 | tf_op jit(solution)/shard_map/pallas_call | solution.py:225
  87.3 5.1 %collective-permute-start.20 = (s16[272,256]{1,0:T(8,128)(2,1)S(1)}, s16[272,256]{1,0:T(8,128)(2,1)S(1)}, u32[]{:S(2)}, u32[]{:S(2)}) collective-permute-start(s16[272,256]{1,0:T(8,128)(2,1)S(1)} %get-tuple-element.65), channel_id=1, source_target_pairs={{0,1},{1,0},{2,3},{3,2},{4,5},{5,4},{6,7},{7,6},{8,9},{9,8},{10,11... | collective-permute-start | bytes 417800 | tf_op jit(solution)/shard_map/ppermute | solution.py:27
  92.4 4.8 %shard_map.59 = (f32[256,384]{1,0:T(8,128)S(1)}, s16[272,384]{1,0:T(8,128)(2,1)S(1)}, f32[8,384]{1,0:T(8,128)S(1)}) custom-call(s32[24]{0:T(128)S(1)} %copy-done.3, bf16[64,4096]{1,0:T(8,128)(2,1)} %collective-permute-done.12.refs_0_, bf16[64,4096]{1,0:T(8,128)(2,1)S(1)} %collective-permute-done.4.refs_2_.refs_1_, ...), custom_call_target="tpu_custom_call" | custom-call | flops 5472647168 | bytes 1048576 | tf_op jit(solution)/shard_map/pallas_call | solution.py:225
  99.4 1.3 %collective-permute-start.21 = (s16[256,256]{1,0:T(8,128)(2,1)S(1)}, s16[256,256]{1,0:T(8,128)(2,1)S(1)}, u32[]{:S(2)}, u32[]{:S(2)}) collective-permute-start(s16[256,256]{1,0:T(8,128)(2,1)S(1)} %shard_map.58), channel_id=1, source_target_pairs={{0,32},{1,33},{2,34},{3,35},{4,36},{5,37},{6,38},{7,39},{8,40},{9,... | collective-permute-start | bytes 393224 | tf_op jit(solution)/shard_map/ppermute | solution.py:27
  100.7 9.8 %collective-permute-done.23.refs_6_ = s16[272,384]{1,0:T(8,128)(2,1)S(1)} collective-permute-done((s16[272,384]{1,0:T(8,128)(2,1)S(1)}, s16[272,384]{1,0:T(8,128)(2,1)S(1)}, u32[]{:S(2)}, u32[]{:S(2)}) %collective-permute-start.23) | collective-permute-done | bytes 208928 | tf_op jit(solution)/shard_map/ppermute | solution.py:27
  110.5 3.3 %shard_map.60 = f32[256,8,128]{2,1,0:T(8,128)} custom-call(s32[24]{0:T(128)S(1)} %copy-done.3, f32[512,128]{1,0:T(8,128)S(1)} %copy-done.1, s16[256,256]{1,0:T(8,128)(2,1)S(1)} %collective-permute-done.21.refs_1_, f32[256,384]{1,0:T(8,128)S(1)} %copy-done, s16[272,384]{1,0:T(8,128)(2,1)S(1)} %collective-permute-done.22.refs_3_, f32[8,384]{1,0:T(8,128)S(1)} %copy-done.2, ...), custom_call_target="tpu_custom_call" | custom-call | flops 16777216 | bytes 1048576 | tf_op jit(solution)/shard_map/pallas_call | solution.py:225
  (63 shorter events, 10.8 us)
Async XLA Ops:
  3.4 15.0 %collective-permute-start = (bf16[64,4096]{1,0:T(8,128)(2,1)}, bf16[64,4096]{1,0:T(8,128)(2,1)S(1)}, u32[]{:S(2)}, u32[]{:S(2)}) collective-permute-start(bf16[64,4096]{1,0:T(8,128)(2,1)} %get-tuple-element.50.refs_1_.refs_0_), channel_id=1, source_target_pairs={{0,16},{1,17},{2,18},{3,19},{4,20},{5,21},{6,22},{7,23},{8,24},{9,... | collective-permute-start | bytes 1572872 | tf_op jit(solution)/shard_map/ppermute | solution.py:27
  3.6 26.1 %collective-permute-start.1 = (bf16[64,4096]{1,0:T(8,128)(2,1)}, bf16[64,4096]{1,0:T(8,128)(2,1)S(1)}, u32[]{:S(2)}, u32[]{:S(2)}) collective-permute-start(bf16[64,4096]{1,0:T(8,128)(2,1)} %get-tuple-element.50.refs_1_.refs_0_), channel_id=1, source_target_pairs={{0,48},{1,49},{2,50},{3,51},{4,52},{5,53},{6,54},{7,55},{8,56},{9,... | collective-permute-start | bytes 1572872 | tf_op jit(solution)/shard_map/ppermute | solution.py:27
  5.4 24.3 %collective-permute-start.2 = (bf16[64,4096]{1,0:T(8,128)(2,1)}, bf16[64,4096]{1,0:T(8,128)(2,1)S(1)}, u32[]{:S(2)}, u32[]{:S(2)}) collective-permute-start(bf16[64,4096]{1,0:T(8,128)(2,1)} %get-tuple-element.50.refs_1_.refs_0_), channel_id=1, source_target_pairs={{0,64},{1,65},{2,66},{3,67},{4,68},{5,69},{6,70},{7,71},{8,72},{9,... | collective-permute-start | bytes 1572872 | tf_op jit(solution)/shard_map/ppermute | solution.py:27
  7.3 23.2 %collective-permute-start.3 = (bf16[64,4096]{1,0:T(8,128)(2,1)}, bf16[64,4096]{1,0:T(8,128)(2,1)S(1)}, u32[]{:S(2)}, u32[]{:S(2)}) collective-permute-start(bf16[64,4096]{1,0:T(8,128)(2,1)} %get-tuple-element.50.refs_1_.refs_0_), channel_id=1, source_target_pairs={{0,32},{1,33},{2,34},{3,35},{4,36},{5,37},{6,38},{7,39},{8,40},{9,... | collective-permute-start | bytes 1572872 | tf_op jit(solution)/shard_map/ppermute | solution.py:27
  8.6 40.8 %all-to-all-start = ((bf16[4,64,4096]{2,1,0:T(8,128)(2,1)}), bf16[4,64,4096]{2,1,0:T(8,128)(2,1)}, u32[]{:S(2)}, u32[]{:S(2)}) async-start(bf16[4,64,4096]{2,1,0:T(8,128)(2,1)} %bitcast.29), calls=%async_computation | async-start | bytes 4194304 | tf_op jit(solution)/shard_map/all_to_all | solution.py:31
  30.6 17.2 %collective-permute-start.4 = (bf16[64,4096]{1,0:T(8,128)(2,1)S(1)}, bf16[64,4096]{1,0:T(8,128)(2,1)S(1)}, u32[]{:S(2)}, u32[]{:S(2)}) collective-permute-start(bf16[64,4096]{1,0:T(8,128)(2,1)S(1)} %collective-permute-done.2.refs_4_.refs_1_), channel_id=1, source_target_pairs={{0,64},{1,65},{2,66},{3,67},{4,68},{5,69},{6,70},{7,71},{8,72},{9,... | collective-permute-start | bytes 1572872 | tf_op jit(solution)/shard_map/ppermute | solution.py:27
  32.6 15.2 %collective-permute-start.5 = (bf16[64,4096]{1,0:T(8,128)(2,1)S(1)}, bf16[64,4096]{1,0:T(8,128)(2,1)S(1)}, u32[]{:S(2)}, u32[]{:S(2)}) collective-permute-start(bf16[64,4096]{1,0:T(8,128)(2,1)S(1)} %collective-permute-done.2.refs_4_.refs_1_), channel_id=1, source_target_pairs={{0,16},{1,17},{2,18},{3,19},{4,20},{5,21},{6,22},{7,23},{8,24},{9,... | collective-permute-start | bytes 1572872 | tf_op jit(solution)/shard_map/ppermute | solution.py:27
  33.1 15.0 %collective-permute-start.6 = (bf16[64,4096]{1,0:T(8,128)(2,1)S(1)}, bf16[64,4096]{1,0:T(8,128)(2,1)S(1)}, u32[]{:S(2)}, u32[]{:S(2)}) collective-permute-start(bf16[64,4096]{1,0:T(8,128)(2,1)S(1)} %collective-permute-done.2.refs_4_.refs_1_), channel_id=1, source_target_pairs={{0,48},{1,49},{2,50},{3,51},{4,52},{5,53},{6,54},{7,55},{8,56},{9,... | collective-permute-start | bytes 1572872 | tf_op jit(solution)/shard_map/ppermute | solution.py:27
  34.7 13.4 %collective-permute-start.8 = (bf16[64,4096]{1,0:T(8,128)(2,1)S(1)}, bf16[64,4096]{1,0:T(8,128)(2,1)S(1)}, u32[]{:S(2)}, u32[]{:S(2)}) collective-permute-start(bf16[64,4096]{1,0:T(8,128)(2,1)S(1)} %collective-permute-done.3.refs_4_), channel_id=1, source_target_pairs={{0,4},{1,5},{2,6},{3,7},{4,8},{5,9},{6,10},{7,11},{8,12},{9,13},{1... | collective-permute-start | bytes 1572872 | tf_op jit(solution)/shard_map/ppermute | solution.py:27
  36.1 13.2 %collective-permute-start.9 = (bf16[64,4096]{1,0:T(8,128)(2,1)S(1)}, bf16[64,4096]{1,0:T(8,128)(2,1)}, u32[]{:S(2)}, u32[]{:S(2)}) collective-permute-start(bf16[64,4096]{1,0:T(8,128)(2,1)S(1)} %collective-permute-done.3.refs_4_), channel_id=1, source_target_pairs={{0,12},{1,13},{2,14},{3,15},{4,0},{5,1},{6,2},{7,3},{8,4},{9,5},{1... | collective-permute-start | bytes 1572872 | tf_op jit(solution)/shard_map/ppermute | solution.py:27
  49.4 7.6 %collective-permute-start.10 = (bf16[256,4096]{1,0:T(8,128)(2,1)}, bf16[256,4096]{1,0:T(8,128)(2,1)}, u32[]{:S(2)}, u32[]{:S(2)}) collective-permute-start(bf16[256,4096]{1,0:T(8,128)(2,1)} %bitcast.27.refs_6_), channel_id=1, source_target_pairs={{0,2},{1,3},{2,0},{3,1},{4,6},{5,7},{6,4},{7,5},{8,10},{9,11},{10,... | collective-permute-start | bytes 6291464 | tf_op jit(solution)/shard_map/ppermute | solution.py:27
  49.5 16.1 %collective-permute-start.14 = (bf16[64,4096]{1,0:T(8,128)(2,1)S(1)}, bf16[64,4096]{1,0:T(8,128)(2,1)}, u32[]{:S(2)}, u32[]{:S(2)}) collective-permute-start(bf16[64,4096]{1,0:T(8,128)(2,1)S(1)} %collective-permute-done.3.refs_4_), channel_id=1, source_target_pairs={{0,8},{1,9},{2,10},{3,11},{4,12},{5,13},{6,14},{7,15},{8,0},{9,1},... | collective-permute-start | bytes 1572872 | tf_op jit(solution)/shard_map/ppermute | solution.py:27
  51.9 16.0 %collective-permute-start.12 = (bf16[64,4096]{1,0:T(8,128)(2,1)S(1)}, bf16[64,4096]{1,0:T(8,128)(2,1)}, u32[]{:S(2)}, u32[]{:S(2)}) collective-permute-start(bf16[64,4096]{1,0:T(8,128)(2,1)S(1)} %collective-permute-done.4.refs_2_.refs_1_), channel_id=1, source_target_pairs={{0,16},{1,17},{2,18},{3,19},{4,20},{5,21},{6,22},{7,23},{8,24},{9,... | collective-permute-start | bytes 1572872 | tf_op jit(solution)/shard_map/ppermute | solution.py:27
  53.7 15.0 %collective-permute-start.13 = (bf16[64,4096]{1,0:T(8,128)(2,1)S(1)}, bf16[64,4096]{1,0:T(8,128)(2,1)}, u32[]{:S(2)}, u32[]{:S(2)}) collective-permute-start(bf16[64,4096]{1,0:T(8,128)(2,1)S(1)} %collective-permute-done.4.refs_2_.refs_1_), channel_id=1, source_target_pairs={{0,48},{1,49},{2,50},{3,51},{4,52},{5,53},{6,54},{7,55},{8,56},{9,... | collective-permute-start | bytes 1572872 | tf_op jit(solution)/shard_map/ppermute | solution.py:27
  53.9 14.0 %collective-permute-start.11 = (bf16[64,4096]{1,0:T(8,128)(2,1)S(1)}, bf16[64,4096]{1,0:T(8,128)(2,1)}, u32[]{:S(2)}, u32[]{:S(2)}) collective-permute-start(bf16[64,4096]{1,0:T(8,128)(2,1)S(1)} %copy-done.4), channel_id=1, source_target_pairs={{0,192},{1,193},{2,194},{3,195},{4,196},{5,197},{6,198},{7,199},{8... | collective-permute-start | bytes 1572872 | tf_op jit(solution)/shard_map/ppermute | solution.py:27
  57.0 14.0 %collective-permute-start.17 = (bf16[64,4096]{1,0:T(8,128)(2,1)S(1)}, bf16[64,4096]{1,0:T(8,128)(2,1)}, u32[]{:S(2)}, u32[]{:S(2)}) collective-permute-start(bf16[64,4096]{1,0:T(8,128)(2,1)S(1)} %collective-permute-done.8.refs_5_), channel_id=1, source_target_pairs={{0,2},{1,3},{2,0},{3,1},{4,6},{5,7},{6,4},{7,5},{8,10},{9,11},{10,... | collective-permute-start | bytes 1572872 | tf_op jit(solution)/shard_map/ppermute | solution.py:27
  65.6 11.7 %collective-permute-start.18 = (bf16[64,4096]{1,0:T(8,128)(2,1)}, bf16[64,4096]{1,0:T(8,128)(2,1)S(1)}, u32[]{:S(2)}, u32[]{:S(2)}) collective-permute-start(bf16[64,4096]{1,0:T(8,128)(2,1)} %collective-permute-done.9.refs_6_), channel_id=1, source_target_pairs={{0,2},{1,3},{2,0},{3,1},{4,6},{5,7},{6,4},{7,5},{8,10},{9,11},{10,... | collective-permute-start | bytes 1572872 | tf_op jit(solution)/shard_map/ppermute | solution.py:27
  68.7 8.7 %collective-permute-start.19 = (bf16[64,4096]{1,0:T(8,128)(2,1)}, bf16[64,4096]{1,0:T(8,128)(2,1)S(1)}, u32[]{:S(2)}, u32[]{:S(2)}) collective-permute-start(bf16[64,4096]{1,0:T(8,128)(2,1)} %collective-permute-done.14.refs_7_), channel_id=1, source_target_pairs={{0,2},{1,3},{2,0},{3,1},{4,6},{5,7},{6,4},{7,5},{8,10},{9,11},{10,... | collective-permute-start | bytes 1572872 | tf_op jit(solution)/shard_map/ppermute | solution.py:27
  68.7 18.6 %collective-permute-start.15 = (bf16[64,4096]{1,0:T(8,128)(2,1)}, bf16[64,4096]{1,0:T(8,128)(2,1)S(1)}, u32[]{:S(2)}, u32[]{:S(2)}) collective-permute-start(bf16[64,4096]{1,0:T(8,128)(2,1)} %collective-permute-done.11.refs_3_.refs_4_), channel_id=1, source_target_pairs={{0,16},{1,17},{2,18},{3,19},{4,20},{5,21},{6,22},{7,23},{8,24},{9,... | collective-permute-start | bytes 1572872 | tf_op jit(solution)/shard_map/ppermute | solution.py:27
  70.9 16.4 %collective-permute-start.16 = (bf16[64,4096]{1,0:T(8,128)(2,1)}, bf16[64,4096]{1,0:T(8,128)(2,1)S(1)}, u32[]{:S(2)}, u32[]{:S(2)}) collective-permute-start(bf16[64,4096]{1,0:T(8,128)(2,1)} %collective-permute-done.11.refs_3_.refs_4_), channel_id=1, source_target_pairs={{0,48},{1,49},{2,50},{3,51},{4,52},{5,53},{6,54},{7,55},{8,56},{9,... | collective-permute-start | bytes 1572872 | tf_op jit(solution)/shard_map/ppermute | solution.py:27
  70.9 29.8 %collective-permute-start.22 = (s16[272,384]{1,0:T(8,128)(2,1)}, s16[272,384]{1,0:T(8,128)(2,1)S(1)}, u32[]{:S(2)}, u32[]{:S(2)}) collective-permute-start(s16[272,384]{1,0:T(8,128)(2,1)} %get-tuple-element.69), channel_id=1, source_target_pairs={{0,1},{1,0},{2,3},{3,2},{4,5},{5,4},{6,7},{7,6},{8,9},{9,8},{10,11... | collective-permute-start | bytes 626696 | tf_op jit(solution)/shard_map/ppermute | solution.py:27
  87.3 11.0 %collective-permute-start.20 = (s16[272,256]{1,0:T(8,128)(2,1)S(1)}, s16[272,256]{1,0:T(8,128)(2,1)S(1)}, u32[]{:S(2)}, u32[]{:S(2)}) collective-permute-start(s16[272,256]{1,0:T(8,128)(2,1)S(1)} %get-tuple-element.65), channel_id=1, source_target_pairs={{0,1},{1,0},{2,3},{3,2},{4,5},{5,4},{6,7},{7,6},{8,9},{9,8},{10,11... | collective-permute-start | bytes 417800 | tf_op jit(solution)/shard_map/ppermute | solution.py:27
  97.3 13.2 %collective-permute-start.23 = (s16[272,384]{1,0:T(8,128)(2,1)S(1)}, s16[272,384]{1,0:T(8,128)(2,1)S(1)}, u32[]{:S(2)}, u32[]{:S(2)}) collective-permute-start(s16[272,384]{1,0:T(8,128)(2,1)S(1)} %get-tuple-element.77), channel_id=1, source_target_pairs={{0,1},{1,0},{2,3},{3,2},{4,5},{5,4},{6,7},{7,6},{8,9},{9,8},{10,11... | collective-permute-start | bytes 626696 | tf_op jit(solution)/shard_map/ppermute | solution.py:27
  99.4 11.1 %collective-permute-start.21 = (s16[256,256]{1,0:T(8,128)(2,1)S(1)}, s16[256,256]{1,0:T(8,128)(2,1)S(1)}, u32[]{:S(2)}, u32[]{:S(2)}) collective-permute-start(s16[256,256]{1,0:T(8,128)(2,1)S(1)} %shard_map.58), channel_id=1, source_target_pairs={{0,32},{1,33},{2,34},{3,35},{4,36},{5,37},{6,38},{7,39},{8,40},{9,... | collective-permute-start | bytes 393224 | tf_op jit(solution)/shard_map/ppermute | solution.py:27
  (16 other events, 210.7 us)

commit v9 on v8

--- a/solution.py
+++ b/solution.py
@@ -361,7 +361,9 @@
     own01, msg01, cst01, rstat, ordered = tiles(
         rows, pieces(0) + pieces(1), None, at_near, True
     )
-    z3, up[2], down[2], own01, across = hold((z3, up[2], down[2], own01, across))
+    z3, up[2], down[2], own01, right, left, across = hold(
+        (z3, up[2], down[2], own01, right, left, across)
+    )
 
     z = [a, z1, z2, z3]
     up[3], down[3] = move(z3, y=1), move(z3, y=-1)

time: 116 us -> 116 us (level)
  no operation moved by 1% of the time
where the time goes in v9:
time: 116 us; the launch traced here: 114 us
  starting transfers between devices  40.5 us (35%)
  waiting for transfers between devices  40.4 us (35%)
  Pallas kernels  28.5 us (25%)
  local copies, waits for them, and re-layouts  4.92 us (4%)
    ppermute x24, waiting for transfers between devices, move(): return lax.ppermute(value, AXES, pairs)  40.4 us
    ppermute x24, starting transfers between devices, move(): return lax.ppermute(value, AXES, pairs)  35.4 us
    pallas_call x5, Pallas kernels, call(): pl.pallas_call(lambda table, *refs: kernel(From(table, first), *refs), in...  25.1 us
    all_to_all x1, starting transfers between devices, spread_x(): return lax.all_to_all(copies, 'x', 0, 0, tiled=True)  5.07 us
    unnamed x30, local copies, waits for them, and re-layouts  4.33 us
    pallas_call x1, Pallas kernels, residuals(): pl.pallas_call(functools.partial(resid_kernel, math.sqrt(cells * NH)), in...  3.38 us
  transfers between devices with their start and end apart: 25, of which 8 were waited for; matrix products, arithmetic and copies ran while one was open for 1% of the time, Pallas kernels for 19%

profile of v9, /device:TPU:26, one launch (start us, length us, event | category | flops | bytes accessed | tf_op | source)
XLA Modules:
  0.0 114.4 jit_solution(9733150676987754882)
XLA Ops:
  0.0 3.4 %shard_map.55 = (bf16[64,4096]{1,0:T(8,128)(2,1)}, bf16[256,4096]{1,0:T(8,128)(2,1)}) custom-call(s32[1]{0:T(128)} %bitcast.place, s32[128]{0:T(128)} %order.1, s32[64,4096]{1,0:T(8,128)} %counts.1, f32[1,4096]{1,0:T(1,128)} %bitcast.32, f32[64,128]{1,0:T(8,128)} %bitcast.30, f32[64,128]{1,0:T(8,128)} %bitcast.31), custom_call_target="tpu_custom_call" | custom-call | tf_op jit(solution)/shard_map/pallas_call | solution.py:59
  3.6 1.8 %collective-permute-start.1 = (bf16[64,4096]{1,0:T(8,128)(2,1)}, bf16[64,4096]{1,0:T(8,128)(2,1)S(1)}, u32[]{:S(2)}, u32[]{:S(2)}) collective-permute-start(bf16[64,4096]{1,0:T(8,128)(2,1)} %get-tuple-element.52.refs_1_.refs_0_), channel_id=1, source_target_pairs={{0,48},{1,49},{2,50},{3,51},{4,52},{5,53},{6,54},{7,55},{8,56},{9,... | collective-permute-start | bytes 1572872 | tf_op jit(solution)/shard_map/ppermute | solution.py:27
  5.4 1.9 %collective-permute-start.2 = (bf16[64,4096]{1,0:T(8,128)(2,1)}, bf16[64,4096]{1,0:T(8,128)(2,1)S(1)}, u32[]{:S(2)}, u32[]{:S(2)}) collective-permute-start(bf16[64,4096]{1,0:T(8,128)(2,1)} %get-tuple-element.52.refs_1_.refs_0_), channel_id=1, source_target_pairs={{0,64},{1,65},{2,66},{3,67},{4,68},{5,69},{6,70},{7,71},{8,72},{9,... | collective-permute-start | bytes 1572872 | tf_op jit(solution)/shard_map/ppermute | solution.py:27
  7.3 1.2 %collective-permute-start.3 = (bf16[64,4096]{1,0:T(8,128)(2,1)}, bf16[64,4096]{1,0:T(8,128)(2,1)S(1)}, u32[]{:S(2)}, u32[]{:S(2)}) collective-permute-start(bf16[64,4096]{1,0:T(8,128)(2,1)} %get-tuple-element.52.refs_1_.refs_0_), channel_id=1, source_target_pairs={{0,32},{1,33},{2,34},{3,35},{4,36},{5,37},{6,38},{7,39},{8,40},{9,... | collective-permute-start | bytes 1572872 | tf_op jit(solution)/shard_map/ppermute | solution.py:27
  8.6 5.1 %all-to-all-start = ((bf16[4,64,4096]{2,1,0:T(8,128)(2,1)}), bf16[4,64,4096]{2,1,0:T(8,128)(2,1)}, u32[]{:S(2)}, u32[]{:S(2)}) async-start(bf16[4,64,4096]{2,1,0:T(8,128)(2,1)} %bitcast.29), calls=%async_computation | async-start | bytes 4194304 | tf_op jit(solution)/shard_map/all_to_all | solution.py:31
  14.2 4.2 %collective-permute-done.refs_0_ = bf16[64,4096]{1,0:T(8,128)(2,1)S(1)} collective-permute-done((bf16[64,4096]{1,0:T(8,128)(2,1)}, bf16[64,4096]{1,0:T(8,128)(2,1)S(1)}, u32[]{:S(2)}, u32[]{:S(2)}) %collective-permute-start) | collective-permute-done | bytes 524320 | tf_op jit(solution)/shard_map/ppermute | solution.py:27
  18.4 11.3 %collective-permute-done.1.refs_2_ = bf16[64,4096]{1,0:T(8,128)(2,1)S(1)} collective-permute-done((bf16[64,4096]{1,0:T(8,128)(2,1)}, bf16[64,4096]{1,0:T(8,128)(2,1)S(1)}, u32[]{:S(2)}, u32[]{:S(2)}) %collective-permute-start.1) | collective-permute-done | bytes 524320 | tf_op jit(solution)/shard_map/ppermute | solution.py:27
  30.6 2.0 %collective-permute-start.4 = (bf16[64,4096]{1,0:T(8,128)(2,1)S(1)}, bf16[64,4096]{1,0:T(8,128)(2,1)S(1)}, u32[]{:S(2)}, u32[]{:S(2)}) collective-permute-start(bf16[64,4096]{1,0:T(8,128)(2,1)S(1)} %collective-permute-done.2.refs_4_.refs_1_), channel_id=1, source_target_pairs={{0,64},{1,65},{2,66},{3,67},{4,68},{5,69},{6,70},{7,71},{8,72},{9,... | collective-permute-start | bytes 1572872 | tf_op jit(solution)/shard_map/ppermute | solution.py:27
  33.1 1.6 %collective-permute-start.6 = (bf16[64,4096]{1,0:T(8,128)(2,1)S(1)}, bf16[64,4096]{1,0:T(8,128)(2,1)S(1)}, u32[]{:S(2)}, u32[]{:S(2)}) collective-permute-start(bf16[64,4096]{1,0:T(8,128)(2,1)S(1)} %collective-permute-done.2.refs_4_.refs_1_), channel_id=1, source_target_pairs={{0,48},{1,49},{2,50},{3,51},{4,52},{5,53},{6,54},{7,55},{8,56},{9,... | collective-permute-start | bytes 1572872 | tf_op jit(solution)/shard_map/ppermute | solution.py:27
  34.7 1.5 %collective-permute-start.8 = (bf16[64,4096]{1,0:T(8,128)(2,1)S(1)}, bf16[64,4096]{1,0:T(8,128)(2,1)S(1)}, u32[]{:S(2)}, u32[]{:S(2)}) collective-permute-start(bf16[64,4096]{1,0:T(8,128)(2,1)S(1)} %collective-permute-done.3.refs_4_), channel_id=1, source_target_pairs={{0,4},{1,5},{2,6},{3,7},{4,8},{5,9},{6,10},{7,11},{8,12},{9,13},{1... | collective-permute-start | bytes 1572872 | tf_op jit(solution)/shard_map/ppermute | solution.py:27
  36.7 11.2 %collective-permute-done.4.refs_2_.refs_1_ = bf16[64,4096]{1,0:T(8,128)(2,1)S(1)} collective-permute-done((bf16[64,4096]{1,0:T(8,128)(2,1)S(1)}, bf16[64,4096]{1,0:T(8,128)(2,1)S(1)}, u32[]{:S(2)}, u32[]{:S(2)}) %collective-permute-start.4) | collective-permute-done | bytes 524320 | tf_op jit(solution)/shard_map/ppermute | solution.py:27
  49.5 2.4 %collective-permute-start.14 = (bf16[64,4096]{1,0:T(8,128)(2,1)S(1)}, bf16[64,4096]{1,0:T(8,128)(2,1)}, u32[]{:S(2)}, u32[]{:S(2)}) collective-permute-start(bf16[64,4096]{1,0:T(8,128)(2,1)S(1)} %collective-permute-done.3.refs_4_), channel_id=1, source_target_pairs={{0,8},{1,9},{2,10},{3,11},{4,12},{5,13},{6,14},{7,15},{8,0},{9,1},... | collective-permute-start | bytes 1572872 | tf_op jit(solution)/shard_map/ppermute | solution.py:27
  51.9 1.7 %collective-permute-start.12 = (bf16[64,4096]{1,0:T(8,128)(2,1)S(1)}, bf16[64,4096]{1,0:T(8,128)(2,1)}, u32[]{:S(2)}, u32[]{:S(2)}) collective-permute-start(bf16[64,4096]{1,0:T(8,128)(2,1)S(1)} %collective-permute-done.4.refs_2_.refs_1_), channel_id=1, source_target_pairs={{0,16},{1,17},{2,18},{3,19},{4,20},{5,21},{6,22},{7,23},{8,24},{9,... | collective-permute-start | bytes 1572872 | tf_op jit(solution)/shard_map/ppermute | solution.py:27
  53.9 3.0 %collective-permute-start.11 = (bf16[64,4096]{1,0:T(8,128)(2,1)S(1)}, bf16[64,4096]{1,0:T(8,128)(2,1)}, u32[]{:S(2)}, u32[]{:S(2)}) collective-permute-start(bf16[64,4096]{1,0:T(8,128)(2,1)S(1)} %copy-done.4), channel_id=1, source_target_pairs={{0,192},{1,193},{2,194},{3,195},{4,196},{5,197},{6,198},{7,199},{8... | collective-permute-start | bytes 1572872 | tf_op jit(solution)/shard_map/ppermute | solution.py:27
  57.0 8.6 %shard_map.56 = (f32[256,384]{1,0:T(8,128)}, s16[272,384]{1,0:T(8,128)(2,1)}, f32[8,384]{1,0:T(8,128)}, f32[512,128]{1,0:T(8,128)}, bf16[512,4096]{1,0:T(8,128)(2,1)}) custom-call(s32[24]{0:T(128)} %stack.93.table, bf16[64,4096]{1,0:T(8,128)(2,1)} %copy-done.9, bf16[64,4096]{1,0:T(8,128)(2,1)} %get-tuple-element.52.refs_1_.refs_0_, ...), custom_call_target="tpu_custom_call" | custom-call | flops 9497647104 | bytes 1048576 | tf_op jit(solution)/shard_map/pallas_call | solution.py:225
  65.6 2.3 %collective-permute-done.11.refs_3_.refs_4_ = bf16[64,4096]{1,0:T(8,128)(2,1)} collective-permute-done((bf16[64,4096]{1,0:T(8,128)(2,1)S(1)}, bf16[64,4096]{1,0:T(8,128)(2,1)}, u32[]{:S(2)}, u32[]{:S(2)}) %collective-permute-start.11) | collective-permute-done | bytes 524320 | tf_op jit(solution)/shard_map/ppermute | solution.py:27
  69.2 2.3 %collective-permute-start.15 = (bf16[64,4096]{1,0:T(8,128)(2,1)}, bf16[64,4096]{1,0:T(8,128)(2,1)S(1)}, u32[]{:S(2)}, u32[]{:S(2)}) collective-permute-start(bf16[64,4096]{1,0:T(8,128)(2,1)} %collective-permute-done.11.refs_3_.refs_4_), channel_id=1, source_target_pairs={{0,16},{1,17},{2,18},{3,19},{4,20},{5,21},{6,22},{7,23},{8,24},{9,... | collective-permute-start | bytes 1572872 | tf_op jit(solution)/shard_map/ppermute | solution.py:27
  71.5 6.4 %collective-permute-start.22 = (s16[272,384]{1,0:T(8,128)(2,1)}, s16[272,384]{1,0:T(8,128)(2,1)S(1)}, u32[]{:S(2)}, u32[]{:S(2)}) collective-permute-start(s16[272,384]{1,0:T(8,128)(2,1)} %get-tuple-element.73), channel_id=1, source_target_pairs={{0,1},{1,0},{2,3},{3,2},{4,5},{5,4},{6,7},{7,6},{8,9},{9,8},{10,11... | collective-permute-start | bytes 626696 | tf_op jit(solution)/shard_map/ppermute | solution.py:27
  80.6 7.3 %shard_map.57 = (f32[256,256]{1,0:T(8,128)S(1)}, s16[272,256]{1,0:T(8,128)(2,1)S(1)}, f32[8,256]{1,0:T(8,128)S(1)}, f32[512,128]{1,0:T(8,128)S(1)}) custom-call(s32[24]{0:T(128)S(1)} %copy-done.3, bf16[64,4096]{1,0:T(8,128)(2,1)S(1)} %copy-done.5, bf16[64,4096]{1,0:T(8,128)(2,1)S(1)} %copy-done.7, ...), custom_call_target="tpu_custom_call" | custom-call | flops 8631764992 | bytes 1048576 | tf_op jit(solution)/shard_map/pallas_call | solution.py:225
  87.8 5.1 %collective-permute-start.20 = (s16[272,256]{1,0:T(8,128)(2,1)S(1)}, s16[272,256]{1,0:T(8,128)(2,1)S(1)}, u32[]{:S(2)}, u32[]{:S(2)}) collective-permute-start(s16[272,256]{1,0:T(8,128)(2,1)S(1)} %get-tuple-element.69), channel_id=1, source_target_pairs={{0,1},{1,0},{2,3},{3,2},{4,5},{5,4},{6,7},{7,6},{8,9},{9,8},{10,11... | collective-permute-start | bytes 417800 | tf_op jit(solution)/shard_map/ppermute | solution.py:27
  93.0 4.8 %shard_map.59 = (f32[256,384]{1,0:T(8,128)S(1)}, s16[272,384]{1,0:T(8,128)(2,1)S(1)}, f32[8,384]{1,0:T(8,128)S(1)}) custom-call(s32[24]{0:T(128)S(1)} %copy-done.3, bf16[64,4096]{1,0:T(8,128)(2,1)} %collective-permute-done.12.refs_0_, bf16[64,4096]{1,0:T(8,128)(2,1)S(1)} %collective-permute-done.4.refs_2_.refs_1_, ...), custom_call_target="tpu_custom_call" | custom-call | flops 5472647168 | bytes 1048576 | tf_op jit(solution)/shard_map/pallas_call | solution.py:225
  99.9 1.2 %collective-permute-start.21 = (s16[256,256]{1,0:T(8,128)(2,1)S(1)}, s16[256,256]{1,0:T(8,128)(2,1)S(1)}, u32[]{:S(2)}, u32[]{:S(2)}) collective-permute-start(s16[256,256]{1,0:T(8,128)(2,1)S(1)} %shard_map.58), channel_id=1, source_target_pairs={{0,32},{1,33},{2,34},{3,35},{4,36},{5,37},{6,38},{7,39},{8,40},{9,... | collective-permute-start | bytes 393224 | tf_op jit(solution)/shard_map/ppermute | solution.py:27
  101.2 9.9 %collective-permute-done.23.refs_6_ = s16[272,384]{1,0:T(8,128)(2,1)S(1)} collective-permute-done((s16[272,384]{1,0:T(8,128)(2,1)S(1)}, s16[272,384]{1,0:T(8,128)(2,1)S(1)}, u32[]{:S(2)}, u32[]{:S(2)}) %collective-permute-start.23) | collective-permute-done | bytes 208928 | tf_op jit(solution)/shard_map/ppermute | solution.py:27
  111.1 3.3 %shard_map.60 = f32[256,8,128]{2,1,0:T(8,128)} custom-call(s32[24]{0:T(128)S(1)} %copy-done.3, f32[512,128]{1,0:T(8,128)S(1)} %copy-done.1, s16[256,256]{1,0:T(8,128)(2,1)S(1)} %collective-permute-done.21.refs_1_, f32[256,384]{1,0:T(8,128)S(1)} %copy-done, s16[272,384]{1,0:T(8,128)(2,1)S(1)} %collective-permute-done.22.refs_3_, f32[8,384]{1,0:T(8,128)S(1)} %copy-done.2, ...), custom_call_target="tpu_custom_call" | custom-call | flops 16777216 | bytes 1048576 | tf_op jit(solution)/shard_map/pallas_call | solution.py:225
  (63 shorter events, 10.8 us)
Async XLA Ops:
  3.4 15.0 %collective-permute-start = (bf16[64,4096]{1,0:T(8,128)(2,1)}, bf16[64,4096]{1,0:T(8,128)(2,1)S(1)}, u32[]{:S(2)}, u32[]{:S(2)}) collective-permute-start(bf16[64,4096]{1,0:T(8,128)(2,1)} %get-tuple-element.52.refs_1_.refs_0_), channel_id=1, source_target_pairs={{0,16},{1,17},{2,18},{3,19},{4,20},{5,21},{6,22},{7,23},{8,24},{9,... | collective-permute-start | bytes 1572872 | tf_op jit(solution)/shard_map/ppermute | solution.py:27
  3.6 26.1 %collective-permute-start.1 = (bf16[64,4096]{1,0:T(8,128)(2,1)}, bf16[64,4096]{1,0:T(8,128)(2,1)S(1)}, u32[]{:S(2)}, u32[]{:S(2)}) collective-permute-start(bf16[64,4096]{1,0:T(8,128)(2,1)} %get-tuple-element.52.refs_1_.refs_0_), channel_id=1, source_target_pairs={{0,48},{1,49},{2,50},{3,51},{4,52},{5,53},{6,54},{7,55},{8,56},{9,... | collective-permute-start | bytes 1572872 | tf_op jit(solution)/shard_map/ppermute | solution.py:27
  5.4 24.3 %collective-permute-start.2 = (bf16[64,4096]{1,0:T(8,128)(2,1)}, bf16[64,4096]{1,0:T(8,128)(2,1)S(1)}, u32[]{:S(2)}, u32[]{:S(2)}) collective-permute-start(bf16[64,4096]{1,0:T(8,128)(2,1)} %get-tuple-element.52.refs_1_.refs_0_), channel_id=1, source_target_pairs={{0,64},{1,65},{2,66},{3,67},{4,68},{5,69},{6,70},{7,71},{8,72},{9,... | collective-permute-start | bytes 1572872 | tf_op jit(solution)/shard_map/ppermute | solution.py:27
  7.3 23.2 %collective-permute-start.3 = (bf16[64,4096]{1,0:T(8,128)(2,1)}, bf16[64,4096]{1,0:T(8,128)(2,1)S(1)}, u32[]{:S(2)}, u32[]{:S(2)}) collective-permute-start(bf16[64,4096]{1,0:T(8,128)(2,1)} %get-tuple-element.52.refs_1_.refs_0_), channel_id=1, source_target_pairs={{0,32},{1,33},{2,34},{3,35},{4,36},{5,37},{6,38},{7,39},{8,40},{9,... | collective-permute-start | bytes 1572872 | tf_op jit(solution)/shard_map/ppermute | solution.py:27
  8.6 40.8 %all-to-all-start = ((bf16[4,64,4096]{2,1,0:T(8,128)(2,1)}), bf16[4,64,4096]{2,1,0:T(8,128)(2,1)}, u32[]{:S(2)}, u32[]{:S(2)}) async-start(bf16[4,64,4096]{2,1,0:T(8,128)(2,1)} %bitcast.29), calls=%async_computation | async-start | bytes 4194304 | tf_op jit(solution)/shard_map/all_to_all | solution.py:31
  30.5 4.1 %collective-permute-start.7 = (bf16[64,4096]{1,0:T(8,128)(2,1)S(1)}, bf16[64,4096]{1,0:T(8,128)(2,1)S(1)}, u32[]{:S(2)}, u32[]{:S(2)}) collective-permute-start(bf16[64,4096]{1,0:T(8,128)(2,1)S(1)} %collective-permute-done.3.refs_4_), channel_id=1, source_target_pairs={{0,2},{1,3},{2,0},{3,1},{4,6},{5,7},{6,4},{7,5},{8,10},{9,11},{10,... | collective-permute-start | bytes 1572872 | tf_op jit(solution)/shard_map/ppermute | solution.py:27
  30.6 17.2 %collective-permute-start.4 = (bf16[64,4096]{1,0:T(8,128)(2,1)S(1)}, bf16[64,4096]{1,0:T(8,128)(2,1)S(1)}, u32[]{:S(2)}, u32[]{:S(2)}) collective-permute-start(bf16[64,4096]{1,0:T(8,128)(2,1)S(1)} %collective-permute-done.2.refs_4_.refs_1_), channel_id=1, source_target_pairs={{0,64},{1,65},{2,66},{3,67},{4,68},{5,69},{6,70},{7,71},{8,72},{9,... | collective-permute-start | bytes 1572872 | tf_op jit(solution)/shard_map/ppermute | solution.py:27
  32.6 15.2 %collective-permute-start.5 = (bf16[64,4096]{1,0:T(8,128)(2,1)S(1)}, bf16[64,4096]{1,0:T(8,128)(2,1)S(1)}, u32[]{:S(2)}, u32[]{:S(2)}) collective-permute-start(bf16[64,4096]{1,0:T(8,128)(2,1)S(1)} %collective-permute-done.2.refs_4_.refs_1_), channel_id=1, source_target_pairs={{0,16},{1,17},{2,18},{3,19},{4,20},{5,21},{6,22},{7,23},{8,24},{9,... | collective-permute-start | bytes 1572872 | tf_op jit(solution)/shard_map/ppermute | solution.py:27
  33.1 15.0 %collective-permute-start.6 = (bf16[64,4096]{1,0:T(8,128)(2,1)S(1)}, bf16[64,4096]{1,0:T(8,128)(2,1)S(1)}, u32[]{:S(2)}, u32[]{:S(2)}) collective-permute-start(bf16[64,4096]{1,0:T(8,128)(2,1)S(1)} %collective-permute-done.2.refs_4_.refs_1_), channel_id=1, source_target_pairs={{0,48},{1,49},{2,50},{3,51},{4,52},{5,53},{6,54},{7,55},{8,56},{9,... | collective-permute-start | bytes 1572872 | tf_op jit(solution)/shard_map/ppermute | solution.py:27
  34.7 13.4 %collective-permute-start.8 = (bf16[64,4096]{1,0:T(8,128)(2,1)S(1)}, bf16[64,4096]{1,0:T(8,128)(2,1)S(1)}, u32[]{:S(2)}, u32[]{:S(2)}) collective-permute-start(bf16[64,4096]{1,0:T(8,128)(2,1)S(1)} %collective-permute-done.3.refs_4_), channel_id=1, source_target_pairs={{0,4},{1,5},{2,6},{3,7},{4,8},{5,9},{6,10},{7,11},{8,12},{9,13},{1... | collective-permute-start | bytes 1572872 | tf_op jit(solution)/shard_map/ppermute | solution.py:27
  36.1 13.2 %collective-permute-start.9 = (bf16[64,4096]{1,0:T(8,128)(2,1)S(1)}, bf16[64,4096]{1,0:T(8,128)(2,1)}, u32[]{:S(2)}, u32[]{:S(2)}) collective-permute-start(bf16[64,4096]{1,0:T(8,128)(2,1)S(1)} %collective-permute-done.3.refs_4_), channel_id=1, source_target_pairs={{0,12},{1,13},{2,14},{3,15},{4,0},{5,1},{6,2},{7,3},{8,4},{9,5},{1... | collective-permute-start | bytes 1572872 | tf_op jit(solution)/shard_map/ppermute | solution.py:27
  49.4 7.6 %collective-permute-start.10 = (bf16[256,4096]{1,0:T(8,128)(2,1)}, bf16[256,4096]{1,0:T(8,128)(2,1)}, u32[]{:S(2)}, u32[]{:S(2)}) collective-permute-start(bf16[256,4096]{1,0:T(8,128)(2,1)} %bitcast.27.refs_6_), channel_id=1, source_target_pairs={{0,2},{1,3},{2,0},{3,1},{4,6},{5,7},{6,4},{7,5},{8,10},{9,11},{10,... | collective-permute-start | bytes 6291464 | tf_op jit(solution)/shard_map/ppermute | solution.py:27
  49.5 16.1 %collective-permute-start.14 = (bf16[64,4096]{1,0:T(8,128)(2,1)S(1)}, bf16[64,4096]{1,0:T(8,128)(2,1)}, u32[]{:S(2)}, u32[]{:S(2)}) collective-permute-start(bf16[64,4096]{1,0:T(8,128)(2,1)S(1)} %collective-permute-done.3.refs_4_), channel_id=1, source_target_pairs={{0,8},{1,9},{2,10},{3,11},{4,12},{5,13},{6,14},{7,15},{8,0},{9,1},... | collective-permute-start | bytes 1572872 | tf_op jit(solution)/shard_map/ppermute | solution.py:27
  51.9 16.0 %collective-permute-start.12 = (bf16[64,4096]{1,0:T(8,128)(2,1)S(1)}, bf16[64,4096]{1,0:T(8,128)(2,1)}, u32[]{:S(2)}, u32[]{:S(2)}) collective-permute-start(bf16[64,4096]{1,0:T(8,128)(2,1)S(1)} %collective-permute-done.4.refs_2_.refs_1_), channel_id=1, source_target_pairs={{0,16},{1,17},{2,18},{3,19},{4,20},{5,21},{6,22},{7,23},{8,24},{9,... | collective-permute-start | bytes 1572872 | tf_op jit(solution)/shard_map/ppermute | solution.py:27
  53.7 15.0 %collective-permute-start.13 = (bf16[64,4096]{1,0:T(8,128)(2,1)S(1)}, bf16[64,4096]{1,0:T(8,128)(2,1)}, u32[]{:S(2)}, u32[]{:S(2)}) collective-permute-start(bf16[64,4096]{1,0:T(8,128)(2,1)S(1)} %collective-permute-done.4.refs_2_.refs_1_), channel_id=1, source_target_pairs={{0,48},{1,49},{2,50},{3,51},{4,52},{5,53},{6,54},{7,55},{8,56},{9,... | collective-permute-start | bytes 1572872 | tf_op jit(solution)/shard_map/ppermute | solution.py:27
  53.9 14.0 %collective-permute-start.11 = (bf16[64,4096]{1,0:T(8,128)(2,1)S(1)}, bf16[64,4096]{1,0:T(8,128)(2,1)}, u32[]{:S(2)}, u32[]{:S(2)}) collective-permute-start(bf16[64,4096]{1,0:T(8,128)(2,1)S(1)} %copy-done.4), channel_id=1, source_target_pairs={{0,192},{1,193},{2,194},{3,195},{4,196},{5,197},{6,198},{7,199},{8... | collective-permute-start | bytes 1572872 | tf_op jit(solution)/shard_map/ppermute | solution.py:27
  68.7 9.2 %collective-permute-start.18 = (bf16[64,4096]{1,0:T(8,128)(2,1)}, bf16[64,4096]{1,0:T(8,128)(2,1)S(1)}, u32[]{:S(2)}, u32[]{:S(2)}) collective-permute-start(bf16[64,4096]{1,0:T(8,128)(2,1)} %collective-permute-done.9.refs_6_), channel_id=1, source_target_pairs={{0,2},{1,3},{2,0},{3,1},{4,6},{5,7},{6,4},{7,5},{8,10},{9,11},{10,... | collective-permute-start | bytes 1572872 | tf_op jit(solution)/shard_map/ppermute | solution.py:27
  69.2 8.7 %collective-permute-start.19 = (bf16[64,4096]{1,0:T(8,128)(2,1)}, bf16[64,4096]{1,0:T(8,128)(2,1)S(1)}, u32[]{:S(2)}, u32[]{:S(2)}) collective-permute-start(bf16[64,4096]{1,0:T(8,128)(2,1)} %collective-permute-done.14.refs_7_), channel_id=1, source_target_pairs={{0,2},{1,3},{2,0},{3,1},{4,6},{5,7},{6,4},{7,5},{8,10},{9,11},{10,... | collective-permute-start | bytes 1572872 | tf_op jit(solution)/shard_map/ppermute | solution.py:27
  69.2 18.6 %collective-permute-start.15 = (bf16[64,4096]{1,0:T(8,128)(2,1)}, bf16[64,4096]{1,0:T(8,128)(2,1)S(1)}, u32[]{:S(2)}, u32[]{:S(2)}) collective-permute-start(bf16[64,4096]{1,0:T(8,128)(2,1)} %collective-permute-done.11.refs_3_.refs_4_), channel_id=1, source_target_pairs={{0,16},{1,17},{2,18},{3,19},{4,20},{5,21},{6,22},{7,23},{8,24},{9,... | collective-permute-start | bytes 1572872 | tf_op jit(solution)/shard_map/ppermute | solution.py:27
  71.5 16.4 %collective-permute-start.16 = (bf16[64,4096]{1,0:T(8,128)(2,1)}, bf16[64,4096]{1,0:T(8,128)(2,1)S(1)}, u32[]{:S(2)}, u32[]{:S(2)}) collective-permute-start(bf16[64,4096]{1,0:T(8,128)(2,1)} %collective-permute-done.11.refs_3_.refs_4_), channel_id=1, source_target_pairs={{0,48},{1,49},{2,50},{3,51},{4,52},{5,53},{6,54},{7,55},{8,56},{9,... | collective-permute-start | bytes 1572872 | tf_op jit(solution)/shard_map/ppermute | solution.py:27
  71.5 29.7 %collective-permute-start.22 = (s16[272,384]{1,0:T(8,128)(2,1)}, s16[272,384]{1,0:T(8,128)(2,1)S(1)}, u32[]{:S(2)}, u32[]{:S(2)}) collective-permute-start(s16[272,384]{1,0:T(8,128)(2,1)} %get-tuple-element.73), channel_id=1, source_target_pairs={{0,1},{1,0},{2,3},{3,2},{4,5},{5,4},{6,7},{7,6},{8,9},{9,8},{10,11... | collective-permute-start | bytes 626696 | tf_op jit(solution)/shard_map/ppermute | solution.py:27
  87.8 11.0 %collective-permute-start.20 = (s16[272,256]{1,0:T(8,128)(2,1)S(1)}, s16[272,256]{1,0:T(8,128)(2,1)S(1)}, u32[]{:S(2)}, u32[]{:S(2)}) collective-permute-start(s16[272,256]{1,0:T(8,128)(2,1)S(1)} %get-tuple-element.69), channel_id=1, source_target_pairs={{0,1},{1,0},{2,3},{3,2},{4,5},{5,4},{6,7},{7,6},{8,9},{9,8},{10,11... | collective-permute-start | bytes 417800 | tf_op jit(solution)/shard_map/ppermute | solution.py:27
  97.8 13.3 %collective-permute-start.23 = (s16[272,384]{1,0:T(8,128)(2,1)S(1)}, s16[272,384]{1,0:T(8,128)(2,1)S(1)}, u32[]{:S(2)}, u32[]{:S(2)}) collective-permute-start(s16[272,384]{1,0:T(8,128)(2,1)S(1)} %get-tuple-element.81), channel_id=1, source_target_pairs={{0,1},{1,0},{2,3},{3,2},{4,5},{5,4},{6,7},{7,6},{8,9},{9,8},{10,11... | collective-permute-start | bytes 626696 | tf_op jit(solution)/shard_map/ppermute | solution.py:27
  99.9 11.2 %collective-permute-start.21 = (s16[256,256]{1,0:T(8,128)(2,1)S(1)}, s16[256,256]{1,0:T(8,128)(2,1)S(1)}, u32[]{:S(2)}, u32[]{:S(2)}) collective-permute-start(s16[256,256]{1,0:T(8,128)(2,1)S(1)} %shard_map.58), channel_id=1, source_target_pairs={{0,32},{1,33},{2,34},{3,35},{4,36},{5,37},{6,38},{7,39},{8,40},{9,... | collective-permute-start | bytes 393224 | tf_op jit(solution)/shard_map/ppermute | solution.py:27
  (16 other events, 210.5 us)
